TPU v7x, 512 devices: a whole 4x4x16 slice. The times are simulated.
512 devices in a mesh: tm: 16 (over z), tile: 32 (over x, y, core).
Axes of the slice: x: 4, y: 4, z: 16, core: 2. Of those that a mesh axis runs over, the one named last changes fastest.
Arguments:
- features: bfloat16 [64, 4, 256, 384], P('tm', None, 'tile'), may hold values from -500 to 500
- skip: bfloat16 [64, 4, 256, 384], P('tm', None, 'tile'), may hold values from -6 to 6
- norm_gain: float32 [384], replicated, may hold values from 0.1 to 1.9
- norm_bias: float32 [384], replicated, may hold values from -3 to 3
- conv_weight: bfloat16 [384, 27, 384], P('tm'), may hold values from -0.0625 to 0.0625
- conv_bias: float32 [384], replicated, may hold values from -3 to 3
- up_weight: bfloat16 [192, 9, 384], P('tm'), may hold values from -0.109375 to 0.109375
- up_bias: float32 [192], replicated, may hold values from -3 to 3
Outputs:
- upsampled: bfloat16 [64, 8, 512, 192], P('tm', None, 'tile')
All inputs are finite; a program needn't handle non-finite values.
Results may differ from a plain program's by a relative error of at most 0.0051.
Values may be sent and summed in bfloat16 or wider, within the bound.
No kernel may reach another device: no remote copies, remote signals or barrier semaphores. Data moves between devices by JAX's collectives and lax.ppermute only.
A program may use at most 128 MiB of HBM per device.

v0:
```python
import jax
import jax.numpy as jnp
from jax import lax
from jax.sharding import PartitionSpec as P

GROUPS = 32


epsilon = 1e-06


def extended(cells, sides, width):
    for axis, dim in sides:
        count = lax.axis_size(axis)
        ends = count - 1
        head = lax.slice_in_dim(cells, 0, width, axis=dim)
        tail = lax.slice_in_dim(cells, cells.shape[dim] - width, cells.shape[dim], axis=dim)
        cells = jnp.concatenate(
            [
                lax.ppermute(tail, axis, [(i, (i + 1) % count) for i in range(ends)]),
                cells,
                lax.ppermute(head, axis, [((i + 1) % count, i) for i in range(ends)]),
            ],
            axis=dim,
        )
    return cells


def shifted(array, axis, by):
    size = lax.axis_size(axis)
    pairs = [(i, i + by) for i in range(size) if 0 <= i + by < size]
    return lax.ppermute(array, axis, pairs)


def group_norm(features, norm_gain, norm_bias):
    frames, row_count, col_count, chan_count = features.shape
    group_width = chan_count // GROUPS
    values = features.astype(jnp.float32).reshape(frames, row_count, col_count, GROUPS, group_width)
    members = float(row_count * col_count * lax.axis_size("tile") * group_width)
    sums = lax.psum(jnp.sum(values, axis=(1, 2, 4)), "tile")
    group_mean = (sums / members)[:, None, None, :, None]
    centered = values - group_mean
    spread = lax.psum(jnp.sum(centered * centered, axis=(1, 2, 4)), "tile")
    group_spread = (spread / members)[:, None, None, :, None]
    normed = (centered * lax.rsqrt(group_spread + epsilon)).reshape(
        frames, row_count, col_count, chan_count
    )
    return jax.nn.silu(normed * norm_gain + norm_bias).astype(jnp.bfloat16)


def conv_taps(padded, weight, frames, row_count, col_count):
    chan_count = padded.shape[-1]
    summed_terms = jnp.zeros((frames * row_count * col_count, weight.shape[0]), jnp.float32)
    for kernel_tap in range(27):
        time_step, row_step, col_step = (kernel_tap // 9, kernel_tap // 3 % 3, kernel_tap % 3)
        window_slice = padded[
            time_step : time_step + frames,
            row_step : row_step + row_count,
            col_step : col_step + col_count,
        ].reshape(-1, chan_count)
        summed_terms = summed_terms + lax.dot_general(
            window_slice,
            weight[:, kernel_tap, :],
            (((1,), (1,)), ((), ())),
            preferred_element_type=jnp.float32,
        )
    return summed_terms.reshape(frames, row_count, col_count, -1)


def per_device(features, skip, norm_gain, norm_bias, conv_weight, conv_bias, up_weight, up_bias):
    frames, row_count, col_count, chan_count = features.shape
    activated = group_norm(features, norm_gain, norm_bias)
    widened = extended(activated, (("tile", 2),), 1)
    cached = shifted(widened[frames - 2 :], "tm", 1)
    padded = jnp.pad(jnp.concatenate([cached, widened], axis=0), ((0, 0), (1, 1), (0, 0), (0, 0)))
    full_kernel = lax.all_gather(conv_weight, "tm", axis=0, tiled=True)
    convolved = conv_taps(padded, full_kernel, frames, row_count, col_count)
    summed = (skip.astype(jnp.float32) + convolved + conv_bias).astype(jnp.bfloat16)
    sided = extended(summed, (("tile", 2),), 1)
    lifted = jnp.repeat(jnp.repeat(sided, 2, axis=1), 2, axis=2)[:, :, 1:-1]
    lifted = jnp.pad(lifted, ((0, 0), (1, 1), (0, 0), (0, 0)))
    full_upper = lax.all_gather(up_weight, "tm", axis=0, tiled=True)
    result = jnp.zeros((frames * 4 * row_count * col_count, full_upper.shape[0]), jnp.float32)
    for kernel_tap in range(9):
        row_step, col_step = (kernel_tap // 3, kernel_tap % 3)
        window_slice = lifted[
            :, row_step : row_step + 2 * row_count, col_step : col_step + 2 * col_count
        ].reshape(-1, chan_count)
        result = result + lax.dot_general(
            window_slice,
            full_upper[:, kernel_tap, :],
            (((1,), (1,)), ((), ())),
            preferred_element_type=jnp.float32,
        )
    upsampled = result.reshape(frames, 2 * row_count, 2 * col_count, -1)
    return (upsampled + up_bias).astype(jnp.bfloat16)


def solution(mesh):
    return jax.shard_map(
        per_device,
        mesh=mesh,
        in_specs=(
            P("tm", None, "tile", None),
            P("tm", None, "tile", None),
            P(),
            P(),
            P("tm", None, None),
            P(),
            P("tm", None, None),
            P(),
        ),
        out_specs=P("tm", None, "tile", None),
        check_vma=False,
    )
```

profile of v0, /device:TPU:6, one launch (start us, length us, event | category | flops | bytes accessed | tf_op | source)
XLA Modules:
  0.0 240.3 jit_solution(12397947384214052415)
XLA Ops:
  8.4 55.8 %psum.14 = f32[4,32]{1,0:T(4,128)S(1)} all-reduce(f32[4,32]{1,0:T(4,128)S(1)} %reduce_sum.25), channel_id=1, replica_groups=mesh['tm'=16,'tile'=32] {'tile'}, use_global_device_ids=true, to_apply=%region_2.0 | all-reduce | flops 128 | bytes 1024 | tf_op jit(solution)/shard_map/psum | solution.py:40
  64.5 0.9 fusion.7
  65.6 57.4 %psum.15 = f32[4,32]{1,0:T(4,128)S(1)} all-reduce(f32[4,32]{1,0:T(4,128)S(1)} %reduce_sum.37), channel_id=1, replica_groups=mesh['tm'=16,'tile'=32] {'tile'}, use_global_device_ids=true, to_apply=%region_5.6 | all-reduce | flops 128 | bytes 1024 | tf_op jit(solution)/shard_map/psum | solution.py:43
  123.2 1.0 fusion.15
  124.2 2.3 collective-permute-start
  126.5 5.4 %collective-permute-start.1 = (bf16[4,4,1,384]{3,2,1,0:T(2,128)(2,1)S(1)}, bf16[4,4,1,384]{3,2,1,0:T(2,128)(2,1)S(1)}, u32[]{:S(2)}, u32[]{:S(2)}) collective-permute-start(bf16[4,4,1,384]{3,2,1,0:T(2,128)(2,1)S(1)} %get-tuple-element.52), channel_id=1, source_target_pairs={{1,0},{2,1},{3,2},{4,3},{5,4},{6,5},{7,6},{8,7},{9,8},{10,9},{11,1... | collective-permute-start | bytes 36872 | tf_op jit(solution)/shard_map/ppermute | solution.py:22
  131.9 1.6 copy.37
  133.8 3.1 %collective-permute-start.2 = (bf16[2,4,10,384]{3,2,1,0:T(8,128)(2,1)S(1)}, bf16[2,4,10,384]{3,2,1,0:T(8,128)(2,1)S(1)}, u32[]{:S(2)}, u32[]{:S(2)}) collective-permute-start(bf16[2,4,10,384]{3,2,1,0:T(8,128)(2,1)S(1)} %pad_maximum_fusion.3), channel_id=1, source_target_pairs={{0,32},{32,64},{64,96},{96,128},{128,160},{160,192},{192,224},{224... | collective-permute-start | bytes 184328 | tf_op jit(solution)/shard_map/ppermute | solution.py:32
  137.0 2.1 collective-permute-done.2
  139.6 1.3 fusion.4
  140.9 1.5 fusion.3
  142.5 1.2 convolution_add_fusion.31
  143.7 1.2 convolution_add_fusion.30
  144.8 1.2 convolution_add_fusion.29
  146.0 1.2 convolution_add_fusion.28
  147.2 1.2 convolution_add_fusion.27
  148.5 1.2 convolution_add_fusion.26
  149.7 1.2 convolution_add_fusion.25
  150.9 1.2 convolution_add_fusion.24
  152.1 1.2 convolution_add_fusion.23
  157.2 3.6 %collective-permute-start.3 = (bf16[4,4,1,384]{3,2,1,0:T(2,128)(2,1)S(1)}, bf16[4,4,1,384]{3,2,1,0:T(2,128)(2,1)S(1)}, u32[]{:S(2)}, u32[]{:S(2)}) collective-permute-start(bf16[4,4,1,384]{3,2,1,0:T(2,128)(2,1)S(1)} %get-tuple-element.47), channel_id=1, source_target_pairs={{0,1},{1,2},{2,3},{3,4},{4,5},{5,6},{6,7},{7,8},{8,9},{9,10},{10,1... | collective-permute-start | bytes 36872 | tf_op jit(solution)/shard_map/ppermute | solution.py:20
  160.8 4.1 %collective-permute-start.4 = (bf16[4,4,1,384]{3,2,1,0:T(2,128)(2,1)S(1)}, bf16[4,4,1,384]{3,2,1,0:T(2,128)(2,1)S(1)}, u32[]{:S(2)}, u32[]{:S(2)}) collective-permute-start(bf16[4,4,1,384]{3,2,1,0:T(2,128)(2,1)S(1)} %get-tuple-element.48), channel_id=1, source_target_pairs={{1,0},{2,1},{3,2},{4,3},{5,4},{6,5},{7,6},{8,7},{9,8},{10,9},{11,1... | collective-permute-start | bytes 36872 | tf_op jit(solution)/shard_map/ppermute | solution.py:22
  164.9 56.3 %all-gather.5.cloned.1.call-done = bf16[192,9,384]{2,1,0:T(8,128)(2,1)} async-done(((bf16[12,9,384]{2,1,0:T(8,128)(2,1)}), bf16[192,9,384]{2,1,0:T(8,128)(2,1)}) %all-gather.5.cloned.1.call-update) | async-done | bytes 1327120 | tf_op jit(solution)/shard_map/all_gather | solution.py:82
  221.2 7.0 %fusion.17 = (bf16[192,1,384]{2,1,0:T(2,128)(2,1)S(1)}, bf16[192,1,384]{2,1,0:T(2,128)(2,1)S(1)}, bf16[192,1,384]{2,1,0:T(2,128)(2,1)S(1)}, bf16[192,1,384]{2,1,...) fusion(bf16[192,9,384]{2,1,0:T(8,128)(2,1)} %all-gather.5.clone, ...), kind=kLoop, calls=%fused_computation.121 | loop fusion | bytes 2654208 | tf_op jit(solution)/shard_map/slice | solution.py:91
  (80 shorter events, 12.1 us)
Async XLA Ops:
  6.5 133.0 %all-gather.3.cloned.1.call-start = ((), (), s32[]{:S(2)}) async-start(), calls=%async_computation | async-start | bytes 8460288 | tf_op jit(solution)/shard_map/all_gather | solution.py:76
  7.3 214.0 %all-gather.5.cloned.1.call-start = ((), (), s32[]{:S(2)}) async-start(), calls=%async_computation.1 | async-start | bytes 2506752 | tf_op jit(solution)/shard_map/all_gather | solution.py:82
  124.2 9.3 %collective-permute-start = (bf16[4,4,1,384]{3,2,1,0:T(2,128)(2,1)S(1)}, bf16[4,4,1,384]{3,2,1,0:T(2,128)(2,1)S(1)}, u32[]{:S(2)}, u32[]{:S(2)}) collective-permute-start(bf16[4,4,1,384]{3,2,1,0:T(2,128)(2,1)S(1)} %get-tuple-element.51), channel_id=1, source_target_pairs={{0,1},{1,2},{2,3},{3,4},{4,5},{5,6},{6,7},{7,8},{8,9},{9,10},{10,1... | collective-permute-start | bytes 36872 | tf_op jit(solution)/shard_map/ppermute | solution.py:20
  126.5 7.2 %collective-permute-start.1 = (bf16[4,4,1,384]{3,2,1,0:T(2,128)(2,1)S(1)}, bf16[4,4,1,384]{3,2,1,0:T(2,128)(2,1)S(1)}, u32[]{:S(2)}, u32[]{:S(2)}) collective-permute-start(bf16[4,4,1,384]{3,2,1,0:T(2,128)(2,1)S(1)} %get-tuple-element.52), channel_id=1, source_target_pairs={{1,0},{2,1},{3,2},{4,3},{5,4},{6,5},{7,6},{8,7},{9,8},{10,9},{11,1... | collective-permute-start | bytes 36872 | tf_op jit(solution)/shard_map/ppermute | solution.py:22
  133.8 5.3 %collective-permute-start.2 = (bf16[2,4,10,384]{3,2,1,0:T(8,128)(2,1)S(1)}, bf16[2,4,10,384]{3,2,1,0:T(8,128)(2,1)S(1)}, u32[]{:S(2)}, u32[]{:S(2)}) collective-permute-start(bf16[2,4,10,384]{3,2,1,0:T(8,128)(2,1)S(1)} %pad_maximum_fusion.3), channel_id=1, source_target_pairs={{0,32},{32,64},{64,96},{96,128},{128,160},{160,192},{192,224},{224... | collective-permute-start | bytes 184328 | tf_op jit(solution)/shard_map/ppermute | solution.py:32
  139.6 13.7 %copy-start = (bf16[384,27,384]{2,0,1:T(8,128)(2,1)S(1)}, bf16[384,27,384]{2,0,1:T(8,128)(2,1)}, u32[]{:S(2)}) copy-start(bf16[384,27,384]{2,0,1:T(8,128)(2,1)} %all-gather.3.cloned.1.call-done) | copy-start | bytes 23887876
  148.4 8.7 %copy-start.1 = (bf16[4,4,8,384]{3,2,1,0:T(8,128)(2,1)S(1)}, bf16[4,4,8,384]{3,2,1,0:T(8,128)(2,1)}, u32[]{:S(2)}) copy-start(bf16[4,4,8,384]{3,2,1,0:T(8,128)(2,1)} %param.9) | copy-start | bytes 294916
  148.4 8.7 %copy-start.2 = (f32[384]{0:T(512)S(1)}, f32[384]{0:T(512)}, u32[]{:S(2)}) copy-start(f32[384]{0:T(512)} %param.13) | copy-start | bytes 4612
  157.2 71.0 %collective-permute-start.3 = (bf16[4,4,1,384]{3,2,1,0:T(2,128)(2,1)S(1)}, bf16[4,4,1,384]{3,2,1,0:T(2,128)(2,1)S(1)}, u32[]{:S(2)}, u32[]{:S(2)}) collective-permute-start(bf16[4,4,1,384]{3,2,1,0:T(2,128)(2,1)S(1)} %get-tuple-element.47), channel_id=1, source_target_pairs={{0,1},{1,2},{2,3},{3,4},{4,5},{5,6},{6,7},{7,8},{8,9},{9,10},{10,1... | collective-permute-start | bytes 36872 | tf_op jit(solution)/shard_map/ppermute | solution.py:20
  160.8 67.4 %collective-permute-start.4 = (bf16[4,4,1,384]{3,2,1,0:T(2,128)(2,1)S(1)}, bf16[4,4,1,384]{3,2,1,0:T(2,128)(2,1)S(1)}, u32[]{:S(2)}, u32[]{:S(2)}) collective-permute-start(bf16[4,4,1,384]{3,2,1,0:T(2,128)(2,1)S(1)} %get-tuple-element.48), channel_id=1, source_target_pairs={{1,0},{2,1},{3,2},{4,3},{5,4},{6,5},{7,6},{8,7},{9,8},{10,9},{11,1... | collective-permute-start | bytes 36872 | tf_op jit(solution)/shard_map/ppermute | solution.py:22
  229.5 3.2 %copy-start.3 = (f32[192]{0:T(256)S(1)}, f32[192]{0:T(256)}, u32[]{:S(2)}) copy-start(f32[192]{0:T(256)} %param.15) | copy-start | bytes 2308
Sparse Core Ops, SparseCore 0:
  9.4 106.0 all-gather.2
  133.7 87.4 all-gather.4
where the time goes:
time: 241 us; the launch traced here: 240 us
  blocking collectives  113 us (47%)
  waiting for transfers between devices  59.3 us (25%)
  matrix products  20 us (8%)
  starting transfers between devices  18.5 us (8%)
  between operations  14 us (6%)
  local copies, waits for them, and re-layouts  11.1 us (5%)
  other arithmetic  4.21 us (2%)
    psum x1, blocking collectives, group_norm(): spread = lax.psum(jnp.sum(centered * centered, axis=(1, 2, 4)), 'tile')  57.4 us
    all_gather x1, waiting for transfers between devices, per_device(): full_upper = lax.all_gather(up_weight, 'tm', axis=0, tiled=True)  56.3 us
    psum x1, blocking collectives, group_norm(): sums = lax.psum(jnp.sum(values, axis=(1, 2, 4)), 'tile')  55.8 us
    dot_general x27, matrix products, conv_taps(): lax.dot_general(window_slice, weight[:, kernel_tap, :], (((1,), (1,)), ((...  17.3 us
    ppermute x2, starting transfers between devices, extended(): lax.ppermute(head, axis, [((i + 1) % count, i) for i in range(ends)])  9.5 us
    slice x1, local copies, waits for them, and re-layouts, per_device(): full_upper[:, kernel_tap, :]  7.02 us
    ppermute x2, starting transfers between devices, extended(): lax.ppermute(tail, axis, [(i, (i + 1) % count) for i in range(ends)])  5.85 us
  transfers between devices with their start and end apart: 7, of which 3 were waited for; matrix products, arithmetic and copies ran while one was open for 13% of the time, Pallas kernels for 0%

commit v1 on v0

v1 whole, which is shorter than its diff:
```python
import jax
import jax.numpy as jnp
from jax import lax
from jax.experimental import pallas as pl
from jax.experimental.pallas import tpu as pltpu
from jax.sharding import Mesh
from jax.sharding import PartitionSpec as P

GROUPS = 32
EPSILON = 1e-06
TILE = ("x", "y", "c")


def strip_shift(array, sizes, by):
    count = sizes["x"] * sizes["y"] * sizes["c"]
    return lax.ppermute(array, TILE, [(i, i + by) for i in range(count) if 0 <= i + by < count])


def sibling(array, sizes):
    count = sizes["x"] * sizes["y"] * sizes["c"]
    return lax.ppermute(array, TILE, [(i, i ^ 1) for i in range(count)])


def local_stats(frames6):
    frames, rows, cols, chans = frames6.shape
    width = chans // GROUPS
    values = frames6.astype(jnp.float32)
    chan_mean = jnp.mean(values, axis=(1, 2))
    centered = values - chan_mean[:, None, None, :]
    chan_m2 = jnp.sum(centered * centered, axis=(1, 2))
    chan_mean = chan_mean.reshape(frames, GROUPS, width)
    mean = jnp.mean(chan_mean, axis=2)
    apart = chan_mean - mean[:, :, None]
    m2 = jnp.sum(chan_m2.reshape(frames, GROUPS, width) + rows * cols * apart * apart, axis=2)
    return jnp.stack([mean, m2])


def whole_stats(local, sizes, members):
    count = sizes["x"] * sizes["y"] * sizes["c"]
    spread_out = jnp.broadcast_to(local[None], (count,) + local.shape)
    everyone = lax.all_to_all(spread_out, TILE, 0, 0, tiled=True)
    mean = jnp.mean(everyone[:, 0], axis=0)
    apart = everyone[:, 0] - mean
    m2 = jnp.sum(everyone[:, 1] + members * apart * apart, axis=0)
    return mean, lax.rsqrt(m2 / (members * count) + EPSILON)


def conv_kernel(core_ref, act_ref, weight_ref, out_ref):
    step = pl.program_id(0)
    core = core_ref[0]
    cols = out_ref.shape[0] // act_ref.shape[2]

    @pl.when(step == 0)
    def _():
        out_ref[...] = jnp.zeros_like(out_ref)

    for inner in range(2):
        tap = core * 13 + step * 2 + inner

        def add():
            window = act_ref[tap // 3, pl.ds(tap % 3, cols)].reshape(out_ref.shape[0], -1)
            out_ref[...] += lax.dot_general(
                window, weight_ref[inner], (((1,), (1,)), ((), ())), preferred_element_type=jnp.float32
            )

        if inner == 0:
            pl.when(jnp.logical_or(core == 0, step > 0))(add)
        else:
            add()


def conv_partial(core, act9, weight):
    taps, outs, chans = weight.shape
    positions = (act9.shape[1] - 2) * act9.shape[2]
    return pl.pallas_call(
        conv_kernel,
        grid=(taps // 2,),
        out_shape=jax.ShapeDtypeStruct((positions, outs), jnp.float32),
        in_specs=[
            pl.BlockSpec(memory_space=pltpu.SMEM),
            pl.BlockSpec(act9.shape, lambda i: (0, 0, 0, 0)),
            pl.BlockSpec((2, outs, chans), lambda i: (i, 0, 0)),
        ],
        out_specs=pl.BlockSpec((positions, outs), lambda i: (0, 0)),
        compiler_params=pltpu.CompilerParams(vmem_limit_bytes=32 * 1024 * 1024),
        cost_estimate=pl.CostEstimate(
            flops=2 * positions * outs * chans * taps, bytes_accessed=weight.size * 2, transcendentals=0
        ),
    )(core.reshape(1), act9, weight)


def per_device(sizes, features, skip, norm_gain, norm_bias, conv_weight, conv_bias, up_weight, up_bias):
    frames, rows, cols, chans = features.shape
    strips = sizes["x"] * sizes["y"] * sizes["c"]
    core = lax.axis_index("c")
    pair = lax.axis_index("x") * sizes["y"] + lax.axis_index("y")
    time = lax.axis_index("tm")
    shard = conv_weight.shape[0]

    by_tap = conv_weight.transpose(1, 0, 2)
    share = shard // sizes["y"]
    mine = lax.dynamic_slice(by_tap, (core * 13, lax.axis_index("y") * share, 0), (14, share, chans))
    half_kernel = lax.all_gather(mine, ("tm", "y"), axis=1, tiled=True)

    up_shard, up_taps, _ = up_weight.shape
    half = up_shard // 2
    up_mine = lax.dynamic_slice_in_dim(up_weight, core * half, half, axis=0)
    up_half = lax.all_to_all(
        jnp.broadcast_to(up_mine[None], (sizes["tm"],) + up_mine.shape), "tm", 0, 0, tiled=True
    )
    up_other = sibling(up_half, sizes)
    first = core == 0
    upper = jnp.stack([jnp.where(first, up_half, up_other), jnp.where(first, up_other, up_half)], axis=1)
    upper = upper.reshape(sizes["tm"] * up_shard, up_taps, chans)

    earlier = lax.ppermute(features[frames - 2 :], "tm", [(i, i + 1) for i in range(sizes["tm"] - 1)])
    frames6 = jnp.concatenate([earlier, features], axis=0)
    mean, scale = whole_stats(local_stats(frames6), sizes, float(rows * cols * (chans // GROUPS)))
    parcel = jnp.concatenate([frames6, skip], axis=0)
    other = sibling(parcel, sizes)
    both = jnp.concatenate([jnp.where(first, parcel, other), jnp.where(first, other, parcel)], axis=2)
    left = strip_shift(both[:, :, 2 * cols - 2 :], sizes, 2)
    right = strip_shift(both[:, :, :2], sizes, -2)
    wide = jnp.concatenate([left, both, right], axis=2)

    width = chans // GROUPS
    mean = jnp.repeat(mean, width, axis=1)[:, None, None, :]
    scale = jnp.repeat(scale, width, axis=1)[:, None, None, :]
    normed = (wide[: frames + 2].astype(jnp.float32) - mean) * scale
    activated = jax.nn.silu(normed * norm_gain + norm_bias)
    column = pair * 2 * cols - 2 + jnp.arange(2 * cols + 4)
    inside = jnp.logical_and(column >= 0, column < strips * cols)
    known = jnp.logical_or(time > 0, jnp.arange(frames + 2) >= 2)
    keep = jnp.logical_and(known[:, None, None, None], inside[None, None, :, None])
    activated = jnp.where(keep, activated, 0.0).astype(jnp.bfloat16)

    turned = jnp.pad(activated, ((0, 0), (1, 1), (0, 0), (0, 0))).transpose(2, 1, 0, 3)
    act9 = jnp.stack(
        [
            turned[:, dy : dy + rows, dt : dt + frames].reshape(2 * cols + 4, rows * frames, chans)
            for dt in range(3)
            for dy in range(3)
        ]
    )
    partial = conv_partial(core, act9, half_kernel).reshape(2 * cols + 2, rows * frames, chans)
    own = lax.dynamic_slice_in_dim(partial, core * cols, cols + 2, axis=0)
    sent = lax.dynamic_slice_in_dim(partial, (1 - core) * cols, cols + 2, axis=0)
    convolved = own + sibling(sent, sizes)

    skip10 = lax.dynamic_slice_in_dim(wide[frames + 2 :], 1 + core * cols, cols + 2, axis=2)
    summed = skip10.transpose(2, 1, 0, 3).reshape(cols + 2, rows * frames, chans).astype(jnp.float32)
    summed = summed + convolved + conv_bias
    inside10 = lax.dynamic_slice_in_dim(inside, 1 + core * cols, cols + 2)
    summed = jnp.where(inside10[:, None, None], summed, 0.0).astype(jnp.bfloat16)

    outs = upper.shape[0]
    taps = lax.dot_general(
        summed.reshape(-1, chans),
        upper.transpose(1, 0, 2).reshape(up_taps * outs, chans),
        (((1,), (1,)), ((), ())),
        preferred_element_type=jnp.float32,
    ).reshape(cols + 2, rows, frames, 3, 3, outs)
    taps = jnp.pad(taps, ((0, 0), (1, 1), (0, 0), (0, 0), (0, 0), (0, 0)))
    phases = []
    for low in range(2):
        line = 0.0
        for dy in range(3):
            at = 1 + (low + dy - 1) // 2
            line = line + taps[:, at : at + rows, :, dy]
        for side in range(2):
            total = 0.0
            for dx in range(3):
                at = 1 + (side + dx - 1) // 2
                total = total + line[at : at + cols, :, :, dx]
            phases.append((total + up_bias).astype(jnp.bfloat16))
    fine = jnp.stack(phases).reshape(2, 2, cols, rows, frames, outs)
    return fine.transpose(4, 3, 0, 2, 1, 5).reshape(frames, 2 * rows, 2 * cols, outs)


def solution(mesh):
    strips = mesh.shape["tile"]
    side = 1
    while side * side * 2 < strips:
        side *= 2
    sizes = {"tm": mesh.shape["tm"], "x": strips // (2 * side), "y": side, "c": 2}
    fine_mesh = Mesh(mesh.devices.reshape(tuple(sizes.values())), tuple(sizes))

    def body(*arrays):
        return per_device(sizes, *arrays)

    return jax.shard_map(
        body,
        mesh=fine_mesh,
        in_specs=(
            P("tm", None, TILE, None),
            P("tm", None, TILE, None),
            P(),
            P(),
            P("tm", None, None),
            P(),
            P("tm", None, None),
            P(),
        ),
        out_specs=P("tm", None, TILE, None),
        check_vma=False,
    )
```

time: 241 us -> 205 us (0.85)
  the two profiles are of different devices: /device:TPU:6 before, /device:TPU:1 now
where the time goes in v1:
time: 205 us
  waiting for transfers between devices  95.5 us (47%)
  starting transfers between devices  52.9 us (26%)
  local copies, waits for them, and re-layouts  27.8 us (14%)
  between operations  14 us (7%)
  other arithmetic  8.15 us (4%)
  Pallas kernels  4.11 us (2%)
  matrix products  2.13 us (1%)
    all_gather x1, waiting for transfers between devices, per_device(): half_kernel = lax.all_gather(mine, ('tm', 'y'), axis=1, tiled=True)  67.7 us
    ppermute x3, starting transfers between devices, sibling(): return lax.ppermute(array, TILE, [(i, i ^ 1) for i in range(count)])  19.8 us
    all_to_all x1, waiting for transfers between devices, per_device(): lax.all_to_all(jnp.broadcast_to(up_mine[None], (sizes['tm'],) + up_mine.s...  16.8 us
    all_to_all x1, starting transfers between devices, per_device(): lax.all_to_all(jnp.broadcast_to(up_mine[None], (sizes['tm'],) + up_mine.s...  16.6 us
    all_to_all x1, starting transfers between devices, whole_stats(): everyone = lax.all_to_all(spread_out, TILE, 0, 0, tiled=True)  8.58 us
    unnamed x32, local copies, waits for them, and re-layouts  8.27 us
    all_to_all x1, waiting for transfers between devices, whole_stats(): everyone = lax.all_to_all(spread_out, TILE, 0, 0, tiled=True)  7.27 us
    another operation x10, local copies, waits for them, and re-layouts, per_device(): jnp.stack([turned[:, dy:dy + rows, dt:dt + frames].reshape(2 * cols + 4,...  4.79 us
  transfers between devices with their start and end apart: 9, of which 4 were waited for; matrix products, arithmetic and copies ran while one was open for 15% of the time, Pallas kernels for 2%

profile of v1, /device:TPU:1, one launch (start us, length us, event | category | flops | bytes accessed | tf_op | source)
XLA Modules:
  0.0 204.5 jit_solution(6129854804061115583)
XLA Ops:
  6.5 1.0 copy-done
  9.1 4.4 %collective-permute-start = (bf16[2,4,8,384]{3,2,1,0:T(8,128)(2,1)S(1)}, bf16[2,4,8,384]{3,2,1,0:T(8,128)(2,1)S(1)}, u32[]{:S(2)}, u32[]{:S(2)}) collective-permute-start(bf16[2,4,8,384]{3,2,1,0:T(8,128)(2,1)S(1)} %slice.100), channel_id=1, source_target_pairs={{0,32},{32,64},{64,96},{96,128},{128,160},{160,192},{192,224},{224... | collective-permute-start | bytes 147464 | tf_op jit(solution)/shard_map/ppermute | solution.py:116
  18.0 8.6 %all-to-all-start = ((f32[32,1,384]{2,1,0:T(1,128)}), f32[32,1,384]{2,1,0:T(1,128)S(1)}, u32[]{:S(2)}, u32[]{:S(2)}) async-start(f32[32,1,384]{2,1,0:T(1,128)} %reshape.257), calls=%async_computation | async-start | bytes 98304 | tf_op jit(solution)/shard_map/all_to_all | solution.py:41
  26.7 7.3 %all-to-all-done = f32[32,1,384]{2,1,0:T(1,128)S(1)} async-done(((f32[32,1,384]{2,1,0:T(1,128)}), f32[32,1,384]{2,1,0:T(1,128)S(1)}, u32[]{:S(2)}, u32[]{:S(2)}) %all-to-all-start) | async-done | bytes 49184 | tf_op jit(solution)/shard_map/all_to_all | solution.py:41
  33.9 1.0 broadcast_in_dim.62
  34.9 16.6 %all-to-all-start.1 = ((bf16[16,6,9,384]{3,1,2,0:T(8,128)(2,1)}), bf16[16,6,9,384]{3,1,2,0:T(8,128)(2,1)}, u32[]{:S(2)}, u32[]{:S(2)}) async-start(bf16[16,6,9,384]{3,1,2,0:T(8,128)(2,1)} %broadcast_in_dim.62), calls=%async_computation.1 | async-start | bytes 1769472 | tf_op jit(solution)/shard_map/all_to_all | solution.py:108
  51.6 2.6 %collective-permute-start.1 = (bf16[10,4,8,384]{3,2,1,0:T(8,128)(2,1)S(1)}, bf16[10,4,8,384]{3,2,1,0:T(8,128)(2,1)S(1)}, u32[]{:S(2)}, u32[]{:S(2)}) collective-permute-start(bf16[10,4,8,384]{3,2,1,0:T(8,128)(2,1)S(1)} %constant_dynamic-update-slice_fusion), channel_id=1, source_target_pairs={{0,1},{1,0},{2,3},{3,2},{4,5},{5,4},{6,7},{7,6},{8,9},{9,8},{10,11... | collective-permute-start | bytes 737288 | tf_op jit(solution)/shard_map/ppermute | solution.py:21
  56.1 2.2 %collective-permute-start.2 = (bf16[10,4,2,384]{3,2,1,0:T(2,128)(2,1)S(1)}, bf16[10,4,2,384]{3,2,1,0:T(2,128)(2,1)S(1)}, u32[]{:S(2)}, u32[]{:S(2)}) collective-permute-start(bf16[10,4,2,384]{3,2,1,0:T(2,128)(2,1)S(1)} %slice.131), channel_id=1, source_target_pairs={{0,2},{1,3},{2,4},{3,5},{4,6},{5,7},{6,8},{7,9},{8,10},{9,11},{10,... | collective-permute-start | bytes 184328 | tf_op jit(solution)/shard_map/ppermute | solution.py:16
  58.3 1.3 collective-permute-start.3
  60.1 3.6 %collective-permute-done.3 = bf16[10,4,2,384]{3,2,1,0:T(2,128)(2,1)S(1)} collective-permute-done((bf16[10,4,2,384]{3,2,1,0:T(2,128)(2,1)S(1)}, bf16[10,4,2,384]{3,2,1,0:T(2,128)(2,1)S(1)}, u32[]{:S(2)}, u32[]{:S(2)}) %collective-permute-start.3) | collective-permute-done | bytes 61472 | tf_op jit(solution)/shard_map/ppermute | solution.py:16
  72.7 1.0 constant_dynamic-update-slice_fusion.10
  73.7 1.0 constant_dynamic-update-slice_fusion.9
  74.7 1.0 constant_dynamic-update-slice_fusion.8
  76.7 16.8 %all-to-all-done.1 = bf16[16,6,9,384]{3,1,2,0:T(8,128)(2,1)} async-done(((bf16[16,6,9,384]{3,1,2,0:T(8,128)(2,1)}), bf16[16,6,9,384]{3,1,2,0:T(8,128)(2,1)}, u32[]{:S(2)}, u32[]{:S(2)}) %all-to-all-start.1) | async-done | bytes 663584 | tf_op jit(solution)/shard_map/all_to_all | solution.py:108
  93.5 2.1 %copy.101 = bf16[16,6,9,384]{3,0,2,1:T(8,128)(2,1)} copy(bf16[16,6,9,384]{3,1,2,0:T(8,128)(2,1)} %all-to-all-done.1) | data formatting | bytes 1327104 | tf_op jit(solution)/shard_map/all_to_all | solution.py:108
  95.7 6.5 %collective-permute-start.5 = (bf16[16,6,9,384]{3,0,2,1:T(8,128)(2,1)}, bf16[16,6,9,384]{3,0,2,1:T(8,128)(2,1)}, u32[]{:S(2)}, u32[]{:S(2)}) collective-permute-start(bf16[16,6,9,384]{3,0,2,1:T(8,128)(2,1)} %copy.101), channel_id=1, source_target_pairs={{0,1},{1,0},{2,3},{3,2},{4,5},{5,4},{6,7},{7,6},{8,9},{9,8},{10,11... | collective-permute-start | bytes 1990664 | tf_op jit(solution)/shard_map/ppermute | solution.py:21
  102.4 67.7 %all-gather.2.cloned.1.call-done = bf16[14,384,384]{2,0,1:T(8,128)(2,1)} async-done(((bf16[14,6,384]{2,0,1:T(8,128)(2,1)}), bf16[14,384,384]{2,0,1:T(8,128)(2,1)}) %all-gather.2.cloned.1.call-update) | async-done | bytes 4128784 | tf_op jit(solution)/shard_map/all_gather | solution.py:103
  170.1 3.3 %copy.100.weight_ref = bf16[14,384,384]{2,1,0:T(8,128)(2,1)S(1)} copy(bf16[14,384,384]{2,0,1:T(8,128)(2,1)} %all-gather.2.cloned.1.call-done) | data formatting | bytes 8257536 | tf_op jit(solution)/shard_map/all_gather | solution.py:103
  173.4 4.1 %shard_map.82 = f32[288,384]{1,0:T(8,128)S(1)} custom-call(s32[1]{0:T(128)} %bitcast.1.core_ref, bf16[9,20,16,384]{3,2,1,0:T(8,128)(2,1)S(1)} %constant_dynamic-update-slice_fusion.3.act_ref, bf16[14,384,384]{2,1,0:T(8,128)(2,1)S(1)} %copy.100.weight_ref), custom_call_target="tpu_custom_call" | custom-call | flops 1189085184 | bytes 4128768 | tf_op jit(solution)/shard_map/pallas_call | solution.py:75
  177.5 10.7 %collective-permute-start.4 = (f32[10,16,384]{2,1,0:T(8,128)S(1)}, f32[10,16,384]{2,1,0:T(8,128)}, u32[]{:S(2)}, u32[]{:S(2)}) collective-permute-start(f32[10,16,384]{2,1,0:T(8,128)S(1)} %constant_dynamic-slice_fusion.1), channel_id=1, source_target_pairs={{0,1},{1,0},{2,3},{3,2},{4,5},{5,4},{6,7},{7,6},{8,9},{9,8},{10,11... | collective-permute-start | bytes 737288 | tf_op jit(solution)/shard_map/ppermute | solution.py:21
  188.3 1.6 fusion
  190.6 1.3 reshape.251
  192.0 1.0 select_convert_fusion.1
  193.1 2.1 %fusion.35 = f32[10,4,4,3,3,192]{5,0,4,3,2,1:T(8,128)S(1)} fusion(bf16[10,4,4,384,1,1]{3,0,5,4,2,1:T(8,128)(2,1)S(1)} %bitcast.115, bf16[3,3,192,384,1,1]{3,2,1,0,5,4:T(8,128)(2,1)} %bitcast.112), kind=kOutput, calls=%fused_computation.97 | convolution fusion | flops 212336640 | bytes 2555904 | tf_op jit(solution)/shard_map/dot_general | solution.py:157
  (101 shorter events, 21.6 us)
Async XLA Ops:
  6.5 1.0 copy-start
  6.5 20.1 %copy-start.1 = (bf16[4,4,8,384]{3,2,1,0:T(8,128)(2,1)S(1)}, bf16[4,4,8,384]{3,2,1,0:T(8,128)(2,1)}, u32[]{:S(2)}) copy-start(bf16[4,4,8,384]{3,2,1,0:T(8,128)(2,1)} %param.8) | copy-start | bytes 294916
  6.5 163.5 %all-gather.2.cloned.1.call-start = ((), (), s32[]{:S(2)}) async-start(), calls=%async_computation.2 | async-start | bytes 4792320 | tf_op jit(solution)/shard_map/all_gather | solution.py:103
  9.1 5.5 %collective-permute-start = (bf16[2,4,8,384]{3,2,1,0:T(8,128)(2,1)S(1)}, bf16[2,4,8,384]{3,2,1,0:T(8,128)(2,1)S(1)}, u32[]{:S(2)}, u32[]{:S(2)}) collective-permute-start(bf16[2,4,8,384]{3,2,1,0:T(8,128)(2,1)S(1)} %slice.100), channel_id=1, source_target_pairs={{0,32},{32,64},{64,96},{96,128},{128,160},{160,192},{192,224},{224... | collective-permute-start | bytes 147464 | tf_op jit(solution)/shard_map/ppermute | solution.py:116
  14.6 37.0 %copy-start.4 = (bf16[4,4,8,384]{3,2,1,0:T(8,128)(2,1)S(1)}, bf16[4,4,8,384]{3,2,1,0:T(8,128)(2,1)}, u32[]{:S(2)}) copy-start(bf16[4,4,8,384]{3,2,1,0:T(8,128)(2,1)} %param.9) | copy-start | bytes 294916
  18.0 15.9 %all-to-all-start = ((f32[32,1,384]{2,1,0:T(1,128)}), f32[32,1,384]{2,1,0:T(1,128)S(1)}, u32[]{:S(2)}, u32[]{:S(2)}) async-start(f32[32,1,384]{2,1,0:T(1,128)} %reshape.257), calls=%async_computation | async-start | bytes 98304 | tf_op jit(solution)/shard_map/all_to_all | solution.py:41
  34.9 58.6 %all-to-all-start.1 = ((bf16[16,6,9,384]{3,1,2,0:T(8,128)(2,1)}), bf16[16,6,9,384]{3,1,2,0:T(8,128)(2,1)}, u32[]{:S(2)}, u32[]{:S(2)}) async-start(bf16[16,6,9,384]{3,1,2,0:T(8,128)(2,1)} %broadcast_in_dim.62), calls=%async_computation.1 | async-start | bytes 1769472 | tf_op jit(solution)/shard_map/all_to_all | solution.py:108
  51.6 4.4 %collective-permute-start.1 = (bf16[10,4,8,384]{3,2,1,0:T(8,128)(2,1)S(1)}, bf16[10,4,8,384]{3,2,1,0:T(8,128)(2,1)S(1)}, u32[]{:S(2)}, u32[]{:S(2)}) collective-permute-start(bf16[10,4,8,384]{3,2,1,0:T(8,128)(2,1)S(1)} %constant_dynamic-update-slice_fusion), channel_id=1, source_target_pairs={{0,1},{1,0},{2,3},{3,2},{4,5},{5,4},{6,7},{7,6},{8,9},{9,8},{10,11... | collective-permute-start | bytes 737288 | tf_op jit(solution)/shard_map/ppermute | solution.py:21
  55.6 9.3 %copy-start.5 = (f32[384]{0:T(512)S(1)}, f32[384]{0:T(512)}, u32[]{:S(2)}) copy-start(f32[384]{0:T(512)} %param.11) | copy-start | bytes 4612
  55.7 9.3 %copy-start.6 = (f32[384]{0:T(512)S(1)}, f32[384]{0:T(512)}, u32[]{:S(2)}) copy-start(f32[384]{0:T(512)} %param.10) | copy-start | bytes 4612
  56.1 4.0 %collective-permute-start.2 = (bf16[10,4,2,384]{3,2,1,0:T(2,128)(2,1)S(1)}, bf16[10,4,2,384]{3,2,1,0:T(2,128)(2,1)S(1)}, u32[]{:S(2)}, u32[]{:S(2)}) collective-permute-start(bf16[10,4,2,384]{3,2,1,0:T(2,128)(2,1)S(1)} %slice.131), channel_id=1, source_target_pairs={{0,2},{1,3},{2,4},{3,5},{4,6},{5,7},{6,8},{7,9},{8,10},{9,11},{10,... | collective-permute-start | bytes 184328 | tf_op jit(solution)/shard_map/ppermute | solution.py:16
  58.3 5.4 %collective-permute-start.3 = (bf16[10,4,2,384]{3,2,1,0:T(2,128)(2,1)S(1)}, bf16[10,4,2,384]{3,2,1,0:T(2,128)(2,1)S(1)}, u32[]{:S(2)}, u32[]{:S(2)}) collective-permute-start(bf16[10,4,2,384]{3,2,1,0:T(2,128)(2,1)S(1)} %slice.132), channel_id=1, source_target_pairs={{2,0},{3,1},{4,2},{5,3},{6,4},{7,5},{8,6},{9,7},{10,8},{11,9},{12,... | collective-permute-start | bytes 184328 | tf_op jit(solution)/shard_map/ppermute | solution.py:16
  93.5 8.8 %copy-start.2 = (bf16[1,20,16,384]{3,2,1,0:T(8,128)(2,1)S(1)}, bf16[1,20,16,384]{3,2,1,0:T(8,128)(2,1)}, u32[]{:S(2)}) copy-start(bf16[1,20,16,384]{3,2,1,0:T(8,128)(2,1)} %stack_reshape.35) | copy-start | bytes 737284
  95.7 92.6 %collective-permute-start.5 = (bf16[16,6,9,384]{3,0,2,1:T(8,128)(2,1)}, bf16[16,6,9,384]{3,0,2,1:T(8,128)(2,1)}, u32[]{:S(2)}, u32[]{:S(2)}) collective-permute-start(bf16[16,6,9,384]{3,0,2,1:T(8,128)(2,1)} %copy.101), channel_id=1, source_target_pairs={{0,1},{1,0},{2,3},{3,2},{4,5},{5,4},{6,7},{7,6},{8,9},{9,8},{10,11... | collective-permute-start | bytes 1990664 | tf_op jit(solution)/shard_map/ppermute | solution.py:21
  177.5 14.4 %collective-permute-start.4 = (f32[10,16,384]{2,1,0:T(8,128)S(1)}, f32[10,16,384]{2,1,0:T(8,128)}, u32[]{:S(2)}, u32[]{:S(2)}) collective-permute-start(f32[10,16,384]{2,1,0:T(8,128)S(1)} %constant_dynamic-slice_fusion.1), channel_id=1, source_target_pairs={{0,1},{1,0},{2,3},{3,2},{4,5},{5,4},{6,7},{7,6},{8,9},{9,8},{10,11... | collective-permute-start | bytes 737288 | tf_op jit(solution)/shard_map/ppermute | solution.py:21
  190.6 1.4 copy-start.3
  190.6 1.3 copy-start.7
  195.5 0.7 copy-start.8
Sparse Core Ops, SparseCore 0:
  10.3 159.7 all-gather.1

commit v2 on v1

v2 whole, which is shorter than its diff:
```python
import jax
import jax.numpy as jnp
from jax import lax
from jax.experimental import pallas as pl
from jax.experimental.pallas import tpu as pltpu
from jax.sharding import Mesh
from jax.sharding import PartitionSpec as P

GROUPS = 32
EPSILON = 1e-06
TIME = ("m", "p")
TILE = ("x", "y1", "y0", "c")
QUAD = ("y0", "c")
TEAM = ("p", "y0", "c")
TAPS = 7
PADDED = 48
NT = (((1,), (1,)), ((), ()))


def swap(array, axis):
    return lax.ppermute(array, axis, [(0, 1), (1, 0)])


def strip_shift(array, count, by):
    return lax.ppermute(array, TILE, [(i, i + by) for i in range(count) if 0 <= i + by < count])


def handed_out(array, axes, members):
    return lax.all_to_all(jnp.broadcast_to(array[None], (members,) + array.shape), axes, 0, 0, tiled=True)


def local_stats(values):
    frames, rows, cols, chans = values.shape
    width = chans // GROUPS
    values = values.astype(jnp.float32)
    chan_mean = jnp.mean(values, axis=(1, 2))
    centered = values - chan_mean[:, None, None, :]
    chan_m2 = jnp.sum(centered * centered, axis=(1, 2))
    chan_mean = chan_mean.reshape(frames, GROUPS, width)
    mean = jnp.mean(chan_mean, axis=2)
    apart = chan_mean - mean[:, :, None]
    m2 = jnp.sum(chan_m2.reshape(frames, GROUPS, width) + rows * cols * apart * apart, axis=2)
    return jnp.concatenate([mean, m2], axis=1)


def whole_stats(everyone, members):
    means, m2s = everyone[:, :, :GROUPS], everyone[:, :, GROUPS:]
    mean = jnp.mean(means, axis=0)
    apart = means - mean
    m2 = jnp.sum(m2s + members * apart * apart, axis=0)
    return mean, lax.rsqrt(m2 / (members * everyone.shape[0]) + EPSILON)


def act_kernel(place_ref, wide_ref, mean_ref, scale_ref, gain_ref, bias_ref, out_ref, *, columns):
    frame = pl.program_id(0)
    rows, padded, chans = wide_ref.shape[1:]
    column = place_ref[0] + lax.broadcasted_iota(jnp.int32, (padded, chans), 0)
    keep = jnp.logical_and(column >= 0, column < columns)
    keep = jnp.logical_and(keep, jnp.logical_or(place_ref[1] > 0, frame >= 2))
    nothing = jnp.zeros((padded, chans), out_ref.dtype)
    for dx in range(3):
        out_ref[dx, 0, 0] = nothing
        out_ref[dx, 0, rows + 1] = nothing
    for row in range(rows):
        normed = (wide_ref[0, row].astype(jnp.float32) - mean_ref[0]) * scale_ref[0]
        value = normed * gain_ref[...] + bias_ref[...]
        value = jnp.where(keep, value / (1.0 + jnp.exp(-value)), 0.0)
        for dx in range(3):
            moved = value if dx == 0 else pltpu.roll(value, padded - dx, 0)
            out_ref[dx, 0, row + 1] = moved.astype(out_ref.dtype)


def activate(place, wide, mean, scale, gain, bias, columns):
    frames, rows, padded, chans = wide.shape
    line = pl.BlockSpec((1, 1, chans), lambda t: (t, 0, 0))
    vector = pl.BlockSpec((1, chans), lambda t: (0, 0))

    def kernel(*refs):
        act_kernel(*refs, columns=columns)

    return pl.pallas_call(
        kernel,
        grid=(frames,),
        out_shape=jax.ShapeDtypeStruct((3, frames, rows + 2, padded, chans), jnp.bfloat16),
        in_specs=[
            pl.BlockSpec(memory_space=pltpu.SMEM),
            pl.BlockSpec((1, rows, padded, chans), lambda t: (t, 0, 0, 0)),
            line,
            line,
            vector,
            vector,
        ],
        out_specs=pl.BlockSpec((3, 1, rows + 2, padded, chans), lambda t: (0, t, 0, 0, 0)),
        cost_estimate=pl.CostEstimate(flops=20 * wide.size, bytes_accessed=12 * wide.size, transcendentals=wide.size),
    )(place, wide, mean[:, None], scale[:, None], gain[None], bias[None])


def conv_kernel(place_ref, act_ref, weight_ref, out_ref, total_ref):
    step = pl.program_id(0)
    frames, rows, padded, outs = total_ref.shape

    @pl.when(step == 0)
    def _():
        total_ref[...] = jnp.zeros_like(total_ref)

    tap = place_ref[0] + step

    @pl.when(jnp.logical_or(step > 0, place_ref[1] == 0))
    def _():
        for frame in range(frames):
            window = act_ref[tap % 3, tap // 9 + frame, pl.ds(tap // 3 % 3, rows)]
            part = lax.dot_general(
                window.reshape(rows * padded, -1), weight_ref[0], NT, preferred_element_type=jnp.float32
            )
            total_ref[frame] += part.reshape(rows, padded, outs)

    @pl.when(step == pl.num_programs(0) - 1)
    def _():
        for member in range(out_ref.shape[0]):
            plane, strip = member // 4, member % 4
            span = out_ref.shape[1]
            part = total_ref[plane * span : (plane + 1) * span, :, strip * 8 : strip * 8 + 16]
            out_ref[member] = part.astype(out_ref.dtype)


def conv_partial(place, act, weight):
    taps, outs, chans = weight.shape
    _, frames, rows, padded, _ = act.shape
    frames, rows = frames - 2, rows - 2
    return pl.pallas_call(
        conv_kernel,
        grid=(taps,),
        out_shape=jax.ShapeDtypeStruct((8, frames // 2, rows, 16, outs), jnp.bfloat16),
        in_specs=[
            pl.BlockSpec(memory_space=pltpu.SMEM),
            pl.BlockSpec(act.shape, lambda i: (0, 0, 0, 0, 0)),
            pl.BlockSpec((1, outs, chans), lambda i: (i, 0, 0)),
        ],
        out_specs=pl.BlockSpec((8, frames // 2, rows, 16, outs), lambda i: (0, 0, 0, 0, 0)),
        scratch_shapes=[pltpu.VMEM((frames, rows, padded, outs), jnp.float32)],
        compiler_params=pltpu.CompilerParams(vmem_limit_bytes=40 * 1024 * 1024),
        cost_estimate=pl.CostEstimate(
            flops=2 * frames * rows * padded * outs * chans * taps,
            bytes_accessed=2 * (weight.size + act.size),
            transcendentals=0,
        ),
    )(place, act, weight)


def tail_kernel(place_ref, parts_ref, skip_ref, bias_ref, upper_ref, up_bias_ref, out_ref, tap_ref, fine_ref, *, columns):
    frames, rows, padded, outs = tap_ref.shape[1:]
    half = parts_ref.shape[-1]
    column = place_ref[0] + lax.broadcasted_iota(jnp.int32, (frames, rows, padded, half), 2)
    keep = jnp.logical_and(column >= 0, column < columns)
    summed = []
    for parity in range(2):
        total = parts_ref[4 * parity].astype(jnp.float32)
        for quarter in range(1, 4):
            total = total + parts_ref[4 * parity + quarter].astype(jnp.float32)
        total = skip_ref[parity].astype(jnp.float32) + total + bias_ref[parity]
        total = jnp.where(keep, total, 0.0).astype(jnp.bfloat16)
        summed.append(total.reshape(frames * rows * padded, half))
    for tap in range(9):
        part = lax.dot_general(summed[0], upper_ref[0, tap], NT, preferred_element_type=jnp.float32)
        part = part + lax.dot_general(summed[1], upper_ref[1, tap], NT, preferred_element_type=jnp.float32)
        tap_ref[tap] = part.reshape(frames, rows, padded, outs)

    cols = padded // 2
    for frame in range(frames):
        for row in range(rows):
            for low in range(2):
                lines = []
                for dx in range(3):
                    line = 0.0
                    for dy in range(3):
                        at = row + (low + dy - 1) // 2
                        if 0 <= at < rows:
                            line = line + tap_ref[3 * dy + dx, frame, at]
                    lines.append(line)
                left = lines[0][0:cols] + (lines[1] + lines[2])[1 : 1 + cols]
                right = (lines[0] + lines[1])[1 : 1 + cols] + lines[2][2 : 2 + cols]
                for side, value in ((0, left), (1, right)):
                    value = value + up_bias_ref[...]
                    spare = jnp.zeros((cols, 256 - outs), jnp.float32)
                    fine_ref[0, pl.ds(side, cols, stride=2), :] = value[:, :128]
                    fine_ref[1, pl.ds(side, cols, stride=2), :] = jnp.concatenate([value[:, 128:], spare], axis=1)
                out_ref[frame, 2 * row + low, :, 0:128] = fine_ref[0].astype(out_ref.dtype)
                out_ref[frame, 2 * row + low, :, 128:outs] = fine_ref[1, :, : outs - 128].astype(out_ref.dtype)


def tail(place, parts, skip, bias, upper, up_bias, columns):
    _, frames, rows, padded, _ = parts.shape
    outs = upper.shape[2]

    def kernel(*refs):
        tail_kernel(*refs, columns=columns)

    vmem = pl.BlockSpec(memory_space=pltpu.VMEM)
    return pl.pallas_call(
        kernel,
        out_shape=jax.ShapeDtypeStruct((frames, 2 * rows, padded, outs), jnp.bfloat16),
        in_specs=[pl.BlockSpec(memory_space=pltpu.SMEM)] + [vmem] * 5,
        out_specs=vmem,
        scratch_shapes=[
            pltpu.VMEM((9, frames, rows, padded, outs), jnp.float32),
            pltpu.VMEM((2, padded, 128), jnp.float32),
        ],
        compiler_params=pltpu.CompilerParams(vmem_limit_bytes=40 * 1024 * 1024),
        cost_estimate=pl.CostEstimate(
            flops=2 * frames * rows * padded * upper.size, bytes_accessed=2 * upper.size, transcendentals=0
        ),
    )(place, parts, skip, bias, upper, up_bias)


def per_device(sizes, features, skip, norm_gain, norm_bias, conv_weight, conv_bias, up_weight, up_bias):
    frames, rows, cols, chans = features.shape
    strips = sizes["x"] * sizes["y1"] * 4
    columns = strips * cols
    planes = sizes["m"] * 2
    quarter = 2 * lax.axis_index("y0") + lax.axis_index("c")
    quad = lax.axis_index("x") * sizes["y1"] + lax.axis_index("y1")
    strip = 4 * quad + quarter
    pair = lax.axis_index("m")

    first_tap = jnp.minimum(quarter * TAPS, 27 - TAPS)
    mine = lax.dynamic_slice_in_dim(conv_weight, first_tap, TAPS, axis=1)
    kernel = lax.all_gather(mine, "m", axis=0, tiled=True).transpose(1, 0, 2)

    other = swap(features, "p")
    first = lax.axis_index("p") == 0
    eight = jnp.concatenate([jnp.where(first, features, other), jnp.where(first, other, features)], axis=0)
    back = lax.ppermute(eight[2 * frames - 2 :], "m", [(i, i + 1) for i in range(sizes["m"] - 1)])
    ten = jnp.concatenate([back, eight], axis=0)
    up_shard, up_taps, _ = up_weight.shape
    share = up_shard // 4
    up_mine = lax.dynamic_slice_in_dim(up_weight, quarter * share, share, axis=0)
    up_mine, ten = lax.optimization_barrier((up_mine, ten))
    up_mine = handed_out(up_mine, TIME, planes)
    everyone = handed_out(local_stats(ten), TILE, strips)

    other = swap(ten, "c")
    first = lax.axis_index("c") == 0
    both = jnp.concatenate([jnp.where(first, ten, other), jnp.where(first, other, ten)], axis=2)
    up_mine, both = lax.optimization_barrier((up_mine, both))
    up_all = handed_out(up_mine, QUAD, 4)
    other = swap(both, "y0")
    first = lax.axis_index("y0") == 0
    four = jnp.concatenate([jnp.where(first, both, other), jnp.where(first, other, both)], axis=2)
    skip, four = lax.optimization_barrier((skip, four))
    left = strip_shift(four[:, :, 4 * cols - 2 :], strips, 4)
    right = strip_shift(four[:, :, :2], strips, -4)
    rest = jnp.zeros((2 * frames + 2, rows, PADDED - 4 * cols - 4, chans), features.dtype)
    wide = jnp.concatenate([left, four, right, rest], axis=2)

    upper = up_all.transpose(3, 1, 0, 2, 4).reshape(up_taps * planes * up_shard, chans)

    shard = conv_weight.shape[0]
    place = jnp.arange(chans).reshape(sizes["m"], 2, shard).transpose(1, 0, 2).reshape(2, chans // 2)
    pick = (place[:, None, :] == jnp.arange(chans)[None, :, None]).astype(jnp.bfloat16)
    upper = lax.dot_general(upper, pick, (((1,), (1,)), ((), ())), preferred_element_type=jnp.float32)
    upper = upper.astype(jnp.bfloat16).reshape(up_taps, planes * up_shard, 2, chans // 2).transpose(2, 0, 1, 3)
    skip_left = strip_shift(skip[:, :, cols - 1 :], strips, 1)
    skip_right = strip_shift(skip[:, :, :1], strips, -1)
    skip_rest = jnp.zeros((frames, rows, cols - 2, chans), skip.dtype)
    skip16 = jnp.concatenate([skip_left, skip, skip_right, skip_rest], axis=2)
    skip16 = [
        jnp.dot(skip16.reshape(-1, chans), pick[parity], preferred_element_type=jnp.float32)
        .astype(jnp.bfloat16)
        .reshape(frames, rows, 2 * cols, chans // 2)
        for parity in range(2)
    ]
    bias = conv_bias.reshape(sizes["m"], 2, shard).transpose(1, 0, 2).reshape(2, 1, 1, 1, chans // 2)

    width = chans // GROUPS
    mean, scale = whole_stats(everyone, float(rows * cols * width))
    mean = jnp.repeat(mean, width, axis=1)
    scale = jnp.repeat(scale, width, axis=1)
    act = activate(
        jnp.stack([quad * 4 * cols - 2, pair]), wide, mean, scale, norm_gain, norm_bias, columns
    )
    parts = conv_partial(jnp.stack([first_tap, (quarter == 3).astype(jnp.int32)]), act, kernel)
    parts = lax.all_to_all(parts, TEAM, 0, 0, tiled=True)
    return tail(
        (strip * cols - 1).reshape(1), parts, jnp.stack(skip16), bias, upper, up_bias[None], columns
    )


def solution(mesh):
    strips = mesh.shape["tile"]
    side = 2
    while side * side * 2 < strips:
        side *= 2
    sizes = {"m": mesh.shape["tm"] // 2, "p": 2, "x": strips // (2 * side), "y1": side // 2, "y0": 2, "c": 2}
    fine_mesh = Mesh(mesh.devices.reshape(tuple(sizes.values())), tuple(sizes))

    def body(*arrays):
        return per_device(sizes, *arrays)

    return jax.shard_map(
        body,
        mesh=fine_mesh,
        in_specs=(
            P(TIME, None, TILE, None),
            P(TIME, None, TILE, None),
            P(),
            P(),
            P(TIME, None, None),
            P(),
            P(TIME, None, None),
            P(),
        ),
        out_specs=P(TIME, None, TILE, None),
        check_vma=False,
    )
```

time: 205 us -> 177 us (0.86)
  waiting for transfers between devices: 95.5 us -> 23 us
  blocking collectives: 0 us -> 35.5 us
  starting transfers between devices: 52.9 us -> 67.6 us
  between operations: 14 us -> 0.45 us
  Pallas kernels: 4.11 us -> 16.1 us
  local copies, waits for them, and re-layouts: 27.8 us -> 19.6 us
  other arithmetic: 8.15 us -> 10.9 us
    all_gather x1 -> x0, waiting for transfers between devices: 67.7 us -> none  [per_device(): half_kernel = lax.all_gather(mine, ('tm', 'y'), axis=1, tiled=True)]
    all_gather x0 -> x1, blocking collectives: none -> 35.5 us  [per_device(): kernel = lax.all_gather(mine, 'm', axis=0, tiled=True).transpose(1, 0, 2)]
    all_to_all x2 -> x4, waiting for transfers between devices: 24.1 us -> 7.58 us  [the longest x3 7.58 us: handed_out(): lax.all_to_all(jnp.broadcast_to(array[None], (members,) + array.shape), a...]
    pallas_call x1 -> x3, Pallas kernels: 4.11 us -> 16.1 us  [the longest x1 8.22 us: activate(): pl.pallas_call(kernel, grid=(frames,), out_shape=jax.ShapeDtypeStruct((3,...]
    all_to_all x2 -> x4, starting transfers between devices: 25.2 us -> 36.4 us  [the longest x3 31.8 us: handed_out(): lax.all_to_all(jnp.broadcast_to(array[None], (members,) + array.shape), a...]
    ppermute x2 -> x4, waiting for transfers between devices: 3.64 us -> 13.4 us  [strip_shift(): lax.ppermute(array, TILE, [(i, i + by) for i in range(count) if 0 <= i +...]
    ppermute x2 -> x4, starting transfers between devices: 3.51 us -> 12.3 us  [strip_shift(): lax.ppermute(array, TILE, [(i, i + by) for i in range(count) if 0 <= i +...]
    ppermute x4, starting transfers between devices: 24.2 us -> 18.9 us  [the longest x3 16.3 us: swap(): return lax.ppermute(array, axis, [(0, 1), (1, 0)])]
  transfers between devices with their start and end apart: 9 -> 12, of which waited for: 4 -> 6; matrix products, arithmetic and copies ran while one was open for 15% -> 16% of each run, Pallas kernels for 2% -> 8%
where the time goes in v2:
time: 177 us; the launch traced here: 176 us
  starting transfers between devices  67.6 us (38%)
  blocking collectives  35.5 us (20%)
  waiting for transfers between devices  23 us (13%)
  local copies, waits for them, and re-layouts  19.6 us (11%)
  Pallas kernels  16.1 us (9%)
  other arithmetic  10.9 us (6%)
  matrix products  2.68 us (2%)
    all_gather x1, blocking collectives, per_device(): kernel = lax.all_gather(mine, 'm', axis=0, tiled=True).transpose(1, 0, 2)  35.5 us
    all_to_all x3, starting transfers between devices, handed_out(): lax.all_to_all(jnp.broadcast_to(array[None], (members,) + array.shape), a...  31.8 us
    ppermute x3, starting transfers between devices, swap(): return lax.ppermute(array, axis, [(0, 1), (1, 0)])  16.3 us
    ppermute x4, waiting for transfers between devices, strip_shift(): lax.ppermute(array, TILE, [(i, i + by) for i in range(count) if 0 <= i +...  13.4 us
    ppermute x4, starting transfers between devices, strip_shift(): lax.ppermute(array, TILE, [(i, i + by) for i in range(count) if 0 <= i +...  12.3 us
    pallas_call x1, Pallas kernels, activate(): pl.pallas_call(kernel, grid=(frames,), out_shape=jax.ShapeDtypeStruct((3,...  8.22 us
    all_to_all x3, waiting for transfers between devices, handed_out(): lax.all_to_all(jnp.broadcast_to(array[None], (members,) + array.shape), a...  7.58 us
    pallas_call x1, Pallas kernels, conv_partial(): pl.pallas_call(conv_kernel, grid=(taps,), out_shape=jax.ShapeDtypeStruct(...  6.02 us
  transfers between devices with their start and end apart: 12, of which 6 were waited for; matrix products, arithmetic and copies ran while one was open for 16% of the time, Pallas kernels for 8%

profile of v2, /device:TPU:1, one launch (start us, length us, event | category | flops | bytes accessed | tf_op | source)
XLA Modules:
  0.0 175.9 jit_solution(14492751758207341985)
XLA Ops:
  0.0 4.5 %collective-permute-start = (bf16[4,4,8,384]{3,2,1,0:T(8,128)(2,1)}, bf16[4,4,8,384]{3,2,1,0:T(8,128)(2,1)S(1)}, u32[]{:S(2)}, u32[]{:S(2)}) collective-permute-start(bf16[4,4,8,384]{3,2,1,0:T(8,128)(2,1)} %param.8), channel_id=1, source_target_pairs={{0,32},{32,0},{1,33},{33,1},{2,34},{34,2},{3,35},{35,3},{4,36},{36... | collective-permute-start | bytes 294920 | tf_op jit(solution)/shard_map/ppermute | solution.py:21
  4.6 35.5 %all_gather.3 = bf16[192,7,384]{2,0,1:T(8,128)(2,1)S(1)} all-gather(bf16[24,7,384]{2,0,1:T(8,128)(2,1)S(1)} %constant_dynamic-slice_fusion), channel_id=1, replica_groups=mesh['m'=8,'p'=2,'x'=4,'y1'=2,'y0'=2,'c'=2] {'m'}, dimensions={0}, use_global_device_ids=true | all-gather | bytes 1161216 | tf_op jit(solution)/shard_map/all_gather | solution.py:227
  42.0 2.6 %collective-permute-start.1 = (bf16[2,4,8,384]{3,2,1,0:T(8,128)(2,1)S(1)}, bf16[2,4,8,384]{3,2,1,0:T(8,128)(2,1)S(1)}, u32[]{:S(2)}, u32[]{:S(2)}) collective-permute-start(bf16[2,4,8,384]{3,2,1,0:T(8,128)(2,1)S(1)} %slice.36), channel_id=1, source_target_pairs={{0,64},{64,128},{128,192},{192,256},{256,320},{320,384},{384,448},... | collective-permute-start | bytes 147464 | tf_op jit(solution)/shard_map/ppermute | solution.py:232
  46.7 10.5 %all-to-all-start = ((bf16[16,3,9,384]{3,1,2,0:T(4,128)(2,1)}), bf16[16,3,9,384]{3,1,2,0:T(4,128)(2,1)S(1)}, u32[]{:S(2)}, u32[]{:S(2)}) async-start(bf16[16,3,9,384]{3,1,2,0:T(4,128)(2,1)} %broadcast_in_dim.20), calls=%async_computation | async-start | bytes 884736 | tf_op jit(solution)/shard_map/all_to_all | solution.py:29
  57.1 8.5 %collective-permute-start.2 = (bf16[10,4,8,384]{3,2,1,0:T(8,128)(2,1)S(1)}, bf16[10,4,8,384]{3,2,1,0:T(8,128)(2,1)S(1)}, u32[]{:S(2)}, u32[]{:S(2)}) collective-permute-start(bf16[10,4,8,384]{3,2,1,0:T(8,128)(2,1)S(1)} %pad_maximum_fusion.3), channel_id=1, source_target_pairs={{0,1},{1,0},{2,3},{3,2},{4,5},{5,4},{6,7},{7,6},{8,9},{9,8},{10,11... | collective-permute-start | bytes 737288 | tf_op jit(solution)/shard_map/ppermute | solution.py:21
  67.5 5.3 %all-to-all-done = bf16[16,3,9,384]{3,1,2,0:T(4,128)(2,1)S(1)} async-done(((bf16[16,3,9,384]{3,1,2,0:T(4,128)(2,1)}), bf16[16,3,9,384]{3,1,2,0:T(4,128)(2,1)S(1)}, u32[]{:S(2)}, u32[]{:S(2)}) %all-to-all-start) | async-done | bytes 331808 | tf_op jit(solution)/shard_map/all_to_all | solution.py:29
  72.8 17.5 %all-to-all-start.1 = ((f32[32,1,640]{2,1,0:T(1,128)}), f32[32,1,640]{2,1,0:T(1,128)S(1)}, u32[]{:S(2)}, u32[]{:S(2)}) async-start(f32[32,1,640]{2,1,0:T(1,128)} %reshape.117), calls=%async_computation.1 | async-start | bytes 163840 | tf_op jit(solution)/shard_map/all_to_all | solution.py:29
  90.3 3.3 %collective-permute-start.3 = (bf16[10,4,16,384]{3,2,1,0:T(8,128)(2,1)S(1)}, bf16[10,4,16,384]{3,2,1,0:T(8,128)(2,1)}, u32[]{:S(2)}, u32[]{:S(2)}) collective-permute-start(bf16[10,4,16,384]{3,2,1,0:T(8,128)(2,1)S(1)} %pad_maximum_fusion.1), channel_id=1, source_target_pairs={{0,2},{2,0},{1,3},{3,1},{4,6},{6,4},{5,7},{7,5},{8,10},{10,8},{9,1... | collective-permute-start | bytes 1474568 | tf_op jit(solution)/shard_map/ppermute | solution.py:21
  95.4 2.3 %all-to-all-done.1 = f32[32,1,640]{2,1,0:T(1,128)S(1)} async-done(((f32[32,1,640]{2,1,0:T(1,128)}), f32[32,1,640]{2,1,0:T(1,128)S(1)}, u32[]{:S(2)}, u32[]{:S(2)}) %all-to-all-start.1) | async-done | bytes 81952 | tf_op jit(solution)/shard_map/all_to_all | solution.py:29
  100.6 3.9 %all-to-all-start.3 = ((bf16[4,16,3,9,384]{4,1,3,2,0:T(8,128)(2,1)}), bf16[4,16,3,9,384]{4,1,3,2,0:T(8,128)(2,1)S(1)}, u32[]{:S(2)}, u32[]{:S(2)}) async-start(bf16[4,16,3,9,384]{4,1,3,2,0:T(8,128)(2,1)} %broadcast_in_dim.51), calls=%async_computation.3 | async-start | bytes 2654208 | tf_op jit(solution)/shard_map/all_to_all | solution.py:29
  110.1 5.5 %collective-permute-start.4 = (bf16[10,4,2,384]{3,2,1,0:T(2,128)(2,1)S(1)}, bf16[10,4,2,384]{3,2,1,0:T(2,128)(2,1)S(1)}, u32[]{:S(2)}, u32[]{:S(2)}) collective-permute-start(bf16[10,4,2,384]{3,2,1,0:T(2,128)(2,1)S(1)} %get-tuple-element.17), channel_id=1, source_target_pairs={{0,4},{1,5},{2,6},{3,7},{4,8},{5,9},{6,10},{7,11},{8,12},{9,13},{1... | collective-permute-start | bytes 184328 | tf_op jit(solution)/shard_map/ppermute | solution.py:25
  117.4 5.6 %collective-permute-done.5 = bf16[10,4,2,384]{3,2,1,0:T(2,128)(2,1)S(1)} collective-permute-done((bf16[10,4,2,384]{3,2,1,0:T(2,128)(2,1)S(1)}, bf16[10,4,2,384]{3,2,1,0:T(2,128)(2,1)S(1)}, u32[]{:S(2)}, u32[]{:S(2)}) %collective-permute-start.5) | collective-permute-done | bytes 61472 | tf_op jit(solution)/shard_map/ppermute | solution.py:25
  123.0 3.1 %maximum_maximum_fusion.refs_1_ = bf16[10,4,48,384]{3,2,1,0:T(8,128)(2,1)} fusion(bf16[10,4,2,384]{3,2,1,0:T(2,128)(2,1)S(1)} %collective-permute-done.5, bf16[10,4,32,384]{3,2,1,0:T(8,128)(2,1)} %pad_maximum_fusion, bf16[10,4,2,384]{3,2,1,0:T(2,128)(2,1)S(1)} %collective-permute-done.4, bf16[48]{0:T(256)(128)(2,1)S(1)} %pad.11.clone), kind=kLoop, calls=%fused_computation | loop fusion | flops 5898240 | bytes 2580576 | tf_op jit(solution)/shard_map/concatenate | solution.py:253
  126.1 8.2 %shard_map.82.act_ref = bf16[3,10,6,48,384]{4,3,2,1,0:T(8,128)(2,1)} custom-call(s32[2]{0:T(128)} %pad_add_fusion.1.refs_0_, bf16[10,4,48,384]{3,2,1,0:T(8,128)(2,1)} %maximum_maximum_fusion.refs_1_, f32[10,1,384]{2,1,0:T(1,128)} %broadcast_in_dim_reshape.9.refs_2_, f32[10,1,384]{2,1,0:T(1,128)} %broadcast_in_dim_reshape.10.refs_3_, ...), custom_call_target="tpu_custom_call" | custom-call | flops 14745600 | bytes 8847360 | tf_op jit(solution)/shard_map/pallas_call | solution.py:81
  134.3 2.9 %copy-done.1 = bf16[3,10,6,48,384]{4,3,2,1,0:T(8,128)(2,1)S(1)} copy-done((bf16[3,10,6,48,384]{4,3,2,1,0:T(8,128)(2,1)S(1)}, bf16[3,10,6,48,384]{4,3,2,1,0:T(8,128)(2,1)}, u32[]{:S(2)}) %copy-start.1) | copy-done | bytes 6635544
  137.2 6.0 %shard_map.83 = bf16[8,4,4,16,192]{4,3,2,1,0:T(8,128)(2,1)} custom-call(s32[2]{0:T(128)S(1)} %pad_add_fusion.place_ref, bf16[3,10,6,48,384]{4,3,2,1,0:T(8,128)(2,1)S(1)} %copy-done.1, bf16[7,192,384]{2,1,0:T(8,128)(2,1)S(1)} %bitcast.30), custom_call_target="tpu_custom_call" | custom-call | flops 1585446912 | bytes 7667712 | tf_op jit(solution)/shard_map/pallas_call | solution.py:130
  143.2 4.5 %all-to-all-start.2 = ((bf16[8,4,4,16,192]{4,3,2,1,0:T(8,128)(2,1)}), bf16[8,4,4,16,192]{4,3,2,1,0:T(8,128)(2,1)S(1)}, u32[]{:S(2)}, u32[]{:S(2)}) async-start(bf16[8,4,4,16,192]{4,3,2,1,0:T(8,128)(2,1)} %shard_map.83), calls=%async_computation.2 | async-start | bytes 2097152 | tf_op jit(solution)/shard_map/all_to_all | solution.py:282
  148.0 2.0 %collective-permute-start.7 = (bf16[4,4,1,384]{3,2,1,0:T(2,128)(2,1)S(1)}, bf16[4,4,1,384]{3,2,1,0:T(2,128)(2,1)S(1)}, u32[]{:S(2)}, u32[]{:S(2)}) collective-permute-start(bf16[4,4,1,384]{3,2,1,0:T(2,128)(2,1)S(1)} %get-tuple-element.26), channel_id=1, source_target_pairs={{1,0},{2,1},{3,2},{4,3},{5,4},{6,5},{7,6},{8,7},{9,8},{10,9},{11,1... | collective-permute-start | bytes 36872 | tf_op jit(solution)/shard_map/ppermute | solution.py:25
  150.0 3.5 %collective-permute-start.6 = (bf16[4,4,1,384]{3,2,1,0:T(2,128)(2,1)S(1)}, bf16[4,4,1,384]{3,2,1,0:T(2,128)(2,1)S(1)}, u32[]{:S(2)}, u32[]{:S(2)}) collective-permute-start(bf16[4,4,1,384]{3,2,1,0:T(2,128)(2,1)S(1)} %get-tuple-element.25), channel_id=1, source_target_pairs={{0,1},{1,2},{2,3},{3,4},{4,5},{5,6},{6,7},{7,8},{8,9},{9,10},{10,1... | collective-permute-start | bytes 36872 | tf_op jit(solution)/shard_map/ppermute | solution.py:25
  154.0 7.8 %collective-permute-done.7 = bf16[4,4,1,384]{3,2,1,0:T(2,128)(2,1)S(1)} collective-permute-done((bf16[4,4,1,384]{3,2,1,0:T(2,128)(2,1)S(1)}, bf16[4,4,1,384]{3,2,1,0:T(2,128)(2,1)S(1)}, u32[]{:S(2)}, u32[]{:S(2)}) %collective-permute-start.7) | collective-permute-done | bytes 12320 | tf_op jit(solution)/shard_map/ppermute | solution.py:25
  163.4 2.0 %copy.42 = bf16[9,16,4,3,384]{4,3,2,1,0:T(4,128)(2,1)S(1)} copy(bf16[9,16,4,3,384]{4,1,0,3,2:T(8,128)(2,1)} %bitcast.33) | data formatting | bytes 2654208 | tf_op jit(solution)/shard_map/transpose | solution.py:255
  165.5 2.3 %reshape.106 = bf16[1728,384]{1,0:T(8,128)(2,1)} reshape(bf16[9,16,4,3,384]{4,3,2,1,0:T(4,128)(2,1)S(1)} %copy.42) | data formatting | bytes 2654208 | tf_op jit(solution)/shard_map/reshape | solution.py:255
  167.8 2.2 %fusion.8 = f32[1728,384]{0,1:S(1)} fusion(bf16[1728,384]{1,0:T(8,128)(2,1)} %reshape.106, pred[384,384]{0,1:T(32,128)(4,1)S(1)} %bitcast.34), kind=kOutput, calls=%fused_computation.41 | convolution fusion | flops 509607936 | bytes 4128768
  174.0 1.8 %shard_map.84 = bf16[4,8,16,192]{3,2,1,0:T(8,128)(2,1)} custom-call(s32[1]{0:T(128)} %bitcast.refs_0_, bf16[8,4,4,16,192]{4,3,2,1,0:T(8,128)(2,1)S(1)} %all-to-all-done.2.refs_1_, bf16[2,4,4,16,192]{4,3,2,1,0:T(8,128)(2,1)S(1)} %copy-done.2, f32[2,1,1,1,192]{4,3,2,1,0:T(1,128)S(1)} %reshape.105.refs_3_, bf16[2,9,192,192]{3,2,1,0:T(8,128)(2,1)S(1)} %bitcast.29, ...), custom_call_target="tpu_custom_call" | custom-call | flops 339738624 | bytes 1327104 | tf_op jit(solution)/shard_map/pallas_call | solution.py:199
  (87 shorter events, 23.9 us)
Async XLA Ops:
  0.0 4.5 %copy-start = (bf16[24,27,384]{2,0,1:T(8,128)(2,1)S(1)}, bf16[24,27,384]{2,0,1:T(8,128)(2,1)}, u32[]{:S(2)}) copy-start(bf16[24,27,384]{2,0,1:T(8,128)(2,1)} %param.12) | copy-start | bytes 1492996
  0.0 41.0 %collective-permute-start = (bf16[4,4,8,384]{3,2,1,0:T(8,128)(2,1)}, bf16[4,4,8,384]{3,2,1,0:T(8,128)(2,1)S(1)}, u32[]{:S(2)}, u32[]{:S(2)}) collective-permute-start(bf16[4,4,8,384]{3,2,1,0:T(8,128)(2,1)} %param.8), channel_id=1, source_target_pairs={{0,32},{32,0},{1,33},{33,1},{2,34},{34,2},{3,35},{35,3},{4,36},{36... | collective-permute-start | bytes 294920 | tf_op jit(solution)/shard_map/ppermute | solution.py:21
  42.0 3.8 %collective-permute-start.1 = (bf16[2,4,8,384]{3,2,1,0:T(8,128)(2,1)S(1)}, bf16[2,4,8,384]{3,2,1,0:T(8,128)(2,1)S(1)}, u32[]{:S(2)}, u32[]{:S(2)}) collective-permute-start(bf16[2,4,8,384]{3,2,1,0:T(8,128)(2,1)S(1)} %slice.36), channel_id=1, source_target_pairs={{0,64},{64,128},{128,192},{192,256},{256,320},{320,384},{384,448},... | collective-permute-start | bytes 147464 | tf_op jit(solution)/shard_map/ppermute | solution.py:232
  46.7 26.1 %all-to-all-start = ((bf16[16,3,9,384]{3,1,2,0:T(4,128)(2,1)}), bf16[16,3,9,384]{3,1,2,0:T(4,128)(2,1)S(1)}, u32[]{:S(2)}, u32[]{:S(2)}) async-start(bf16[16,3,9,384]{3,1,2,0:T(4,128)(2,1)} %broadcast_in_dim.20), calls=%async_computation | async-start | bytes 884736 | tf_op jit(solution)/shard_map/all_to_all | solution.py:29
  57.1 10.3 %collective-permute-start.2 = (bf16[10,4,8,384]{3,2,1,0:T(8,128)(2,1)S(1)}, bf16[10,4,8,384]{3,2,1,0:T(8,128)(2,1)S(1)}, u32[]{:S(2)}, u32[]{:S(2)}) collective-permute-start(bf16[10,4,8,384]{3,2,1,0:T(8,128)(2,1)S(1)} %pad_maximum_fusion.3), channel_id=1, source_target_pairs={{0,1},{1,0},{2,3},{3,2},{4,5},{5,4},{6,7},{7,6},{8,9},{9,8},{10,11... | collective-permute-start | bytes 737288 | tf_op jit(solution)/shard_map/ppermute | solution.py:21
  66.0 28.2 %copy-start.7 = (f32[384]{0:T(512)S(1)}, f32[384]{0:T(512)}, u32[]{:S(2)}) copy-start(f32[384]{0:T(512)} %param.10) | copy-start | bytes 4612
  66.0 28.7 %copy-start.8 = (f32[384]{0:T(512)S(1)}, f32[384]{0:T(512)}, u32[]{:S(2)}) copy-start(f32[384]{0:T(512)} %param.11) | copy-start | bytes 4612
  72.8 24.9 %all-to-all-start.1 = ((f32[32,1,640]{2,1,0:T(1,128)}), f32[32,1,640]{2,1,0:T(1,128)S(1)}, u32[]{:S(2)}, u32[]{:S(2)}) async-start(f32[32,1,640]{2,1,0:T(1,128)} %reshape.117), calls=%async_computation.1 | async-start | bytes 163840 | tf_op jit(solution)/shard_map/all_to_all | solution.py:29
  90.3 15.2 %collective-permute-start.3 = (bf16[10,4,16,384]{3,2,1,0:T(8,128)(2,1)S(1)}, bf16[10,4,16,384]{3,2,1,0:T(8,128)(2,1)}, u32[]{:S(2)}, u32[]{:S(2)}) collective-permute-start(bf16[10,4,16,384]{3,2,1,0:T(8,128)(2,1)S(1)} %pad_maximum_fusion.1), channel_id=1, source_target_pairs={{0,2},{2,0},{1,3},{3,1},{4,6},{6,4},{5,7},{7,5},{8,10},{10,8},{9,1... | collective-permute-start | bytes 1474568 | tf_op jit(solution)/shard_map/ppermute | solution.py:21
  100.6 42.6 %all-to-all-start.3 = ((bf16[4,16,3,9,384]{4,1,3,2,0:T(8,128)(2,1)}), bf16[4,16,3,9,384]{4,1,3,2,0:T(8,128)(2,1)S(1)}, u32[]{:S(2)}, u32[]{:S(2)}) async-start(bf16[4,16,3,9,384]{4,1,3,2,0:T(8,128)(2,1)} %broadcast_in_dim.51), calls=%async_computation.3 | async-start | bytes 2654208 | tf_op jit(solution)/shard_map/all_to_all | solution.py:29
  108.8 14.1 %collective-permute-start.5 = (bf16[10,4,2,384]{3,2,1,0:T(2,128)(2,1)S(1)}, bf16[10,4,2,384]{3,2,1,0:T(2,128)(2,1)S(1)}, u32[]{:S(2)}, u32[]{:S(2)}) collective-permute-start(bf16[10,4,2,384]{3,2,1,0:T(2,128)(2,1)S(1)} %get-tuple-element.18), channel_id=1, source_target_pairs={{4,0},{5,1},{6,2},{7,3},{8,4},{9,5},{10,6},{11,7},{12,8},{13,9},{1... | collective-permute-start | bytes 184328 | tf_op jit(solution)/shard_map/ppermute | solution.py:25
  110.1 12.8 %collective-permute-start.4 = (bf16[10,4,2,384]{3,2,1,0:T(2,128)(2,1)S(1)}, bf16[10,4,2,384]{3,2,1,0:T(2,128)(2,1)S(1)}, u32[]{:S(2)}, u32[]{:S(2)}) collective-permute-start(bf16[10,4,2,384]{3,2,1,0:T(2,128)(2,1)S(1)} %get-tuple-element.17), channel_id=1, source_target_pairs={{0,4},{1,5},{2,6},{3,7},{4,8},{5,9},{6,10},{7,11},{8,12},{9,13},{1... | collective-permute-start | bytes 184328 | tf_op jit(solution)/shard_map/ppermute | solution.py:25
  134.3 2.9 %copy-start.1 = (bf16[3,10,6,48,384]{4,3,2,1,0:T(8,128)(2,1)S(1)}, bf16[3,10,6,48,384]{4,3,2,1,0:T(8,128)(2,1)}, u32[]{:S(2)}) copy-start(bf16[3,10,6,48,384]{4,3,2,1,0:T(8,128)(2,1)} %shard_map.82.act_ref) | copy-start | bytes 19906564
  143.2 4.7 %copy-start.5 = (bf16[4,4,8,384]{3,2,1,0:T(8,128)(2,1)S(1)}, bf16[4,4,8,384]{3,2,1,0:T(8,128)(2,1)}, u32[]{:S(2)}) copy-start(bf16[4,4,8,384]{3,2,1,0:T(8,128)(2,1)} %param.9) | copy-start | bytes 294916
  143.2 10.6 %copy-start.6 = (f32[384]{0:T(512)S(1)}, f32[384]{0:T(512)}, u32[]{:S(2)}) copy-start(f32[384]{0:T(512)} %param.13) | copy-start | bytes 4612
  143.2 19.4 %copy-start.4 = (bf16[4,16,3,9,384]{4,1,3,2,0:T(8,128)(2,1)}, bf16[4,16,3,9,384]{4,1,3,2,0:T(8,128)(2,1)S(1)}, u32[]{:S(2)}) copy-start(bf16[4,16,3,9,384]{4,1,3,2,0:T(8,128)(2,1)S(1)} %all-to-all-done.3) | copy-start | bytes 3981316
  143.2 29.8 %all-to-all-start.2 = ((bf16[8,4,4,16,192]{4,3,2,1,0:T(8,128)(2,1)}), bf16[8,4,4,16,192]{4,3,2,1,0:T(8,128)(2,1)S(1)}, u32[]{:S(2)}, u32[]{:S(2)}) async-start(bf16[8,4,4,16,192]{4,3,2,1,0:T(8,128)(2,1)} %shard_map.83), calls=%async_computation.2 | async-start | bytes 2097152 | tf_op jit(solution)/shard_map/all_to_all | solution.py:282
  148.0 13.9 %collective-permute-start.7 = (bf16[4,4,1,384]{3,2,1,0:T(2,128)(2,1)S(1)}, bf16[4,4,1,384]{3,2,1,0:T(2,128)(2,1)S(1)}, u32[]{:S(2)}, u32[]{:S(2)}) collective-permute-start(bf16[4,4,1,384]{3,2,1,0:T(2,128)(2,1)S(1)} %get-tuple-element.26), channel_id=1, source_target_pairs={{1,0},{2,1},{3,2},{4,3},{5,4},{6,5},{7,6},{8,7},{9,8},{10,9},{11,1... | collective-permute-start | bytes 36872 | tf_op jit(solution)/shard_map/ppermute | solution.py:25
  150.0 11.8 %collective-permute-start.6 = (bf16[4,4,1,384]{3,2,1,0:T(2,128)(2,1)S(1)}, bf16[4,4,1,384]{3,2,1,0:T(2,128)(2,1)S(1)}, u32[]{:S(2)}, u32[]{:S(2)}) collective-permute-start(bf16[4,4,1,384]{3,2,1,0:T(2,128)(2,1)S(1)} %get-tuple-element.25), channel_id=1, source_target_pairs={{0,1},{1,2},{2,3},{3,4},{4,5},{5,6},{6,7},{7,8},{8,9},{9,10},{10,1... | collective-permute-start | bytes 36872 | tf_op jit(solution)/shard_map/ppermute | solution.py:25
  171.3 1.8 %copy-start.3 = (f32[192]{0:T(256)S(1)}, f32[192]{0:T(256)}, u32[]{:S(2)}) copy-start(f32[192]{0:T(256)} %param.15) | copy-start | bytes 2308
  173.1 1.0 copy-start.2

commit v3 on v2

v3 whole, which is shorter than its diff:
```python
import jax
import jax.numpy as jnp
from jax import lax
from jax.experimental import pallas as pl
from jax.experimental.pallas import tpu as pltpu
from jax.sharding import Mesh
from jax.sharding import PartitionSpec as P

GROUPS = 32
EPSILON = 1e-06
TIME = ("m", "p")
TILE = ("x", "y1", "y0", "c")
QUAD = ("y0", "c")
TEAM = ("p", "y0", "c")
TAPS = 7
PADDED = 48
NT = (((1,), (1,)), ((), ()))


def swap(array, axis):
    return lax.ppermute(array, axis, [(0, 1), (1, 0)])


def strip_shift(array, count, by):
    return lax.ppermute(array, TILE, [(i, i + by) for i in range(count) if 0 <= i + by < count])


def handed_out(array, axes, members):
    return lax.all_to_all(jnp.broadcast_to(array[None], (members,) + array.shape), axes, 0, 0, tiled=True)


def local_stats(values):
    frames, rows, cols, chans = values.shape
    width = chans // GROUPS
    values = values.astype(jnp.float32)
    chan_mean = jnp.mean(values, axis=(1, 2))
    centered = values - chan_mean[:, None, None, :]
    chan_m2 = jnp.sum(centered * centered, axis=(1, 2))
    chan_mean = chan_mean.reshape(frames, GROUPS, width)
    mean = jnp.mean(chan_mean, axis=2)
    apart = chan_mean - mean[:, :, None]
    m2 = jnp.sum(chan_m2.reshape(frames, GROUPS, width) + rows * cols * apart * apart, axis=2)
    return jnp.concatenate([mean, m2], axis=1)


def whole_stats(everyone, members):
    means, m2s = everyone[:, :, :GROUPS], everyone[:, :, GROUPS:]
    mean = jnp.mean(means, axis=0)
    apart = means - mean
    m2 = jnp.sum(m2s + members * apart * apart, axis=0)
    return mean, lax.rsqrt(m2 / (members * everyone.shape[0]) + EPSILON)


def act_kernel(
    place_ref, own_ref, by_y_ref, by_c_ref, by_yc_ref, left_ref, right_ref, mean_ref, scale_ref, gain_ref, bias_ref,
    out_ref, slab_ref, *, columns,
):
    frames, rows, cols, chans = own_ref.shape
    padded = slab_ref.shape[0]
    first, pair, quarter = place_ref[0], place_ref[1], place_ref[2]
    column = first - 6 + lax.broadcasted_iota(jnp.int32, (padded, chans), 0)
    inside = jnp.logical_and(column >= 0, column < columns)
    slab_ref[...] = jnp.zeros_like(slab_ref)
    nothing = jnp.zeros((padded, chans), out_ref.dtype)

    def one_frame(frame, carry):
        keep = jnp.logical_and(inside, jnp.logical_or(pair > 0, frame >= 2))
        gain = scale_ref[frame] * gain_ref[...]
        for dx in range(3):
            out_ref[dx, frame, 0] = nothing
            out_ref[dx, frame, rows + 1] = nothing
        for row in range(rows):
            for flip, ref in enumerate((own_ref, by_c_ref, by_y_ref, by_yc_ref)):
                at = pl.multiple_of(8 + cols * jnp.bitwise_xor(quarter, flip), 8)
                slab_ref[pl.ds(at, cols), :] = ref[frame, row].astype(jnp.float32)
            slab_ref[6:8, :] = left_ref[frame, row].astype(jnp.float32)
            slab_ref[8 + 4 * cols : 10 + 4 * cols, :] = right_ref[frame, row].astype(jnp.float32)
            value = (slab_ref[...] - mean_ref[frame]) * gain + bias_ref[...]
            value = 0.5 * value
            value = jnp.where(keep, value + value * jnp.tanh(value), 0.0)
            for dx in range(3):
                out_ref[dx, frame, row + 1] = pltpu.roll(value, padded - 6 - dx, 0).astype(out_ref.dtype)
        return carry

    lax.fori_loop(0, frames, one_frame, 0)


def activate(place, strips, left, right, mean, scale, gain, bias, columns):
    frames, rows, cols, chans = strips[0].shape

    def kernel(*refs):
        act_kernel(*refs, columns=columns)

    vmem = pl.BlockSpec(memory_space=pltpu.VMEM)
    return pl.pallas_call(
        kernel,
        out_shape=jax.ShapeDtypeStruct((3, frames, rows + 2, PADDED, chans), jnp.bfloat16),
        in_specs=[pl.BlockSpec(memory_space=pltpu.SMEM)] + [vmem] * 10,
        out_specs=vmem,
        scratch_shapes=[pltpu.VMEM((PADDED, chans), jnp.float32)],
        compiler_params=pltpu.CompilerParams(vmem_limit_bytes=40 * 1024 * 1024),
        cost_estimate=pl.CostEstimate(
            flops=100 * strips[0].size, bytes_accessed=60 * strips[0].size, transcendentals=6 * strips[0].size
        ),
    )(place, *strips, left, right, mean[:, None], scale[:, None], gain[None], bias[None])


def conv_kernel(place_ref, act_ref, weight_ref, out_ref, total_ref, held_ref, arrived):
    frames, rows, padded, outs = total_ref.shape
    taps = held_ref.shape[0]
    copies = [pltpu.make_async_copy(weight_ref.at[i], held_ref.at[i], arrived.at[i]) for i in range(taps)]
    for copy in copies:
        copy.start()
    doubled = (place_ref[1] > 0).astype(jnp.float32)
    for i in range(taps):
        copies[i].wait()
        tap = place_ref[0] + i
        window = act_ref[tap % 3, pl.ds(tap // 9, frames), pl.ds(tap // 3 % 3, rows)]
        part = lax.dot_general(
            window.reshape(frames * rows * padded, -1), held_ref[i], NT, preferred_element_type=jnp.float32
        ).reshape(total_ref.shape)
        if i == 0:
            total_ref[...] = part * (1.0 - doubled)
        else:
            total_ref[...] += part
    span = out_ref.shape[1]
    for member in range(out_ref.shape[0]):
        plane, strip = member // 4, member % 4
        part = total_ref[plane * span : (plane + 1) * span, :, strip * 8 : strip * 8 + 16]
        out_ref[member] = part.astype(out_ref.dtype)


def conv_partial(place, act, weight):
    slots, outs, chans = weight.shape
    _, frames, rows, padded, _ = act.shape
    frames, rows = frames - 2, rows - 2
    vmem = pl.BlockSpec(memory_space=pltpu.VMEM)
    return pl.pallas_call(
        conv_kernel,
        out_shape=jax.ShapeDtypeStruct((8, frames // 2, rows, 16, outs), jnp.bfloat16),
        in_specs=[pl.BlockSpec(memory_space=pltpu.SMEM), vmem, pl.BlockSpec(memory_space=pl.ANY)],
        out_specs=vmem,
        scratch_shapes=[
            pltpu.VMEM((frames, rows, padded, outs), jnp.float32),
            pltpu.VMEM((TAPS, outs, chans), jnp.bfloat16),
            pltpu.SemaphoreType.DMA((TAPS,)),
        ],
        compiler_params=pltpu.CompilerParams(vmem_limit_bytes=40 * 1024 * 1024),
        cost_estimate=pl.CostEstimate(
            flops=2 * frames * rows * padded * outs * chans * TAPS,
            bytes_accessed=2 * (TAPS * outs * chans + act.size),
            transcendentals=0,
        ),
    )(place, act, weight)


def tail_kernel(
    place_ref, parts_ref, skip_ref, bias_ref, pick_ref, upper_ref, up_bias_ref, out_ref, tap_ref, fine_ref, *, columns
):
    frames, rows, padded, outs = tap_ref.shape[1:]
    chans = skip_ref.shape[-1]
    flat = (frames * rows * padded, -1)
    column = place_ref[0] + lax.broadcasted_iota(jnp.int32, (frames, rows, padded, chans), 2)
    keep = jnp.logical_and(column >= 0, column < columns)
    summed = skip_ref[...].astype(jnp.float32).reshape(flat[0], chans) + bias_ref[...]
    for parity in range(2):
        total = parts_ref[4 * parity].astype(jnp.float32)
        for quarter in range(1, 4):
            total = total + parts_ref[4 * parity + quarter].astype(jnp.float32)
        total = total.reshape(flat)
        upper_half = total.astype(jnp.bfloat16)
        lower_half = (total - upper_half.astype(jnp.float32)).astype(jnp.bfloat16)
        for part in (lower_half, upper_half):
            summed = summed + jnp.dot(part, pick_ref[parity], preferred_element_type=jnp.float32)
    summed = jnp.where(keep.reshape(flat[0], chans), summed, 0.0).astype(jnp.bfloat16)
    for tap in range(9):
        part = lax.dot_general(summed, upper_ref[tap], NT, preferred_element_type=jnp.float32)
        tap_ref[tap] = part.reshape(frames, rows, padded, outs)

    cols = padded // 2
    for frame in range(frames):
        for row in range(rows):
            for low in range(2):
                lines = []
                for dx in range(3):
                    line = 0.0
                    for dy in range(3):
                        at = row + (low + dy - 1) // 2
                        if 0 <= at < rows:
                            line = line + tap_ref[3 * dy + dx, frame, at]
                    lines.append(line)
                left = lines[0][0:cols] + (lines[1] + lines[2])[1 : 1 + cols]
                right = (lines[0] + lines[1])[1 : 1 + cols] + lines[2][2 : 2 + cols]
                for side, value in ((0, left), (1, right)):
                    value = value + up_bias_ref[...]
                    spare = jnp.zeros((cols, 256 - outs), jnp.float32)
                    fine_ref[0, pl.ds(side, cols, stride=2), :] = value[:, :128]
                    fine_ref[1, pl.ds(side, cols, stride=2), :] = jnp.concatenate([value[:, 128:], spare], axis=1)
                out_ref[frame, 2 * row + low, :, 0:128] = fine_ref[0].astype(out_ref.dtype)
                out_ref[frame, 2 * row + low, :, 128:outs] = fine_ref[1, :, : outs - 128].astype(out_ref.dtype)


def tail(place, parts, skip, bias, pick, upper, up_bias, columns):
    _, frames, rows, padded, _ = parts.shape
    outs = upper.shape[1]

    def kernel(*refs):
        tail_kernel(*refs, columns=columns)

    vmem = pl.BlockSpec(memory_space=pltpu.VMEM)
    return pl.pallas_call(
        kernel,
        out_shape=jax.ShapeDtypeStruct((frames, 2 * rows, padded, outs), jnp.bfloat16),
        in_specs=[pl.BlockSpec(memory_space=pltpu.SMEM)] + [vmem] * 6,
        out_specs=vmem,
        scratch_shapes=[
            pltpu.VMEM((9, frames, rows, padded, outs), jnp.float32),
            pltpu.VMEM((2, padded, 128), jnp.float32),
        ],
        compiler_params=pltpu.CompilerParams(vmem_limit_bytes=40 * 1024 * 1024),
        cost_estimate=pl.CostEstimate(
            flops=2 * frames * rows * padded * upper.size, bytes_accessed=2 * upper.size, transcendentals=0
        ),
    )(place, parts, skip, bias, pick, upper, up_bias)


def per_device(sizes, features, skip, norm_gain, norm_bias, conv_weight, conv_bias, up_weight, up_bias):
    frames, rows, cols, chans = features.shape
    pairs = sizes["m"]
    strips = sizes["x"] * sizes["y1"] * 4
    columns = strips * cols
    core = lax.axis_index("c")
    quarter = 2 * lax.axis_index("y0") + core
    quad = lax.axis_index("x") * sizes["y1"] + lax.axis_index("y1")
    strip = 4 * quad + quarter
    even = lax.axis_index("p") == 0

    shard, up_shard = conv_weight.shape[0], up_weight.shape[0]
    first_tap = jnp.minimum(quarter * TAPS, 27 - TAPS)
    mine = lax.dynamic_slice_in_dim(conv_weight, first_tap, TAPS, axis=1)
    up_mine = lax.dynamic_slice_in_dim(up_weight, core * 3, 6, axis=1).reshape(up_shard, 3, 2, chans)
    up_mine = up_mine.transpose(2, 0, 1, 3).reshape(shard, 3, chans)
    mine = jnp.concatenate([mine, up_mine], axis=1)
    gathered = lax.all_gather(mine, "m", axis=0, tiled=True).transpose(1, 0, 2)

    other = swap(features, "p")
    eight = jnp.concatenate([jnp.where(even, features, other), jnp.where(even, other, features)], axis=0)
    back = lax.ppermute(eight[2 * frames - 2 :], "m", [(i, i + 1) for i in range(pairs - 1)])
    ten = jnp.concatenate([back, eight], axis=0)
    by_y = swap(ten, "y0")
    everyone = handed_out(local_stats(ten), TILE, strips)

    by_c = swap(jnp.stack([ten, by_y]), "c")
    held = (ten, by_c[0], by_y, by_c[1])
    head, tail_end = held[0][:, :, :2], held[0][:, :, cols - 2 :]
    for flip in range(1, 4):
        head = jnp.where(quarter == flip, held[flip][:, :, :2], head)
        tail_end = jnp.where(quarter == 3 - flip, held[flip][:, :, cols - 2 :], tail_end)
    skip, head, tail_end = lax.optimization_barrier((skip, head, tail_end))
    left = strip_shift(tail_end, strips, 4)
    right = strip_shift(head, strips, -4)
    skip_left = strip_shift(skip[:, :, cols - 1 :], strips, 1)
    skip_right = strip_shift(skip[:, :, :1], strips, -1)
    skip_rest = jnp.zeros((frames, rows, cols - 2, chans), skip.dtype)
    skip16 = jnp.concatenate([skip_left, skip, skip_right, skip_rest], axis=2)

    width = chans // GROUPS
    mean, scale = whole_stats(everyone, float(rows * cols * width))
    mean = jnp.repeat(mean, width, axis=1)
    scale = jnp.repeat(scale, width, axis=1)
    place = jnp.stack([quad * 4 * cols - 2, lax.axis_index("m"), quarter])
    act = activate(
        place, (ten, by_y, by_c[0], by_c[1]), left, right, mean, scale, norm_gain, norm_bias, columns
    )

    gathered, act = lax.optimization_barrier((gathered, act))
    up_own = gathered[TAPS:]
    other = swap(up_own, "p")
    up_pair = jnp.stack([jnp.where(even, up_own, other), jnp.where(even, other, up_own)])
    parts = conv_partial(jnp.stack([first_tap, (quarter == 3).astype(jnp.int32)]), act, gathered)
    other = swap(up_pair, "c")
    upper = [
        jnp.where(core == which, up_pair, other)
        .reshape(2, 3, pairs, 2, up_shard, chans)
        .transpose(1, 3, 2, 0, 4, 5)
        .reshape(6, 2 * pairs * up_shard, chans)
        for which in range(2)
    ]
    upper = jnp.concatenate([upper[0][:5], upper[1][2:]], axis=0)

    channel = jnp.arange(chans).reshape(pairs, 2, shard).transpose(1, 0, 2).reshape(2, chans // 2)
    pick = (channel[:, :, None] == jnp.arange(chans)[None, None, :]).astype(jnp.bfloat16)
    parts = lax.all_to_all(parts, TEAM, 0, 0, tiled=True)
    return tail(
        (strip * cols - 1).reshape(1), parts, skip16, conv_bias[None], pick, upper, up_bias[None], columns
    )


def solution(mesh):
    strips = mesh.shape["tile"]
    side = 2
    while side * side * 2 < strips:
        side *= 2
    sizes = {"m": mesh.shape["tm"] // 2, "p": 2, "x": strips // (2 * side), "y1": side // 2, "y0": 2, "c": 2}
    fine_mesh = Mesh(mesh.devices.reshape(tuple(sizes.values())), tuple(sizes))

    def body(*arrays):
        return per_device(sizes, *arrays)

    return jax.shard_map(
        body,
        mesh=fine_mesh,
        in_specs=(
            P(TIME, None, TILE, None),
            P(TIME, None, TILE, None),
            P(),
            P(),
            P(TIME, None, None),
            P(),
            P(TIME, None, None),
            P(),
        ),
        out_specs=P(TIME, None, TILE, None),
        check_vma=False,
    )
```

time: 177 us -> 153 us (0.86)
  the two profiles are of different devices: /device:TPU:1 before, /device:TPU:4 now
where the time goes in v3:
time: 153 us; the launch traced here: 152 us
  waiting for transfers between devices  49.7 us (32%)
  starting transfers between devices  47.7 us (31%)
  local copies, waits for them, and re-layouts  19 us (12%)
  Pallas kernels  14.2 us (9%)
  between operations  14 us (9%)
  other arithmetic  7.7 us (5%)
    ppermute x5, waiting for transfers between devices, swap(): return lax.ppermute(array, axis, [(0, 1), (1, 0)])  20.9 us
    all_gather x1, waiting for transfers between devices, per_device(): gathered = lax.all_gather(mine, 'm', axis=0, tiled=True).transpose(1, 0, 2)  17.2 us
    ppermute x4, starting transfers between devices, strip_shift(): lax.ppermute(array, TILE, [(i, i + by) for i in range(count) if 0 <= i +...  15.7 us
    ppermute x5, starting transfers between devices, swap(): return lax.ppermute(array, axis, [(0, 1), (1, 0)])  15.7 us
    pallas_call x1, Pallas kernels, conv_partial(): pl.pallas_call(conv_kernel, out_shape=jax.ShapeDtypeStruct((8, frames //...  9.57 us
    unnamed x26, local copies, waits for them, and re-layouts  8.57 us
    all_to_all x1, starting transfers between devices, handed_out(): lax.all_to_all(jnp.broadcast_to(array[None], (members,) + array.shape), a...  7.3 us
    ppermute x4, waiting for transfers between devices, strip_shift(): lax.ppermute(array, TILE, [(i, i + by) for i in range(count) if 0 <= i +...  6.68 us
  transfers between devices with their start and end apart: 13, of which 7 were waited for; matrix products, arithmetic and copies ran while one was open for 12% of the time, Pallas kernels for 2%

profile of v3, /device:TPU:4, one launch (start us, length us, event | category | flops | bytes accessed | tf_op | source)
XLA Modules:
  0.0 152.3 jit_solution(13089060151827936450)
XLA Ops:
  6.5 3.9 %collective-permute-start = (bf16[4,4,8,384]{3,2,1,0:T(8,128)(2,1)}, bf16[4,4,8,384]{3,2,1,0:T(8,128)(2,1)S(1)}, u32[]{:S(2)}, u32[]{:S(2)}) collective-permute-start(bf16[4,4,8,384]{3,2,1,0:T(8,128)(2,1)} %param.8), channel_id=1, source_target_pairs={{0,32},{32,0},{1,33},{33,1},{2,34},{34,2},{3,35},{35,3},{4,36},{36... | collective-permute-start | bytes 294920 | tf_op jit(solution)/shard_map/ppermute | solution.py:21
  14.4 5.2 %collective-permute-start.1 = (bf16[2,4,8,384]{3,2,1,0:T(8,128)(2,1)S(1)}, bf16[2,4,8,384]{3,2,1,0:T(8,128)(2,1)S(1)}, u32[]{:S(2)}, u32[]{:S(2)}) collective-permute-start(bf16[2,4,8,384]{3,2,1,0:T(8,128)(2,1)S(1)} %slice.78), channel_id=1, source_target_pairs={{0,64},{64,128},{128,192},{192,256},{256,320},{320,384},{384,448},... | collective-permute-start | bytes 147464 | tf_op jit(solution)/shard_map/ppermute | solution.py:248
  19.7 1.7 %collective-permute-done.1 = bf16[2,4,8,384]{3,2,1,0:T(8,128)(2,1)S(1)} collective-permute-done((bf16[2,4,8,384]{3,2,1,0:T(8,128)(2,1)S(1)}, bf16[2,4,8,384]{3,2,1,0:T(8,128)(2,1)S(1)}, u32[]{:S(2)}, u32[]{:S(2)}) %collective-permute-start.1) | collective-permute-done | bytes 49184 | tf_op jit(solution)/shard_map/ppermute | solution.py:248
  21.4 3.5 %collective-permute-start.2 = (bf16[10,4,8,384]{3,2,1,0:T(8,128)(2,1)S(1)}, bf16[10,4,8,384]{3,2,1,0:T(8,128)(2,1)S(1)}, u32[]{:S(2)}, u32[]{:S(2)}) collective-permute-start(bf16[10,4,8,384]{3,2,1,0:T(8,128)(2,1)S(1)} %get-tuple-element.16.refs_1_), channel_id=1, source_target_pairs={{0,2},{2,0},{1,3},{3,1},{4,6},{6,4},{5,7},{7,5},{8,10},{10,8},{9,1... | collective-permute-start | bytes 737288 | tf_op jit(solution)/shard_map/ppermute | solution.py:21
  26.6 7.3 %all-to-all-start = ((f32[32,1,640]{2,1,0:T(1,128)}), f32[32,1,640]{2,1,0:T(1,128)S(1)}, u32[]{:S(2)}, u32[]{:S(2)}) async-start(f32[32,1,640]{2,1,0:T(1,128)} %reshape.95), calls=%async_computation | async-start | bytes 163840 | tf_op jit(solution)/shard_map/all_to_all | solution.py:29
  34.0 2.1 %collective-permute-start.3 = (bf16[2,10,4,8,384]{4,3,2,1,0:T(8,128)(2,1)S(1)}, bf16[2,10,4,8,384]{4,3,2,1,0:T(8,128)(2,1)S(1)}, u32[]{:S(2)}, u32[]{:S(2)}) collective-permute-start(bf16[2,10,4,8,384]{4,3,2,1,0:T(8,128)(2,1)S(1)} %pad_maximum_fusion.2), channel_id=1, source_target_pairs={{0,1},{1,0},{2,3},{3,2},{4,5},{5,4},{6,7},{7,6},{8,9},{9,8},{10,11... | collective-permute-start | bytes 1474568 | tf_op jit(solution)/shard_map/ppermute | solution.py:21
  36.2 3.3 %all-to-all-done = f32[32,1,640]{2,1,0:T(1,128)S(1)} async-done(((f32[32,1,640]{2,1,0:T(1,128)}), f32[32,1,640]{2,1,0:T(1,128)S(1)}, u32[]{:S(2)}, u32[]{:S(2)}) %all-to-all-start) | async-done | bytes 81952 | tf_op jit(solution)/shard_map/all_to_all | solution.py:29
  41.4 3.0 %collective-permute-start.4 = (bf16[10,4,2,384]{3,2,1,0:T(2,128)(2,1)S(1)}, bf16[10,4,2,384]{3,2,1,0:T(2,128)(2,1)S(1)}, u32[]{:S(2)}, u32[]{:S(2)}) collective-permute-start(bf16[10,4,2,384]{3,2,1,0:T(2,128)(2,1)S(1)} %get-tuple-element.10), channel_id=1, source_target_pairs={{0,4},{1,5},{2,6},{3,7},{4,8},{5,9},{6,10},{7,11},{8,12},{9,13},{1... | collective-permute-start | bytes 184328 | tf_op jit(solution)/shard_map/ppermute | solution.py:25
  44.4 5.3 %collective-permute-start.5 = (bf16[10,4,2,384]{3,2,1,0:T(2,128)(2,1)S(1)}, bf16[10,4,2,384]{3,2,1,0:T(2,128)(2,1)S(1)}, u32[]{:S(2)}, u32[]{:S(2)}) collective-permute-start(bf16[10,4,2,384]{3,2,1,0:T(2,128)(2,1)S(1)} %get-tuple-element.11), channel_id=1, source_target_pairs={{4,0},{5,1},{6,2},{7,3},{8,4},{9,5},{10,6},{11,7},{12,8},{13,9},{1... | collective-permute-start | bytes 184328 | tf_op jit(solution)/shard_map/ppermute | solution.py:25
  50.2 1.8 %collective-permute-done.5.refs_6_ = bf16[10,4,2,384]{3,2,1,0:T(2,128)(2,1)S(1)} collective-permute-done((bf16[10,4,2,384]{3,2,1,0:T(2,128)(2,1)S(1)}, bf16[10,4,2,384]{3,2,1,0:T(2,128)(2,1)S(1)}, u32[]{:S(2)}, u32[]{:S(2)}) %collective-permute-start.5) | collective-permute-done | bytes 61472 | tf_op jit(solution)/shard_map/ppermute | solution.py:25
  52.0 2.5 %shard_map.82.act_ref = bf16[3,10,6,48,384]{4,3,2,1,0:T(8,128)(2,1)S(1)} custom-call(s32[3]{0:T(128)S(1)} %pad_add_fusion.1.refs_0_, bf16[10,4,8,384]{3,2,1,0:T(8,128)(2,1)S(1)} %get-tuple-element.16.refs_1_, bf16[10,4,8,384]{3,2,1,0:T(8,128)(2,1)S(1)} %collective-permute-done.2.refs_2_, bf16[10,4,8,384]{3,2,1,0:T(8,128)(2,1)S(1)} %get-tuple-element.24.refs_3_, ...), custom_call_target="tpu_custom_call" | custom-call | flops 12288000 | bytes 7372800 | tf_op jit(solution)/shard_map/pallas_call | solution.py:95
  54.5 2.7 %copy-done.1 = bf16[3,10,6,48,384]{4,3,2,1,0:T(8,128)(2,1)} copy-done((bf16[3,10,6,48,384]{4,3,2,1,0:T(8,128)(2,1)}, bf16[3,10,6,48,384]{4,3,2,1,0:T(8,128)(2,1)S(1)}, u32[]{:S(2)}) %copy-start.1) | copy-done | bytes 6635544
  57.2 17.2 %all-gather.2.cloned.1.call-done = bf16[192,10,384]{2,0,1:T(8,128)(2,1)} async-done(((bf16[24,10,384]{2,0,1:T(8,128)(2,1)}), bf16[192,10,384]{2,0,1:T(8,128)(2,1)}) %all-gather.2.cloned.1.call-update) | async-done | bytes 1474576 | tf_op jit(solution)/shard_map/all_gather | solution.py:244
  74.4 2.9 %copy-done.2 = bf16[3,10,6,48,384]{4,3,2,1,0:T(8,128)(2,1)S(1)} copy-done((bf16[3,10,6,48,384]{4,3,2,1,0:T(8,128)(2,1)S(1)}, bf16[3,10,6,48,384]{4,3,2,1,0:T(8,128)(2,1)}, u32[]{:S(2)}) %copy-start.2) | copy-done | bytes 6635544
  78.7 9.6 %shard_map.83 = bf16[8,4,4,16,192]{4,3,2,1,0:T(8,128)(2,1)} custom-call(s32[2]{0:T(128)S(1)} %pad_add_fusion.place_ref, bf16[3,10,6,48,384]{4,3,2,1,0:T(8,128)(2,1)S(1)} %copy-done.2, bf16[10,192,384]{2,1,0:T(8,128)(2,1)S(1)} %bitcast.30), custom_call_target="tpu_custom_call" | custom-call | flops 1585446912 | bytes 7667712 | tf_op jit(solution)/shard_map/pallas_call | solution.py:138
  88.2 3.8 %all-to-all-start.1 = ((bf16[8,4,4,16,192]{4,3,2,1,0:T(8,128)(2,1)}), bf16[8,4,4,16,192]{4,3,2,1,0:T(8,128)(2,1)S(1)}, u32[]{:S(2)}, u32[]{:S(2)}) async-start(bf16[8,4,4,16,192]{4,3,2,1,0:T(8,128)(2,1)} %shard_map.83), calls=%async_computation.1 | async-start | bytes 2097152 | tf_op jit(solution)/shard_map/all_to_all | solution.py:293
  92.1 4.2 %collective-permute-start.8 = (bf16[3,192,384]{2,1,0:T(8,128)(2,1)S(1)}, bf16[3,192,384]{2,1,0:T(8,128)(2,1)}, u32[]{:S(2)}, u32[]{:S(2)}) collective-permute-start(bf16[3,192,384]{2,1,0:T(8,128)(2,1)S(1)} %slice.74), channel_id=1, source_target_pairs={{0,32},{32,0},{1,33},{33,1},{2,34},{34,2},{3,35},{35,3},{4,36},{36... | collective-permute-start | bytes 1327112 | tf_op jit(solution)/shard_map/ppermute | solution.py:21
  96.4 19.7 %collective-permute-done.8 = bf16[3,192,384]{2,1,0:T(8,128)(2,1)} collective-permute-done((bf16[3,192,384]{2,1,0:T(8,128)(2,1)S(1)}, bf16[3,192,384]{2,1,0:T(8,128)(2,1)}, u32[]{:S(2)}, u32[]{:S(2)}) %collective-permute-start.8) | collective-permute-done | bytes 442400 | tf_op jit(solution)/shard_map/ppermute | solution.py:21
  117.3 2.1 %collective-permute-start.9 = (bf16[2,3,192,384]{3,2,1,0:T(8,128)(2,1)S(1)}, bf16[2,3,192,384]{3,2,1,0:T(8,128)(2,1)}, u32[]{:S(2)}, u32[]{:S(2)}) collective-permute-start(bf16[2,3,192,384]{3,2,1,0:T(8,128)(2,1)S(1)} %pad_maximum_fusion.1), channel_id=1, source_target_pairs={{0,1},{1,0},{2,3},{3,2},{4,5},{5,4},{6,7},{7,6},{8,9},{9,8},{10,11... | collective-permute-start | bytes 2654216 | tf_op jit(solution)/shard_map/ppermute | solution.py:21
  119.5 5.4 %collective-permute-start.7 = (bf16[4,4,1,384]{3,2,1,0:T(2,128)(2,1)S(1)}, bf16[4,4,1,384]{3,2,1,0:T(2,128)(2,1)S(1)}, u32[]{:S(2)}, u32[]{:S(2)}) collective-permute-start(bf16[4,4,1,384]{3,2,1,0:T(2,128)(2,1)S(1)} %get-tuple-element.28), channel_id=1, source_target_pairs={{1,0},{2,1},{3,2},{4,3},{5,4},{6,5},{7,6},{8,7},{9,8},{10,9},{11,1... | collective-permute-start | bytes 36872 | tf_op jit(solution)/shard_map/ppermute | solution.py:25
  124.9 2.1 %collective-permute-start.6 = (bf16[4,4,1,384]{3,2,1,0:T(2,128)(2,1)S(1)}, bf16[4,4,1,384]{3,2,1,0:T(2,128)(2,1)S(1)}, u32[]{:S(2)}, u32[]{:S(2)}) collective-permute-start(bf16[4,4,1,384]{3,2,1,0:T(2,128)(2,1)S(1)} %get-tuple-element.27), channel_id=1, source_target_pairs={{0,1},{1,2},{2,3},{3,4},{4,5},{5,6},{6,7},{7,8},{8,9},{9,10},{10,1... | collective-permute-start | bytes 36872 | tf_op jit(solution)/shard_map/ppermute | solution.py:25
  127.2 4.9 %collective-permute-done.6 = bf16[4,4,1,384]{3,2,1,0:T(2,128)(2,1)S(1)} collective-permute-done((bf16[4,4,1,384]{3,2,1,0:T(2,128)(2,1)S(1)}, bf16[4,4,1,384]{3,2,1,0:T(2,128)(2,1)S(1)}, u32[]{:S(2)}, u32[]{:S(2)}) %collective-permute-start.6) | collective-permute-done | bytes 12320 | tf_op jit(solution)/shard_map/ppermute | solution.py:25
  137.1 2.0 %reshape.88 = bf16[4,192,384]{2,1,0:T(8,128)(2,1)} reshape(bf16[2,2,8,2,12,384]{5,4,3,2,1,0:T(8,128)(2,1)} %copy.34) | data formatting | bytes 1179648 | tf_op jit(solution)/shard_map/slice | solution.py:289
  143.3 2.1 %shard_map.84 = bf16[4,8,16,192]{3,2,1,0:T(8,128)(2,1)} custom-call(s32[1]{0:T(128)} %bitcast.refs_0_, bf16[8,4,4,16,192]{4,3,2,1,0:T(8,128)(2,1)S(1)} %all-to-all-done.1.refs_1_, bf16[4,4,16,384]{3,2,1,0:T(8,128)(2,1)S(1)} %maximum_maximum_fusion.refs_2_, f32[1,384]{1,0:T(1,128)S(1)} %broadcast_in_dim.37.refs_3_, bf16[2,192,384]{2,1,0:T(8,128)(2,1)S(1)} %fusion.refs_4_, ...), custom_call_target="tpu_custom_call" | custom-call | flops 339738624 | bytes 1327104 | tf_op jit(solution)/shard_map/pallas_call | solution.py:211
  (90 shorter events, 20.4 us)
Async XLA Ops:
  6.5 4.9 %copy-start = (bf16[24,27,384]{2,0,1:T(8,128)(2,1)S(1)}, bf16[24,27,384]{2,0,1:T(8,128)(2,1)}, u32[]{:S(2)}) copy-start(bf16[24,27,384]{2,0,1:T(8,128)(2,1)} %param.12) | copy-start | bytes 1492996
  6.5 67.9 %all-gather.2.cloned.1.call-start = ((), (), s32[]{:S(2)}) async-start(), calls=%async_computation.2 | async-start | bytes 1658880 | tf_op jit(solution)/shard_map/all_gather | solution.py:244
  6.5 6.9 %collective-permute-start = (bf16[4,4,8,384]{3,2,1,0:T(8,128)(2,1)}, bf16[4,4,8,384]{3,2,1,0:T(8,128)(2,1)S(1)}, u32[]{:S(2)}, u32[]{:S(2)}) collective-permute-start(bf16[4,4,8,384]{3,2,1,0:T(8,128)(2,1)} %param.8), channel_id=1, source_target_pairs={{0,32},{32,0},{1,33},{33,1},{2,34},{34,2},{3,35},{35,3},{4,36},{36... | collective-permute-start | bytes 294920 | tf_op jit(solution)/shard_map/ppermute | solution.py:21
  14.4 6.9 %collective-permute-start.1 = (bf16[2,4,8,384]{3,2,1,0:T(8,128)(2,1)S(1)}, bf16[2,4,8,384]{3,2,1,0:T(8,128)(2,1)S(1)}, u32[]{:S(2)}, u32[]{:S(2)}) collective-permute-start(bf16[2,4,8,384]{3,2,1,0:T(8,128)(2,1)S(1)} %slice.78), channel_id=1, source_target_pairs={{0,64},{64,128},{128,192},{192,256},{256,320},{320,384},{384,448},... | collective-permute-start | bytes 147464 | tf_op jit(solution)/shard_map/ppermute | solution.py:248
  21.4 12.5 %collective-permute-start.2 = (bf16[10,4,8,384]{3,2,1,0:T(8,128)(2,1)S(1)}, bf16[10,4,8,384]{3,2,1,0:T(8,128)(2,1)S(1)}, u32[]{:S(2)}, u32[]{:S(2)}) collective-permute-start(bf16[10,4,8,384]{3,2,1,0:T(8,128)(2,1)S(1)} %get-tuple-element.16.refs_1_), channel_id=1, source_target_pairs={{0,2},{2,0},{1,3},{3,1},{4,6},{6,4},{5,7},{7,5},{8,10},{10,8},{9,1... | collective-permute-start | bytes 737288 | tf_op jit(solution)/shard_map/ppermute | solution.py:21
  25.2 10.9 %copy-start.9 = (f32[384]{0:T(512)S(1)}, f32[384]{0:T(512)}, u32[]{:S(2)}) copy-start(f32[384]{0:T(512)} %param.10) | copy-start | bytes 4612
  25.2 10.9 %copy-start.10 = (f32[384]{0:T(512)S(1)}, f32[384]{0:T(512)}, u32[]{:S(2)}) copy-start(f32[384]{0:T(512)} %param.11) | copy-start | bytes 4612
  26.6 12.8 %all-to-all-start = ((f32[32,1,640]{2,1,0:T(1,128)}), f32[32,1,640]{2,1,0:T(1,128)S(1)}, u32[]{:S(2)}, u32[]{:S(2)}) async-start(f32[32,1,640]{2,1,0:T(1,128)} %reshape.95), calls=%async_computation | async-start | bytes 163840 | tf_op jit(solution)/shard_map/all_to_all | solution.py:29
  34.0 7.0 %collective-permute-start.3 = (bf16[2,10,4,8,384]{4,3,2,1,0:T(8,128)(2,1)S(1)}, bf16[2,10,4,8,384]{4,3,2,1,0:T(8,128)(2,1)S(1)}, u32[]{:S(2)}, u32[]{:S(2)}) collective-permute-start(bf16[2,10,4,8,384]{4,3,2,1,0:T(8,128)(2,1)S(1)} %pad_maximum_fusion.2), channel_id=1, source_target_pairs={{0,1},{1,0},{2,3},{3,2},{4,5},{5,4},{6,7},{7,6},{8,9},{9,8},{10,11... | collective-permute-start | bytes 1474568 | tf_op jit(solution)/shard_map/ppermute | solution.py:21
  41.4 8.8 %collective-permute-start.4 = (bf16[10,4,2,384]{3,2,1,0:T(2,128)(2,1)S(1)}, bf16[10,4,2,384]{3,2,1,0:T(2,128)(2,1)S(1)}, u32[]{:S(2)}, u32[]{:S(2)}) collective-permute-start(bf16[10,4,2,384]{3,2,1,0:T(2,128)(2,1)S(1)} %get-tuple-element.10), channel_id=1, source_target_pairs={{0,4},{1,5},{2,6},{3,7},{4,8},{5,9},{6,10},{7,11},{8,12},{9,13},{1... | collective-permute-start | bytes 184328 | tf_op jit(solution)/shard_map/ppermute | solution.py:25
  44.4 7.6 %collective-permute-start.5 = (bf16[10,4,2,384]{3,2,1,0:T(2,128)(2,1)S(1)}, bf16[10,4,2,384]{3,2,1,0:T(2,128)(2,1)S(1)}, u32[]{:S(2)}, u32[]{:S(2)}) collective-permute-start(bf16[10,4,2,384]{3,2,1,0:T(2,128)(2,1)S(1)} %get-tuple-element.11), channel_id=1, source_target_pairs={{4,0},{5,1},{6,2},{7,3},{8,4},{9,5},{10,6},{11,7},{12,8},{13,9},{1... | collective-permute-start | bytes 184328 | tf_op jit(solution)/shard_map/ppermute | solution.py:25
  54.5 2.7 %copy-start.1 = (bf16[3,10,6,48,384]{4,3,2,1,0:T(8,128)(2,1)}, bf16[3,10,6,48,384]{4,3,2,1,0:T(8,128)(2,1)S(1)}, u32[]{:S(2)}) copy-start(bf16[3,10,6,48,384]{4,3,2,1,0:T(8,128)(2,1)S(1)} %shard_map.82.act_ref) | copy-start | bytes 19906564
  74.4 2.9 %copy-start.2 = (bf16[3,10,6,48,384]{4,3,2,1,0:T(8,128)(2,1)S(1)}, bf16[3,10,6,48,384]{4,3,2,1,0:T(8,128)(2,1)}, u32[]{:S(2)}) copy-start(bf16[3,10,6,48,384]{4,3,2,1,0:T(8,128)(2,1)} %copy-done.1) | copy-start | bytes 19906564
  77.3 1.4 copy-start.3
  88.2 3.8 %copy-start.4 = (bf16[192,10,384]{2,0,1:T(8,128)(2,1)S(1)}, bf16[192,10,384]{2,0,1:T(8,128)(2,1)}, u32[]{:S(2)}) copy-start(bf16[192,10,384]{2,0,1:T(8,128)(2,1)} %all-gather.2.cloned.1.call-done) | copy-start | bytes 4423684
  88.2 54.6 %all-to-all-start.1 = ((bf16[8,4,4,16,192]{4,3,2,1,0:T(8,128)(2,1)}), bf16[8,4,4,16,192]{4,3,2,1,0:T(8,128)(2,1)S(1)}, u32[]{:S(2)}, u32[]{:S(2)}) async-start(bf16[8,4,4,16,192]{4,3,2,1,0:T(8,128)(2,1)} %shard_map.83), calls=%async_computation.1 | async-start | bytes 2097152 | tf_op jit(solution)/shard_map/all_to_all | solution.py:293
  92.1 24.0 %collective-permute-start.8 = (bf16[3,192,384]{2,1,0:T(8,128)(2,1)S(1)}, bf16[3,192,384]{2,1,0:T(8,128)(2,1)}, u32[]{:S(2)}, u32[]{:S(2)}) collective-permute-start(bf16[3,192,384]{2,1,0:T(8,128)(2,1)S(1)} %slice.74), channel_id=1, source_target_pairs={{0,32},{32,0},{1,33},{33,1},{2,34},{34,2},{3,35},{35,3},{4,36},{36... | collective-permute-start | bytes 1327112 | tf_op jit(solution)/shard_map/ppermute | solution.py:21
  117.2 7.7 %copy-start.6 = (bf16[1,3,192,384]{3,2,1,0:T(8,128)(2,1)}, bf16[1,3,192,384]{3,2,1,0:T(8,128)(2,1)S(1)}, u32[]{:S(2)}) copy-start(bf16[1,3,192,384]{3,2,1,0:T(8,128)(2,1)S(1)} %get-tuple-element.18) | copy-start | bytes 1327108
  117.2 2.2 %copy-start.8 = (bf16[4,4,8,384]{3,2,1,0:T(8,128)(2,1)S(1)}, bf16[4,4,8,384]{3,2,1,0:T(8,128)(2,1)}, u32[]{:S(2)}) copy-start(bf16[4,4,8,384]{3,2,1,0:T(8,128)(2,1)} %param.9) | copy-start | bytes 294916
  117.2 9.9 %copy-start.11 = (f32[384]{0:T(512)S(1)}, f32[384]{0:T(512)}, u32[]{:S(2)}) copy-start(f32[384]{0:T(512)} %param.13) | copy-start | bytes 4612
  117.3 15.8 %collective-permute-start.9 = (bf16[2,3,192,384]{3,2,1,0:T(8,128)(2,1)S(1)}, bf16[2,3,192,384]{3,2,1,0:T(8,128)(2,1)}, u32[]{:S(2)}, u32[]{:S(2)}) collective-permute-start(bf16[2,3,192,384]{3,2,1,0:T(8,128)(2,1)S(1)} %pad_maximum_fusion.1), channel_id=1, source_target_pairs={{0,1},{1,0},{2,3},{3,2},{4,5},{5,4},{6,7},{7,6},{8,9},{9,8},{10,11... | collective-permute-start | bytes 2654216 | tf_op jit(solution)/shard_map/ppermute | solution.py:21
  119.5 7.8 %collective-permute-start.7 = (bf16[4,4,1,384]{3,2,1,0:T(2,128)(2,1)S(1)}, bf16[4,4,1,384]{3,2,1,0:T(2,128)(2,1)S(1)}, u32[]{:S(2)}, u32[]{:S(2)}) collective-permute-start(bf16[4,4,1,384]{3,2,1,0:T(2,128)(2,1)S(1)} %get-tuple-element.28), channel_id=1, source_target_pairs={{1,0},{2,1},{3,2},{4,3},{5,4},{6,5},{7,6},{8,7},{9,8},{10,9},{11,1... | collective-permute-start | bytes 36872 | tf_op jit(solution)/shard_map/ppermute | solution.py:25
  124.9 7.3 %collective-permute-start.6 = (bf16[4,4,1,384]{3,2,1,0:T(2,128)(2,1)S(1)}, bf16[4,4,1,384]{3,2,1,0:T(2,128)(2,1)S(1)}, u32[]{:S(2)}, u32[]{:S(2)}) collective-permute-start(bf16[4,4,1,384]{3,2,1,0:T(2,128)(2,1)S(1)} %get-tuple-element.27), channel_id=1, source_target_pairs={{0,1},{1,2},{2,3},{3,4},{4,5},{5,6},{6,7},{7,8},{8,9},{9,10},{10,1... | collective-permute-start | bytes 36872 | tf_op jit(solution)/shard_map/ppermute | solution.py:25
  141.4 1.3 copy-start.7
  (2 other events, 1.8 us)
Sparse Core Ops, SparseCore 0:
  12.3 62.0 all-gather.1

commit v4 on v3

--- a/solution.py
+++ b/solution.py
@@ -10,7 +10,6 @@
 EPSILON = 1e-06
 TIME = ("m", "p")
 TILE = ("x", "y1", "y0", "c")
-QUAD = ("y0", "c")
 TEAM = ("p", "y0", "c")
 TAPS = 7
 PADDED = 48
@@ -105,44 +104,54 @@
     )(place, *strips, left, right, mean[:, None], scale[:, None], gain[None], bias[None])
 
 
-def conv_kernel(place_ref, act_ref, weight_ref, out_ref, total_ref, held_ref, arrived):
-    frames, rows, padded, outs = total_ref.shape
-    taps = held_ref.shape[0]
-    copies = [pltpu.make_async_copy(weight_ref.at[i], held_ref.at[i], arrived.at[i]) for i in range(taps)]
+def conv_kernel(place_ref, act_ref, weight_ref, out_ref, held_ref, stage_ref, arrived):
+    taps, outs, _ = held_ref.shape
+    frames, rows, padded = act_ref.shape[1] - 2, act_ref.shape[2] - 2, act_ref.shape[3]
+    members, span = out_ref.shape[0], frames // 2
+    cols = out_ref.shape[1] // (span * rows)
+    first, doubled = place_ref[0], place_ref[1]
+    copies = [
+        pltpu.make_async_copy(weight_ref.at[doubled + i], held_ref.at[i], arrived.at[i]) for i in range(taps)
+    ]
     for copy in copies:
         copy.start()
-    doubled = (place_ref[1] > 0).astype(jnp.float32)
-    for i in range(taps):
-        copies[i].wait()
-        tap = place_ref[0] + i
-        window = act_ref[tap % 3, pl.ds(tap // 9, frames), pl.ds(tap // 3 % 3, rows)]
-        part = lax.dot_general(
-            window.reshape(frames * rows * padded, -1), held_ref[i], NT, preferred_element_type=jnp.float32
-        ).reshape(total_ref.shape)
-        if i == 0:
-            total_ref[...] = part * (1.0 - doubled)
-        else:
-            total_ref[...] += part
-    span = out_ref.shape[1]
-    for member in range(out_ref.shape[0]):
-        plane, strip = member // 4, member % 4
-        part = total_ref[plane * span : (plane + 1) * span, :, strip * 8 : strip * 8 + 16]
-        out_ref[member] = part.astype(out_ref.dtype)
-
-
-def conv_partial(place, act, weight):
+    counted = 1.0 - doubled.astype(jnp.float32)
+    for chunk in range(0, frames, 2):
+        total = None
+        for i in range(taps):
+            if chunk == 0:
+                copies[i].wait()
+            tap = first + i
+            window = act_ref[tap % 3, pl.ds(tap // 9 + chunk, 2), pl.ds(tap // 3 % 3, rows)]
+            part = lax.dot_general(
+                window.reshape(2 * rows * padded, -1), held_ref[i], NT, preferred_element_type=jnp.float32
+            )
+            total = part * counted if i == 0 else total + part
+        total = total.reshape(2, rows, padded, outs)
+        for step in range(2):
+            plane, frame = (chunk + step) // span, (chunk + step) % span
+            for row in range(rows):
+                at = (frame * rows + row) * cols
+                for strip in range(4):
+                    stage_ref[4 * plane + strip, at : at + cols, :] = total[step, row, strip * 8 : strip * 8 + cols]
+    for member in range(members):
+        out_ref[member] = stage_ref[member].astype(out_ref.dtype)
+
+
+def conv_partial(place, act, weight, cols):
     slots, outs, chans = weight.shape
     _, frames, rows, padded, _ = act.shape
     frames, rows = frames - 2, rows - 2
+    block = (8, frames // 2 * rows * cols, outs)
     vmem = pl.BlockSpec(memory_space=pltpu.VMEM)
     return pl.pallas_call(
         conv_kernel,
-        out_shape=jax.ShapeDtypeStruct((8, frames // 2, rows, 16, outs), jnp.bfloat16),
-        in_specs=[pl.BlockSpec(memory_space=pltpu.SMEM), vmem, pl.BlockSpec(memory_space=pl.ANY)],
+        out_shape=jax.ShapeDtypeStruct(block, jnp.bfloat16),
+        in_specs=[pl.BlockSpec(memory_space=pltpu.SMEM), vmem, pl.BlockSpec(memory_space=pltpu.HBM)],
         out_specs=vmem,
         scratch_shapes=[
-            pltpu.VMEM((frames, rows, padded, outs), jnp.float32),
             pltpu.VMEM((TAPS, outs, chans), jnp.bfloat16),
+            pltpu.VMEM(block, jnp.float32),
             pltpu.SemaphoreType.DMA((TAPS,)),
         ],
         compiler_params=pltpu.CompilerParams(vmem_limit_bytes=40 * 1024 * 1024),
@@ -155,73 +164,70 @@
 
 
 def tail_kernel(
-    place_ref, parts_ref, skip_ref, bias_ref, pick_ref, upper_ref, up_bias_ref, out_ref, tap_ref, fine_ref, *, columns
+    parts_ref, skip_ref, inside_ref, bias_ref, pick_ref, upper_ref, up_bias_ref, order_ref,
+    out_ref, tap_ref, fine_ref, all_ref,
 ):
-    frames, rows, padded, outs = tap_ref.shape[1:]
-    chans = skip_ref.shape[-1]
-    flat = (frames * rows * padded, -1)
-    column = place_ref[0] + lax.broadcasted_iota(jnp.int32, (frames, rows, padded, chans), 2)
-    keep = jnp.logical_and(column >= 0, column < columns)
-    summed = skip_ref[...].astype(jnp.float32).reshape(flat[0], chans) + bias_ref[...]
+    frames, fine_rows, fine_cols, outs = out_ref.shape
+    rows, cols = fine_rows // 2, fine_cols // 2
+    wide = cols + 2
+    summed = skip_ref[...].astype(jnp.float32) + bias_ref[...]
     for parity in range(2):
         total = parts_ref[4 * parity].astype(jnp.float32)
         for quarter in range(1, 4):
             total = total + parts_ref[4 * parity + quarter].astype(jnp.float32)
-        total = total.reshape(flat)
         upper_half = total.astype(jnp.bfloat16)
         lower_half = (total - upper_half.astype(jnp.float32)).astype(jnp.bfloat16)
         for part in (lower_half, upper_half):
             summed = summed + jnp.dot(part, pick_ref[parity], preferred_element_type=jnp.float32)
-    summed = jnp.where(keep.reshape(flat[0], chans), summed, 0.0).astype(jnp.bfloat16)
+    summed = jnp.where(inside_ref[...] > 0.0, summed, 0.0).astype(jnp.bfloat16)
+    held = outs // upper_ref.shape[1]
     for tap in range(9):
-        part = lax.dot_general(summed, upper_ref[tap], NT, preferred_element_type=jnp.float32)
-        tap_ref[tap] = part.reshape(frames, rows, padded, outs)
-
-    cols = padded // 2
+        weight = upper_ref[tap * held : (tap + 1) * held].reshape(outs, -1)
+        tap_ref[tap] = lax.dot_general(summed, weight, NT, preferred_element_type=jnp.float32)
+
+    spare = jnp.zeros((cols, 256 - outs), jnp.float32)
     for frame in range(frames):
         for row in range(rows):
             for low in range(2):
                 lines = []
                 for dx in range(3):
-                    line = 0.0
+                    line = up_bias_ref[...] if dx == 1 else 0.0
                     for dy in range(3):
                         at = row + (low + dy - 1) // 2
                         if 0 <= at < rows:
-                            line = line + tap_ref[3 * dy + dx, frame, at]
+                            at = (frame * rows + at) * wide
+                            line = line + tap_ref[3 * dy + dx, at : at + wide, :]
                     lines.append(line)
                 left = lines[0][0:cols] + (lines[1] + lines[2])[1 : 1 + cols]
                 right = (lines[0] + lines[1])[1 : 1 + cols] + lines[2][2 : 2 + cols]
                 for side, value in ((0, left), (1, right)):
-                    value = value + up_bias_ref[...]
-                    spare = jnp.zeros((cols, 256 - outs), jnp.float32)
                     fine_ref[0, pl.ds(side, cols, stride=2), :] = value[:, :128]
                     fine_ref[1, pl.ds(side, cols, stride=2), :] = jnp.concatenate([value[:, 128:], spare], axis=1)
-                out_ref[frame, 2 * row + low, :, 0:128] = fine_ref[0].astype(out_ref.dtype)
-                out_ref[frame, 2 * row + low, :, 128:outs] = fine_ref[1, :, : outs - 128].astype(out_ref.dtype)
-
-
-def tail(place, parts, skip, bias, pick, upper, up_bias, columns):
-    _, frames, rows, padded, _ = parts.shape
-    outs = upper.shape[1]
-
-    def kernel(*refs):
-        tail_kernel(*refs, columns=columns)
-
+                at = (frame * fine_rows + 2 * row + low) * fine_cols
+                all_ref[at : at + fine_cols, 0:128] = fine_ref[0].astype(jnp.bfloat16)
+                all_ref[at : at + fine_cols, 128:256] = fine_ref[1].astype(jnp.bfloat16)
+    result = jnp.dot(all_ref[...], order_ref[...], preferred_element_type=jnp.float32)
+    out_ref[...] = result.astype(out_ref.dtype).reshape(out_ref.shape)
+
+
+def tail(parts, skip, inside, bias, pick, upper, up_bias, order, shape):
+    frames, fine_rows, fine_cols, outs = shape
     vmem = pl.BlockSpec(memory_space=pltpu.VMEM)
     return pl.pallas_call(
-        kernel,
-        out_shape=jax.ShapeDtypeStruct((frames, 2 * rows, padded, outs), jnp.bfloat16),
-        in_specs=[pl.BlockSpec(memory_space=pltpu.SMEM)] + [vmem] * 6,
+        tail_kernel,
+        out_shape=jax.ShapeDtypeStruct(shape, jnp.bfloat16),
+        in_specs=[vmem] * 8,
         out_specs=vmem,
         scratch_shapes=[
-            pltpu.VMEM((9, frames, rows, padded, outs), jnp.float32),
-            pltpu.VMEM((2, padded, 128), jnp.float32),
+            pltpu.VMEM((9, skip.shape[0], outs), jnp.float32),
+            pltpu.VMEM((2, fine_cols, 128), jnp.float32),
+            pltpu.VMEM((frames * fine_rows * fine_cols, 256), jnp.bfloat16),
         ],
         compiler_params=pltpu.CompilerParams(vmem_limit_bytes=40 * 1024 * 1024),
         cost_estimate=pl.CostEstimate(
-            flops=2 * frames * rows * padded * upper.size, bytes_accessed=2 * upper.size, transcendentals=0
+            flops=2 * skip.shape[0] * upper.size, bytes_accessed=2 * upper.size, transcendentals=0
         ),
-    )(place, parts, skip, bias, pick, upper, up_bias)
+    )(parts, skip, inside, bias, pick, upper, up_bias, order)
 
 
 def per_device(sizes, features, skip, norm_gain, norm_bias, conv_weight, conv_bias, up_weight, up_bias):
@@ -229,19 +235,21 @@
     pairs = sizes["m"]
     strips = sizes["x"] * sizes["y1"] * 4
     columns = strips * cols
-    core = lax.axis_index("c")
-    quarter = 2 * lax.axis_index("y0") + core
+    quarter = 2 * lax.axis_index("y0") + lax.axis_index("c")
     quad = lax.axis_index("x") * sizes["y1"] + lax.axis_index("y1")
     strip = 4 * quad + quarter
     even = lax.axis_index("p") == 0
 
     shard, up_shard = conv_weight.shape[0], up_weight.shape[0]
-    first_tap = jnp.minimum(quarter * TAPS, 27 - TAPS)
-    mine = lax.dynamic_slice_in_dim(conv_weight, first_tap, TAPS, axis=1)
-    up_mine = lax.dynamic_slice_in_dim(up_weight, core * 3, 6, axis=1).reshape(up_shard, 3, 2, chans)
-    up_mine = up_mine.transpose(2, 0, 1, 3).reshape(shard, 3, chans)
-    mine = jnp.concatenate([mine, up_mine], axis=1)
+    mine = lax.dynamic_slice_in_dim(conv_weight, jnp.minimum(quarter * TAPS, 27 - TAPS - 1), TAPS + 1, axis=1)
     gathered = lax.all_gather(mine, "m", axis=0, tiled=True).transpose(1, 0, 2)
+
+    planes = 2 * pairs
+    outs = up_shard * planes
+    share = next(r for r in range(1, up_shard + 1) if up_shard % r == 0 and 9 * up_shard // r <= strips)
+    held_rows = up_weight.transpose(1, 0, 2).reshape(9 * up_shard, chans)
+    up_mine = lax.dynamic_slice_in_dim(held_rows, jnp.minimum(strip * share, 9 * up_shard - share), share, axis=0)
+    up_mine = handed_out(up_mine, TIME, planes).reshape(planes * share, chans)
 
     other = swap(features, "p")
     eight = jnp.concatenate([jnp.where(even, features, other), jnp.where(even, other, features)], axis=0)
@@ -249,6 +257,8 @@
     ten = jnp.concatenate([back, eight], axis=0)
     by_y = swap(ten, "y0")
     everyone = handed_out(local_stats(ten), TILE, strips)
+    up_mine, everyone = lax.optimization_barrier((up_mine, everyone))
+    upper = handed_out(up_mine, TILE, strips)
 
     by_c = swap(jnp.stack([ten, by_y]), "c")
     held = (ten, by_c[0], by_y, by_c[1])
@@ -256,13 +266,14 @@
     for flip in range(1, 4):
         head = jnp.where(quarter == flip, held[flip][:, :, :2], head)
         tail_end = jnp.where(quarter == 3 - flip, held[flip][:, :, cols - 2 :], tail_end)
-    skip, head, tail_end = lax.optimization_barrier((skip, head, tail_end))
+    skip_left = strip_shift(skip[:, :, cols - 1 :], strips, 1)
+    skip_right = strip_shift(skip[:, :, :1], strips, -1)
+    skip_left, skip_right, head, tail_end = lax.optimization_barrier((skip_left, skip_right, head, tail_end))
     left = strip_shift(tail_end, strips, 4)
     right = strip_shift(head, strips, -4)
-    skip_left = strip_shift(skip[:, :, cols - 1 :], strips, 1)
-    skip_right = strip_shift(skip[:, :, :1], strips, -1)
-    skip_rest = jnp.zeros((frames, rows, cols - 2, chans), skip.dtype)
-    skip16 = jnp.concatenate([skip_left, skip, skip_right, skip_rest], axis=2)
+    skip10 = jnp.concatenate([skip_left, skip, skip_right], axis=2).reshape(-1, chans)
+    column = strip * cols - 1 + jnp.arange(skip10.shape[0]) % (cols + 2)
+    inside = jnp.logical_and(column >= 0, column < columns).astype(jnp.float32)[:, None]
 
     width = chans // GROUPS
     mean, scale = whole_stats(everyone, float(rows * cols * width))
@@ -273,26 +284,20 @@
         place, (ten, by_y, by_c[0], by_c[1]), left, right, mean, scale, norm_gain, norm_bias, columns
     )
 
-    gathered, act = lax.optimization_barrier((gathered, act))
-    up_own = gathered[TAPS:]
-    other = swap(up_own, "p")
-    up_pair = jnp.stack([jnp.where(even, up_own, other), jnp.where(even, other, up_own)])
-    parts = conv_partial(jnp.stack([first_tap, (quarter == 3).astype(jnp.int32)]), act, gathered)
-    other = swap(up_pair, "c")
-    upper = [
-        jnp.where(core == which, up_pair, other)
-        .reshape(2, 3, pairs, 2, up_shard, chans)
-        .transpose(1, 3, 2, 0, 4, 5)
-        .reshape(6, 2 * pairs * up_shard, chans)
-        for which in range(2)
-    ]
-    upper = jnp.concatenate([upper[0][:5], upper[1][2:]], axis=0)
+    gathered, act, skip10 = lax.optimization_barrier((gathered, act, skip10))
+    last = (quarter == 3).astype(jnp.int32)
+    parts = conv_partial(jnp.stack([jnp.minimum(quarter * TAPS, 27 - TAPS), last]), act, gathered, cols + 2)
 
     channel = jnp.arange(chans).reshape(pairs, 2, shard).transpose(1, 0, 2).reshape(2, chans // 2)
     pick = (channel[:, :, None] == jnp.arange(chans)[None, None, :]).astype(jnp.bfloat16)
+    gathered_as = (planes, up_shard // share, share)
+    out_channel = jnp.arange(outs).reshape(gathered_as).transpose(1, 0, 2).reshape(outs)
+    order = jnp.pad(out_channel, (0, 256 - outs), constant_values=-1)[:, None] == jnp.arange(outs)[None, :]
+    up_bias = up_bias.reshape(gathered_as).transpose(1, 0, 2).reshape(1, outs)
     parts = lax.all_to_all(parts, TEAM, 0, 0, tiled=True)
     return tail(
-        (strip * cols - 1).reshape(1), parts, skip16, conv_bias[None], pick, upper, up_bias[None], columns
+        parts, skip10, inside, conv_bias[None], pick, upper.reshape(strips, planes * share, chans),
+        up_bias, order.astype(jnp.bfloat16), (frames, 2 * rows, 2 * cols, outs),
     )
 
 

time: 153 us -> 134 us (0.88)
  the two profiles are of different devices: /device:TPU:4 before, /device:TPU:1 now
where the time goes in v4:
time: 134 us; the launch traced here: 133 us
  starting transfers between devices  57 us (43%)
  waiting for transfers between devices  26.9 us (20%)
  local copies, waits for them, and re-layouts  16.9 us (13%)
  between operations  13.8 us (10%)
  Pallas kernels  12.3 us (9%)
  other arithmetic  5.74 us (4%)
    all_to_all x3, starting transfers between devices, handed_out(): lax.all_to_all(jnp.broadcast_to(array[None], (members,) + array.shape), a...  26.2 us
    ppermute x4, starting transfers between devices, strip_shift(): lax.ppermute(array, TILE, [(i, i + by) for i in range(count) if 0 <= i +...  12.3 us
    ppermute x3, starting transfers between devices, swap(): return lax.ppermute(array, axis, [(0, 1), (1, 0)])  9.95 us
    ppermute x4, waiting for transfers between devices, strip_shift(): lax.ppermute(array, TILE, [(i, i + by) for i in range(count) if 0 <= i +...  9.87 us
    all_to_all x1, waiting for transfers between devices, per_device(): parts = lax.all_to_all(parts, TEAM, 0, 0, tiled=True)  8.52 us
    unnamed x13, local copies, waits for them, and re-layouts  7.66 us
    pallas_call x1, Pallas kernels, conv_partial(): pl.pallas_call(conv_kernel, out_shape=jax.ShapeDtypeStruct(block, jnp.bfl...  7.57 us
    all_to_all x3, waiting for transfers between devices, handed_out(): lax.all_to_all(jnp.broadcast_to(array[None], (members,) + array.shape), a...  7.32 us
  transfers between devices with their start and end apart: 13, of which 5 were waited for; matrix products, arithmetic and copies ran while one was open for 12% of the time, Pallas kernels for 8%

profile of v4, /device:TPU:1, one launch (start us, length us, event | category | flops | bytes accessed | tf_op | source)
XLA Modules:
  0.0 132.6 jit_solution(14697354752685155371)
XLA Ops:
  6.5 4.5 %collective-permute-start = (bf16[4,4,8,384]{3,2,1,0:T(8,128)(2,1)}, bf16[4,4,8,384]{3,2,1,0:T(8,128)(2,1)S(1)}, u32[]{:S(2)}, u32[]{:S(2)}) collective-permute-start(bf16[4,4,8,384]{3,2,1,0:T(8,128)(2,1)} %param.8), channel_id=1, source_target_pairs={{0,32},{32,0},{1,33},{33,1},{2,34},{34,2},{3,35},{35,3},{4,36},{36... | collective-permute-start | bytes 294920 | tf_op jit(solution)/shard_map/ppermute | solution.py:20
  12.6 14.0 %all-to-all-start = ((bf16[16,4,384]{2,1,0:T(4,128)(2,1)}), bf16[16,4,384]{2,1,0:T(4,128)(2,1)S(1)}, u32[]{:S(2)}, u32[]{:S(2)}) async-start(bf16[16,4,384]{2,1,0:T(4,128)(2,1)} %broadcast_in_dim.16), calls=%async_computation | async-start | bytes 98304 | tf_op jit(solution)/shard_map/all_to_all | solution.py:28
  27.7 4.3 %collective-permute-start.4 = (bf16[4,4,1,384]{3,2,1,0:T(2,128)(2,1)S(1)}, bf16[4,4,1,384]{3,2,1,0:T(2,128)(2,1)}, u32[]{:S(2)}, u32[]{:S(2)}) collective-permute-start(bf16[4,4,1,384]{3,2,1,0:T(2,128)(2,1)S(1)} %get-tuple-element.32), channel_id=1, source_target_pairs={{0,1},{1,2},{2,3},{3,4},{4,5},{5,6},{6,7},{7,8},{8,9},{9,10},{10,1... | collective-permute-start | bytes 36872 | tf_op jit(solution)/shard_map/ppermute | solution.py:24
  32.1 1.9 %collective-permute-start.5 = (bf16[4,4,1,384]{3,2,1,0:T(2,128)(2,1)S(1)}, bf16[4,4,1,384]{3,2,1,0:T(2,128)(2,1)}, u32[]{:S(2)}, u32[]{:S(2)}) collective-permute-start(bf16[4,4,1,384]{3,2,1,0:T(2,128)(2,1)S(1)} %get-tuple-element.31), channel_id=1, source_target_pairs={{1,0},{2,1},{3,2},{4,3},{5,4},{6,5},{7,6},{8,7},{9,8},{10,9},{11,1... | collective-permute-start | bytes 36872 | tf_op jit(solution)/shard_map/ppermute | solution.py:24
  35.7 4.4 %collective-permute-start.1 = (bf16[2,4,8,384]{3,2,1,0:T(8,128)(2,1)S(1)}, bf16[2,4,8,384]{3,2,1,0:T(8,128)(2,1)S(1)}, u32[]{:S(2)}, u32[]{:S(2)}) collective-permute-start(bf16[2,4,8,384]{3,2,1,0:T(8,128)(2,1)S(1)} %slice.62), channel_id=1, source_target_pairs={{0,64},{64,128},{128,192},{192,256},{256,320},{320,384},{384,448},... | collective-permute-start | bytes 147464 | tf_op jit(solution)/shard_map/ppermute | solution.py:256
  41.9 3.2 %collective-permute-start.2 = (bf16[10,4,8,384]{3,2,1,0:T(8,128)(2,1)S(1)}, bf16[10,4,8,384]{3,2,1,0:T(8,128)(2,1)S(1)}, u32[]{:S(2)}, u32[]{:S(2)}) collective-permute-start(bf16[10,4,8,384]{3,2,1,0:T(8,128)(2,1)S(1)} %get-tuple-element.24.refs_1_), channel_id=1, source_target_pairs={{0,2},{2,0},{1,3},{3,1},{4,6},{6,4},{5,7},{7,5},{8,10},{10,8},{9,1... | collective-permute-start | bytes 737288 | tf_op jit(solution)/shard_map/ppermute | solution.py:20
  46.5 8.2 %all-to-all-start.1 = ((f32[32,1,640]{2,1,0:T(1,128)}), f32[32,1,640]{2,1,0:T(1,128)S(1)}, u32[]{:S(2)}, u32[]{:S(2)}) async-start(f32[32,1,640]{2,1,0:T(1,128)} %reshape.166), calls=%async_computation.1 | async-start | bytes 163840 | tf_op jit(solution)/shard_map/all_to_all | solution.py:28
  54.8 7.3 %all-to-all-done.1 = f32[32,1,640]{2,1,0:T(1,128)S(1)} async-done(((f32[32,1,640]{2,1,0:T(1,128)}), f32[32,1,640]{2,1,0:T(1,128)S(1)}, u32[]{:S(2)}, u32[]{:S(2)}) %all-to-all-start.1) | async-done | bytes 81952 | tf_op jit(solution)/shard_map/all_to_all | solution.py:28
  63.6 1.4 %broadcast_in_dim.23 = bf16[32,64,384]{2,1,0:T(8,128)(2,1)} broadcast(bf16[64,384]{1,0:T(8,128)(2,1)S(1)} %reshape.134), dimensions={1,2} | broadcast | bytes 1622016 | tf_op jit(solution)/shard_map/broadcast_in_dim | solution.py:28
  65.0 4.0 %all-to-all-start.3 = ((bf16[32,64,384]{2,1,0:T(8,128)(2,1)}), bf16[32,64,384]{2,1,0:T(8,128)(2,1)S(1)}, u32[]{:S(2)}, u32[]{:S(2)}) async-start(bf16[32,64,384]{2,1,0:T(8,128)(2,1)} %broadcast_in_dim.23), calls=%async_computation.3 | async-start | bytes 3145728 | tf_op jit(solution)/shard_map/all_to_all | solution.py:28
  69.9 2.2 %collective-permute-start.3 = (bf16[2,10,4,8,384]{4,3,2,1,0:T(8,128)(2,1)}, bf16[2,10,4,8,384]{4,3,2,1,0:T(8,128)(2,1)}, u32[]{:S(2)}, u32[]{:S(2)}) collective-permute-start(bf16[2,10,4,8,384]{4,3,2,1,0:T(8,128)(2,1)} %pad_maximum_fusion), channel_id=1, source_target_pairs={{0,1},{1,0},{2,3},{3,2},{4,5},{5,4},{6,7},{7,6},{8,9},{9,8},{10,11... | collective-permute-start | bytes 1474568 | tf_op jit(solution)/shard_map/ppermute | solution.py:20
  72.9 1.1 collective-permute-done.3
  76.1 4.8 %collective-permute-start.6 = (bf16[10,4,2,384]{3,2,1,0:T(2,128)(2,1)}, bf16[10,4,2,384]{3,2,1,0:T(2,128)(2,1)S(1)}, u32[]{:S(2)}, u32[]{:S(2)}) collective-permute-start(bf16[10,4,2,384]{3,2,1,0:T(2,128)(2,1)} %get-tuple-element.14), channel_id=1, source_target_pairs={{0,4},{1,5},{2,6},{3,7},{4,8},{5,9},{6,10},{7,11},{8,12},{9,13},{1... | collective-permute-start | bytes 184328 | tf_op jit(solution)/shard_map/ppermute | solution.py:24
  80.9 1.3 collective-permute-start.7
  83.3 4.3 %collective-permute-done.6.refs_5_ = bf16[10,4,2,384]{3,2,1,0:T(2,128)(2,1)S(1)} collective-permute-done((bf16[10,4,2,384]{3,2,1,0:T(2,128)(2,1)}, bf16[10,4,2,384]{3,2,1,0:T(2,128)(2,1)S(1)}, u32[]{:S(2)}, u32[]{:S(2)}) %collective-permute-start.6) | collective-permute-done | bytes 61472 | tf_op jit(solution)/shard_map/ppermute | solution.py:24
  87.6 5.6 %collective-permute-done.7.refs_6_ = bf16[10,4,2,384]{3,2,1,0:T(2,128)(2,1)S(1)} collective-permute-done((bf16[10,4,2,384]{3,2,1,0:T(2,128)(2,1)}, bf16[10,4,2,384]{3,2,1,0:T(2,128)(2,1)S(1)}, u32[]{:S(2)}, u32[]{:S(2)}) %collective-permute-start.7) | collective-permute-done | bytes 61472 | tf_op jit(solution)/shard_map/ppermute | solution.py:24
  93.2 2.5 %shard_map.82.act_ref = bf16[3,10,6,48,384]{4,3,2,1,0:T(8,128)(2,1)S(1)} custom-call(s32[3]{0:T(128)S(1)} %pad_add_fusion.1.refs_0_, bf16[10,4,8,384]{3,2,1,0:T(8,128)(2,1)S(1)} %get-tuple-element.24.refs_1_, bf16[10,4,8,384]{3,2,1,0:T(8,128)(2,1)S(1)} %collective-permute-done.2.refs_2_, bf16[10,4,8,384]{3,2,1,0:T(8,128)(2,1)S(1)} %get-tuple-element.28.refs_3_, ...), custom_call_target="tpu_custom_call" | custom-call | flops 12288000 | bytes 7372800 | tf_op jit(solution)/shard_map/pallas_call | solution.py:94
  95.7 2.7 %copy-done.1 = bf16[3,10,6,48,384]{4,3,2,1,0:T(8,128)(2,1)} copy-done((bf16[3,10,6,48,384]{4,3,2,1,0:T(8,128)(2,1)}, bf16[3,10,6,48,384]{4,3,2,1,0:T(8,128)(2,1)S(1)}, u32[]{:S(2)}) %copy-start.1) | copy-done | bytes 6635544
  98.4 2.9 %copy-done.2 = bf16[3,10,6,48,384]{4,3,2,1,0:T(8,128)(2,1)S(1)} copy-done((bf16[3,10,6,48,384]{4,3,2,1,0:T(8,128)(2,1)S(1)}, bf16[3,10,6,48,384]{4,3,2,1,0:T(8,128)(2,1)}, u32[]{:S(2)}) %copy-start.2) | copy-done | bytes 6635544
  101.3 1.3 copy-done.3
  102.6 7.6 %shard_map.83 = bf16[8,160,192]{2,1,0:T(8,128)(2,1)} custom-call(s32[2]{0:T(128)S(1)} %pad_add_fusion.place_ref, bf16[3,10,6,48,384]{4,3,2,1,0:T(8,128)(2,1)S(1)} %copy-done.2, bf16[8,192,384]{2,1,0:T(8,128)(2,1)S(1)} %bitcast.16), custom_call_target="tpu_custom_call" | custom-call | flops 1585446912 | bytes 7667712 | tf_op jit(solution)/shard_map/pallas_call | solution.py:147
  110.1 4.0 %all-to-all-start.2 = ((bf16[8,160,192]{2,1,0:T(8,128)(2,1)}), bf16[8,160,192]{2,1,0:T(8,128)(2,1)S(1)}, u32[]{:S(2)}, u32[]{:S(2)}) async-start(bf16[8,160,192]{2,1,0:T(8,128)(2,1)} %shard_map.83), calls=%async_computation.2 | async-start | bytes 1310720 | tf_op jit(solution)/shard_map/all_to_all | solution.py:297
  115.0 8.5 %all-to-all-done.2.parts_ref = bf16[8,160,192]{2,1,0:T(8,128)(2,1)S(1)} async-done(((bf16[8,160,192]{2,1,0:T(8,128)(2,1)}), bf16[8,160,192]{2,1,0:T(8,128)(2,1)S(1)}, u32[]{:S(2)}, u32[]{:S(2)}) %all-to-all-start.2) | async-done | bytes 491552 | tf_op jit(solution)/shard_map/all_to_all | solution.py:297
  123.6 2.2 %shard_map.84 = bf16[4,8,16,192]{3,2,1,0:T(8,128)(2,1)} custom-call(bf16[8,160,192]{2,1,0:T(8,128)(2,1)S(1)} %all-to-all-done.2.parts_ref, bf16[160,384]{1,0:T(8,128)(2,1)S(1)} %reshape.136.skip_ref, f32[160,1]{1,0:T(8,128)S(1)} %fusion.14.inside_ref, f32[1,384]{1,0:T(1,128)S(1)} %broadcast_in_dim.22.bias_ref, bf16[2,192,384]{2,1,0:T(8,128)(2,1)S(1)} %fusion.pick_ref, ...), custom_call_target="tpu_custom_call" | custom-call | flops 251658240 | bytes 1572864 | tf_op jit(solution)/shard_map/pallas_call | solution.py:216
  (73 shorter events, 14.4 us)
Async XLA Ops:
  6.5 27.5 %copy-start = (bf16[24,27,384]{2,0,1:T(8,128)(2,1)S(1)}, bf16[24,27,384]{2,0,1:T(8,128)(2,1)}, u32[]{:S(2)}) copy-start(bf16[24,27,384]{2,0,1:T(8,128)(2,1)} %param.12) | copy-start | bytes 1492996
  6.5 28.2 %collective-permute-start = (bf16[4,4,8,384]{3,2,1,0:T(8,128)(2,1)}, bf16[4,4,8,384]{3,2,1,0:T(8,128)(2,1)S(1)}, u32[]{:S(2)}, u32[]{:S(2)}) collective-permute-start(bf16[4,4,8,384]{3,2,1,0:T(8,128)(2,1)} %param.8), channel_id=1, source_target_pairs={{0,32},{32,0},{1,33},{33,1},{2,34},{34,2},{3,35},{35,3},{4,36},{36... | collective-permute-start | bytes 294920 | tf_op jit(solution)/shard_map/ppermute | solution.py:20
  12.6 33.9 %all-to-all-start = ((bf16[16,4,384]{2,1,0:T(4,128)(2,1)}), bf16[16,4,384]{2,1,0:T(4,128)(2,1)S(1)}, u32[]{:S(2)}, u32[]{:S(2)}) async-start(bf16[16,4,384]{2,1,0:T(4,128)(2,1)} %broadcast_in_dim.16), calls=%async_computation | async-start | bytes 98304 | tf_op jit(solution)/shard_map/all_to_all | solution.py:28
  26.7 71.7 %all-gather.2.cloned.1.call-start = ((), (), s32[]{:S(2)}) async-start(), calls=%async_computation.4 | async-start | bytes 1327104 | tf_op jit(solution)/shard_map/all_gather | solution.py:245
  27.7 48.4 %collective-permute-start.4 = (bf16[4,4,1,384]{3,2,1,0:T(2,128)(2,1)S(1)}, bf16[4,4,1,384]{3,2,1,0:T(2,128)(2,1)}, u32[]{:S(2)}, u32[]{:S(2)}) collective-permute-start(bf16[4,4,1,384]{3,2,1,0:T(2,128)(2,1)S(1)} %get-tuple-element.32), channel_id=1, source_target_pairs={{0,1},{1,2},{2,3},{3,4},{4,5},{5,6},{6,7},{7,8},{8,9},{9,10},{10,1... | collective-permute-start | bytes 36872 | tf_op jit(solution)/shard_map/ppermute | solution.py:24
  32.1 44.1 %collective-permute-start.5 = (bf16[4,4,1,384]{3,2,1,0:T(2,128)(2,1)S(1)}, bf16[4,4,1,384]{3,2,1,0:T(2,128)(2,1)}, u32[]{:S(2)}, u32[]{:S(2)}) collective-permute-start(bf16[4,4,1,384]{3,2,1,0:T(2,128)(2,1)S(1)} %get-tuple-element.31), channel_id=1, source_target_pairs={{1,0},{2,1},{3,2},{4,3},{5,4},{6,5},{7,6},{8,7},{9,8},{10,9},{11,1... | collective-permute-start | bytes 36872 | tf_op jit(solution)/shard_map/ppermute | solution.py:24
  35.7 5.9 %collective-permute-start.1 = (bf16[2,4,8,384]{3,2,1,0:T(8,128)(2,1)S(1)}, bf16[2,4,8,384]{3,2,1,0:T(8,128)(2,1)S(1)}, u32[]{:S(2)}, u32[]{:S(2)}) collective-permute-start(bf16[2,4,8,384]{3,2,1,0:T(8,128)(2,1)S(1)} %slice.62), channel_id=1, source_target_pairs={{0,64},{64,128},{128,192},{192,256},{256,320},{320,384},{384,448},... | collective-permute-start | bytes 147464 | tf_op jit(solution)/shard_map/ppermute | solution.py:256
  41.9 27.1 %collective-permute-start.2 = (bf16[10,4,8,384]{3,2,1,0:T(8,128)(2,1)S(1)}, bf16[10,4,8,384]{3,2,1,0:T(8,128)(2,1)S(1)}, u32[]{:S(2)}, u32[]{:S(2)}) collective-permute-start(bf16[10,4,8,384]{3,2,1,0:T(8,128)(2,1)S(1)} %get-tuple-element.24.refs_1_), channel_id=1, source_target_pairs={{0,2},{2,0},{1,3},{3,1},{4,6},{6,4},{5,7},{7,5},{8,10},{10,8},{9,1... | collective-permute-start | bytes 737288 | tf_op jit(solution)/shard_map/ppermute | solution.py:20
  46.5 15.6 %all-to-all-start.1 = ((f32[32,1,640]{2,1,0:T(1,128)}), f32[32,1,640]{2,1,0:T(1,128)S(1)}, u32[]{:S(2)}, u32[]{:S(2)}) async-start(f32[32,1,640]{2,1,0:T(1,128)} %reshape.166), calls=%async_computation.1 | async-start | bytes 163840 | tf_op jit(solution)/shard_map/all_to_all | solution.py:28
  65.0 45.1 %all-to-all-start.3 = ((bf16[32,64,384]{2,1,0:T(8,128)(2,1)}), bf16[32,64,384]{2,1,0:T(8,128)(2,1)S(1)}, u32[]{:S(2)}, u32[]{:S(2)}) async-start(bf16[32,64,384]{2,1,0:T(8,128)(2,1)} %broadcast_in_dim.23), calls=%async_computation.3 | async-start | bytes 3145728 | tf_op jit(solution)/shard_map/all_to_all | solution.py:28
  69.9 4.1 %collective-permute-start.3 = (bf16[2,10,4,8,384]{4,3,2,1,0:T(8,128)(2,1)}, bf16[2,10,4,8,384]{4,3,2,1,0:T(8,128)(2,1)}, u32[]{:S(2)}, u32[]{:S(2)}) collective-permute-start(bf16[2,10,4,8,384]{4,3,2,1,0:T(8,128)(2,1)} %pad_maximum_fusion), channel_id=1, source_target_pairs={{0,1},{1,0},{2,3},{3,2},{4,5},{5,4},{6,7},{7,6},{8,9},{9,8},{10,11... | collective-permute-start | bytes 1474568 | tf_op jit(solution)/shard_map/ppermute | solution.py:20
  76.1 11.4 %collective-permute-start.6 = (bf16[10,4,2,384]{3,2,1,0:T(2,128)(2,1)}, bf16[10,4,2,384]{3,2,1,0:T(2,128)(2,1)S(1)}, u32[]{:S(2)}, u32[]{:S(2)}) collective-permute-start(bf16[10,4,2,384]{3,2,1,0:T(2,128)(2,1)} %get-tuple-element.14), channel_id=1, source_target_pairs={{0,4},{1,5},{2,6},{3,7},{4,8},{5,9},{6,10},{7,11},{8,12},{9,13},{1... | collective-permute-start | bytes 184328 | tf_op jit(solution)/shard_map/ppermute | solution.py:24
  80.9 12.2 %collective-permute-start.7 = (bf16[10,4,2,384]{3,2,1,0:T(2,128)(2,1)}, bf16[10,4,2,384]{3,2,1,0:T(2,128)(2,1)S(1)}, u32[]{:S(2)}, u32[]{:S(2)}) collective-permute-start(bf16[10,4,2,384]{3,2,1,0:T(2,128)(2,1)} %get-tuple-element.15), channel_id=1, source_target_pairs={{4,0},{5,1},{6,2},{7,3},{8,4},{9,5},{10,6},{11,7},{12,8},{13,9},{1... | collective-permute-start | bytes 184328 | tf_op jit(solution)/shard_map/ppermute | solution.py:24
  95.7 2.7 %copy-start.1 = (bf16[3,10,6,48,384]{4,3,2,1,0:T(8,128)(2,1)}, bf16[3,10,6,48,384]{4,3,2,1,0:T(8,128)(2,1)S(1)}, u32[]{:S(2)}) copy-start(bf16[3,10,6,48,384]{4,3,2,1,0:T(8,128)(2,1)S(1)} %shard_map.82.act_ref) | copy-start | bytes 19906564
  98.4 2.9 %copy-start.2 = (bf16[3,10,6,48,384]{4,3,2,1,0:T(8,128)(2,1)S(1)}, bf16[3,10,6,48,384]{4,3,2,1,0:T(8,128)(2,1)}, u32[]{:S(2)}) copy-start(bf16[3,10,6,48,384]{4,3,2,1,0:T(8,128)(2,1)} %copy-done.1) | copy-start | bytes 19906564
  101.3 1.3 copy-start.3
  102.6 11.9 %copy-start.5 = (f32[192]{0:T(256)S(1)}, f32[192]{0:T(256)}, u32[]{:S(2)}) copy-start(f32[192]{0:T(256)} %param.15) | copy-start | bytes 2308
  102.6 12.1 %copy-start.4 = (f32[384]{0:T(512)S(1)}, f32[384]{0:T(512)}, u32[]{:S(2)}) copy-start(f32[384]{0:T(512)} %param.13) | copy-start | bytes 4612
  110.1 13.4 %all-to-all-start.2 = ((bf16[8,160,192]{2,1,0:T(8,128)(2,1)}), bf16[8,160,192]{2,1,0:T(8,128)(2,1)S(1)}, u32[]{:S(2)}, u32[]{:S(2)}) async-start(bf16[8,160,192]{2,1,0:T(8,128)(2,1)} %shard_map.83), calls=%async_computation.2 | async-start | bytes 1310720 | tf_op jit(solution)/shard_map/all_to_all | solution.py:297
Sparse Core Ops, SparseCore 0:
  34.8 53.4 all-gather.1

commit v5 on v4

--- a/solution.py
+++ b/solution.py
@@ -11,6 +11,7 @@
 TIME = ("m", "p")
 TILE = ("x", "y1", "y0", "c")
 TEAM = ("p", "y0", "c")
+CHIPS = ("p", "x", "y1", "y0")
 TAPS = 7
 PADDED = 48
 NT = (((1,), (1,)), ((), ()))
@@ -51,8 +52,8 @@
 
 
 def act_kernel(
-    place_ref, own_ref, by_y_ref, by_c_ref, by_yc_ref, left_ref, right_ref, mean_ref, scale_ref, gain_ref, bias_ref,
-    out_ref, slab_ref, *, columns,
+    place_ref, own_ref, by_y_ref, by_c_ref, left_ref, right_ref, mean_ref, scale_ref, gain_ref, bias_ref,
+    out_ref, done_ref, slab_ref, *, columns,
 ):
     frames, rows, cols, chans = own_ref.shape
     padded = slab_ref.shape[0]
@@ -60,6 +61,7 @@
     column = first - 6 + lax.broadcasted_iota(jnp.int32, (padded, chans), 0)
     inside = jnp.logical_and(column >= 0, column < columns)
     slab_ref[...] = jnp.zeros_like(slab_ref)
+    done_ref[...] = jnp.zeros_like(done_ref)
     nothing = jnp.zeros((padded, chans), out_ref.dtype)
 
     def one_frame(frame, carry):
@@ -69,9 +71,9 @@
             out_ref[dx, frame, 0] = nothing
             out_ref[dx, frame, rows + 1] = nothing
         for row in range(rows):
-            for flip, ref in enumerate((own_ref, by_c_ref, by_y_ref, by_yc_ref)):
+            for flip, strip in enumerate((own_ref, by_c_ref.at[0], by_y_ref, by_c_ref.at[1])):
                 at = pl.multiple_of(8 + cols * jnp.bitwise_xor(quarter, flip), 8)
-                slab_ref[pl.ds(at, cols), :] = ref[frame, row].astype(jnp.float32)
+                slab_ref[pl.ds(at, cols), :] = strip[frame, row].astype(jnp.float32)
             slab_ref[6:8, :] = left_ref[frame, row].astype(jnp.float32)
             slab_ref[8 + 4 * cols : 10 + 4 * cols, :] = right_ref[frame, row].astype(jnp.float32)
             value = (slab_ref[...] - mean_ref[frame]) * gain + bias_ref[...]
@@ -84,8 +86,8 @@
     lax.fori_loop(0, frames, one_frame, 0)
 
 
-def activate(place, strips, left, right, mean, scale, gain, bias, columns):
-    frames, rows, cols, chans = strips[0].shape
+def activate(place, own, by_y, by_c, left, right, mean, scale, gain, bias, columns):
+    frames, rows, cols, chans = own.shape
 
     def kernel(*refs):
         act_kernel(*refs, columns=columns)
@@ -93,40 +95,47 @@
     vmem = pl.BlockSpec(memory_space=pltpu.VMEM)
     return pl.pallas_call(
         kernel,
-        out_shape=jax.ShapeDtypeStruct((3, frames, rows + 2, PADDED, chans), jnp.bfloat16),
-        in_specs=[pl.BlockSpec(memory_space=pltpu.SMEM)] + [vmem] * 10,
-        out_specs=vmem,
+        out_shape=(
+            jax.ShapeDtypeStruct((3, frames, rows + 2, PADDED, chans), jnp.bfloat16),
+            jax.ShapeDtypeStruct((8, 128), jnp.float32),
+        ),
+        in_specs=[pl.BlockSpec(memory_space=pltpu.SMEM)] + [vmem] * 9,
+        out_specs=(vmem, vmem),
         scratch_shapes=[pltpu.VMEM((PADDED, chans), jnp.float32)],
         compiler_params=pltpu.CompilerParams(vmem_limit_bytes=40 * 1024 * 1024),
         cost_estimate=pl.CostEstimate(
-            flops=100 * strips[0].size, bytes_accessed=60 * strips[0].size, transcendentals=6 * strips[0].size
-        ),
-    )(place, *strips, left, right, mean[:, None], scale[:, None], gain[None], bias[None])
-
-
-def conv_kernel(place_ref, act_ref, weight_ref, out_ref, held_ref, stage_ref, arrived):
-    taps, outs, _ = held_ref.shape
+            flops=100 * own.size, bytes_accessed=60 * own.size, transcendentals=6 * own.size
+        ),
+    )(place, own, by_y, by_c, left, right, mean[:, None], scale[:, None], gain[None], bias[None])
+
+
+def conv_kernel(place_ref, act_ref, weight_ref, out_ref, held_ref, stage_ref):
+    outs, chans = weight_ref.shape[1:]
     frames, rows, padded = act_ref.shape[1] - 2, act_ref.shape[2] - 2, act_ref.shape[3]
     members, span = out_ref.shape[0], frames // 2
     cols = out_ref.shape[1] // (span * rows)
     first, doubled = place_ref[0], place_ref[1]
-    copies = [
-        pltpu.make_async_copy(weight_ref.at[doubled + i], held_ref.at[i], arrived.at[i]) for i in range(taps)
-    ]
-    for copy in copies:
-        copy.start()
-    counted = 1.0 - doubled.astype(jnp.float32)
+    for i in range(TAPS):
+        weight = weight_ref[i]
+        if i == 0:
+            weight = weight * (1.0 - doubled.astype(jnp.float32)).astype(weight.dtype)
+        held_ref[i // 2, :, (i % 2) * chans : (i % 2 + 1) * chans] = weight
+
+    def window(chunk, i):
+        tap = first + i
+        taken = act_ref[tap % 3, pl.ds(tap // 9 + chunk, 2), pl.ds(tap // 3 % 3, rows)]
+        return taken.reshape(2 * rows * padded, chans)
+
     for chunk in range(0, frames, 2):
         total = None
-        for i in range(taps):
-            if chunk == 0:
-                copies[i].wait()
-            tap = first + i
-            window = act_ref[tap % 3, pl.ds(tap // 9 + chunk, 2), pl.ds(tap // 3 % 3, rows)]
-            part = lax.dot_general(
-                window.reshape(2 * rows * padded, -1), held_ref[i], NT, preferred_element_type=jnp.float32
-            )
-            total = part * counted if i == 0 else total + part
+        for pair in range((TAPS + 1) // 2):
+            taken, weight = window(chunk, 2 * pair), held_ref[pair]
+            if 2 * pair + 1 < TAPS:
+                taken = jnp.concatenate([taken, window(chunk, 2 * pair + 1)], axis=1)
+            else:
+                weight = weight[:, :chans]
+            part = lax.dot_general(taken, weight, NT, preferred_element_type=jnp.float32)
+            total = part if pair == 0 else total + part
         total = total.reshape(2, rows, padded, outs)
         for step in range(2):
             plane, frame = (chunk + step) // span, (chunk + step) % span
@@ -147,12 +156,11 @@
     return pl.pallas_call(
         conv_kernel,
         out_shape=jax.ShapeDtypeStruct(block, jnp.bfloat16),
-        in_specs=[pl.BlockSpec(memory_space=pltpu.SMEM), vmem, pl.BlockSpec(memory_space=pltpu.HBM)],
+        in_specs=[pl.BlockSpec(memory_space=pltpu.SMEM), vmem, vmem],
         out_specs=vmem,
         scratch_shapes=[
-            pltpu.VMEM((TAPS, outs, chans), jnp.bfloat16),
+            pltpu.VMEM(((TAPS + 1) // 2, outs, 2 * chans), jnp.bfloat16),
             pltpu.VMEM(block, jnp.float32),
-            pltpu.SemaphoreType.DMA((TAPS,)),
         ],
         compiler_params=pltpu.CompilerParams(vmem_limit_bytes=40 * 1024 * 1024),
         cost_estimate=pl.CostEstimate(
@@ -164,7 +172,7 @@
 
 
 def tail_kernel(
-    parts_ref, skip_ref, inside_ref, bias_ref, pick_ref, upper_ref, up_bias_ref, order_ref,
+    core_ref, parts_ref, skip_ref, inside_ref, bias_ref, pick_ref, upper_ref, upper_by_c_ref, up_bias_ref, order_ref,
     out_ref, tap_ref, fine_ref, all_ref,
 ):
     frames, fine_rows, fine_cols, outs = out_ref.shape
@@ -180,9 +188,15 @@
         for part in (lower_half, upper_half):
             summed = summed + jnp.dot(part, pick_ref[parity], preferred_element_type=jnp.float32)
     summed = jnp.where(inside_ref[...] > 0.0, summed, 0.0).astype(jnp.bfloat16)
-    held = outs // upper_ref.shape[1]
+    chips, held = upper_ref.shape[0] // 2, outs // (2 * upper_ref.shape[1])
     for tap in range(9):
-        weight = upper_ref[tap * held : (tap + 1) * held].reshape(outs, -1)
+        weight = []
+        for group in range(tap * held, (tap + 1) * held):
+            for parity in range(2):
+                at = parity * chips + group // 2
+                mine = core_ref[0] == group % 2
+                weight.append(jnp.where(mine, upper_ref[at], upper_by_c_ref[at]))
+        weight = jnp.concatenate(weight, axis=0)
         tap_ref[tap] = lax.dot_general(summed, weight, NT, preferred_element_type=jnp.float32)
 
     spare = jnp.zeros((cols, 256 - outs), jnp.float32)
@@ -210,13 +224,13 @@
     out_ref[...] = result.astype(out_ref.dtype).reshape(out_ref.shape)
 
 
-def tail(parts, skip, inside, bias, pick, upper, up_bias, order, shape):
+def tail(core, parts, skip, inside, bias, pick, upper, upper_by_c, up_bias, order, shape):
     frames, fine_rows, fine_cols, outs = shape
     vmem = pl.BlockSpec(memory_space=pltpu.VMEM)
     return pl.pallas_call(
         tail_kernel,
         out_shape=jax.ShapeDtypeStruct(shape, jnp.bfloat16),
-        in_specs=[vmem] * 8,
+        in_specs=[pl.BlockSpec(memory_space=pltpu.SMEM)] + [vmem] * 9,
         out_specs=vmem,
         scratch_shapes=[
             pltpu.VMEM((9, skip.shape[0], outs), jnp.float32),
@@ -227,7 +241,7 @@
         cost_estimate=pl.CostEstimate(
             flops=2 * skip.shape[0] * upper.size, bytes_accessed=2 * upper.size, transcendentals=0
         ),
-    )(parts, skip, inside, bias, pick, upper, up_bias, order)
+    )(core, parts, skip, inside, bias, pick, upper, upper_by_c, up_bias, order)
 
 
 def per_device(sizes, features, skip, norm_gain, norm_bias, conv_weight, conv_bias, up_weight, up_bias):
@@ -241,15 +255,20 @@
     even = lax.axis_index("p") == 0
 
     shard, up_shard = conv_weight.shape[0], up_weight.shape[0]
-    mine = lax.dynamic_slice_in_dim(conv_weight, jnp.minimum(quarter * TAPS, 27 - TAPS - 1), TAPS + 1, axis=1)
+    outs = up_shard * 2 * pairs
+    first_tap = jnp.minimum(quarter * TAPS, 27 - TAPS)
+    share = next(r for r in range(1, up_shard + 1) if up_shard % r == 0 and 9 * up_shard // r <= strips)
+    up_rows = up_weight.transpose(1, 0, 2).reshape(9 * up_shard, chans)
+    up_rows = lax.dynamic_slice_in_dim(up_rows, jnp.minimum(strip * share, 9 * up_shard - share), share, axis=0)
+    mine = jnp.concatenate(
+        [
+            lax.dynamic_slice_in_dim(conv_weight, first_tap, TAPS, axis=1),
+            jnp.pad(up_rows, ((0, shard - share), (0, 0)))[:, None],
+        ],
+        axis=1,
+    )
+    mine, features = lax.optimization_barrier((mine, features))
     gathered = lax.all_gather(mine, "m", axis=0, tiled=True).transpose(1, 0, 2)
-
-    planes = 2 * pairs
-    outs = up_shard * planes
-    share = next(r for r in range(1, up_shard + 1) if up_shard % r == 0 and 9 * up_shard // r <= strips)
-    held_rows = up_weight.transpose(1, 0, 2).reshape(9 * up_shard, chans)
-    up_mine = lax.dynamic_slice_in_dim(held_rows, jnp.minimum(strip * share, 9 * up_shard - share), share, axis=0)
-    up_mine = handed_out(up_mine, TIME, planes).reshape(planes * share, chans)
 
     other = swap(features, "p")
     eight = jnp.concatenate([jnp.where(even, features, other), jnp.where(even, other, features)], axis=0)
@@ -257,8 +276,6 @@
     ten = jnp.concatenate([back, eight], axis=0)
     by_y = swap(ten, "y0")
     everyone = handed_out(local_stats(ten), TILE, strips)
-    up_mine, everyone = lax.optimization_barrier((up_mine, everyone))
-    upper = handed_out(up_mine, TILE, strips)
 
     by_c = swap(jnp.stack([ten, by_y]), "c")
     held = (ten, by_c[0], by_y, by_c[1])
@@ -266,11 +283,14 @@
     for flip in range(1, 4):
         head = jnp.where(quarter == flip, held[flip][:, :, :2], head)
         tail_end = jnp.where(quarter == 3 - flip, held[flip][:, :, cols - 2 :], tail_end)
-    skip_left = strip_shift(skip[:, :, cols - 1 :], strips, 1)
-    skip_right = strip_shift(skip[:, :, :1], strips, -1)
-    skip_left, skip_right, head, tail_end = lax.optimization_barrier((skip_left, skip_right, head, tail_end))
+    ending, start, head, tail_end = lax.optimization_barrier(
+        (skip[:, :, cols - 1 :], skip[:, :, :1], head, tail_end)
+    )
     left = strip_shift(tail_end, strips, 4)
     right = strip_shift(head, strips, -4)
+    skip_left = strip_shift(ending, strips, 1)
+    skip_right = strip_shift(start, strips, -1)
+    left, right, skip_left, skip_right = lax.optimization_barrier((left, right, skip_left, skip_right))
     skip10 = jnp.concatenate([skip_left, skip, skip_right], axis=2).reshape(-1, chans)
     column = strip * cols - 1 + jnp.arange(skip10.shape[0]) % (cols + 2)
     inside = jnp.logical_and(column >= 0, column < columns).astype(jnp.float32)[:, None]
@@ -280,23 +300,25 @@
     mean = jnp.repeat(mean, width, axis=1)
     scale = jnp.repeat(scale, width, axis=1)
     place = jnp.stack([quad * 4 * cols - 2, lax.axis_index("m"), quarter])
-    act = activate(
-        place, (ten, by_y, by_c[0], by_c[1]), left, right, mean, scale, norm_gain, norm_bias, columns
-    )
-
-    gathered, act, skip10 = lax.optimization_barrier((gathered, act, skip10))
+    act, done = activate(place, ten, by_y, by_c, left, right, mean, scale, norm_gain, norm_bias, columns)
+
+    gathered, done = lax.optimization_barrier((gathered, done))
+    up_rows = gathered[TAPS].reshape(pairs, shard, chans)[:, :share].reshape(pairs * share, chans)
+    upper = handed_out(up_rows, CHIPS, strips)
     last = (quarter == 3).astype(jnp.int32)
-    parts = conv_partial(jnp.stack([jnp.minimum(quarter * TAPS, 27 - TAPS), last]), act, gathered, cols + 2)
+    parts = conv_partial(jnp.stack([first_tap, last]), act, gathered, cols + 2)
+    upper = upper.reshape(strips, pairs * share, chans)
+    upper_by_c = swap(upper, "c")
 
     channel = jnp.arange(chans).reshape(pairs, 2, shard).transpose(1, 0, 2).reshape(2, chans // 2)
     pick = (channel[:, :, None] == jnp.arange(chans)[None, None, :]).astype(jnp.bfloat16)
-    gathered_as = (planes, up_shard // share, share)
-    out_channel = jnp.arange(outs).reshape(gathered_as).transpose(1, 0, 2).reshape(outs)
+    gathered_as, turn = (pairs, 2, up_shard // share, share), (2, 1, 0, 3)
+    out_channel = jnp.arange(outs).reshape(gathered_as).transpose(turn).reshape(outs)
     order = jnp.pad(out_channel, (0, 256 - outs), constant_values=-1)[:, None] == jnp.arange(outs)[None, :]
-    up_bias = up_bias.reshape(gathered_as).transpose(1, 0, 2).reshape(1, outs)
+    up_bias = up_bias.reshape(gathered_as).transpose(turn).reshape(1, outs)
     parts = lax.all_to_all(parts, TEAM, 0, 0, tiled=True)
     return tail(
-        parts, skip10, inside, conv_bias[None], pick, upper.reshape(strips, planes * share, chans),
+        lax.axis_index("c").reshape(1), parts, skip10, inside, conv_bias[None], pick, upper, upper_by_c,
         up_bias, order.astype(jnp.bfloat16), (frames, 2 * rows, 2 * cols, outs),
     )
 

time: 134 us -> 151 us (1.13); the launches traced: 133 us -> 148 us
  waiting for transfers between devices: 26.9 us -> 53.3 us
  starting transfers between devices: 57 us -> 50.1 us
  local copies, waits for them, and re-layouts: 16.9 us -> 12.3 us
  other arithmetic: 5.74 us -> 8.83 us
  Pallas kernels: 12.3 us -> 9.53 us
    all_gather x1, waiting for transfers between devices: 0.01 us -> 33.1 us  [per_device(): gathered = lax.all_gather(mine, 'm', axis=0, tiled=True).transpose(1, 0, 2)]
    ppermute x3 -> x4, waiting for transfers between devices: 1.13 us -> 14.2 us  [swap(): return lax.ppermute(array, axis, [(0, 1), (1, 0)])]
    all_to_all x3 -> x2, starting transfers between devices: 26.2 us -> 15.5 us  [handed_out(): lax.all_to_all(jnp.broadcast_to(array[None], (members,) + array.shape), a...]
    ppermute x4, waiting for transfers between devices: 9.87 us -> 0.01 us  [strip_shift(): lax.ppermute(array, TILE, [(i, i + by) for i in range(count) if 0 <= i +...]
    all_to_all x3 -> x2, waiting for transfers between devices: 7.32 us -> 0.01 us  [handed_out(): lax.all_to_all(jnp.broadcast_to(array[None], (members,) + array.shape), a...]
    unnamed x13 -> x18, local copies, waits for them, and re-layouts: 7.66 us -> 2.49 us
    all_to_all x1, waiting for transfers between devices: 8.52 us -> 4.81 us  [per_device(): parts = lax.all_to_all(parts, TEAM, 0, 0, tiled=True)]
    pallas_call x1, Pallas kernels: 7.57 us -> 3.89 us  [conv_partial(): pl.pallas_call(conv_kernel, out_shape=jax.ShapeDtypeStruct(block, jnp.bfl...]
  transfers between devices with their start and end apart: 13 -> 13, of which waited for: 5 -> 5; matrix products, arithmetic and copies ran while one was open for 12% -> 12% of each run, Pallas kernels for 8% -> 5%
where the time goes in v5:
time: 151 us; the launch traced here: 148 us
  waiting for transfers between devices  53.3 us (35%)
  starting transfers between devices  50.1 us (33%)
  between operations  13.9 us (9%)
  local copies, waits for them, and re-layouts  12.3 us (8%)
  Pallas kernels  9.53 us (6%)
  other arithmetic  8.83 us (6%)
    all_gather x1, waiting for transfers between devices, per_device(): gathered = lax.all_gather(mine, 'm', axis=0, tiled=True).transpose(1, 0, 2)  33.1 us
    all_to_all x2, starting transfers between devices, handed_out(): lax.all_to_all(jnp.broadcast_to(array[None], (members,) + array.shape), a...  15.5 us
    ppermute x4, waiting for transfers between devices, swap(): return lax.ppermute(array, axis, [(0, 1), (1, 0)])  14.2 us
    ppermute x4, starting transfers between devices, swap(): return lax.ppermute(array, axis, [(0, 1), (1, 0)])  13 us
    ppermute x4, starting transfers between devices, strip_shift(): lax.ppermute(array, TILE, [(i, i + by) for i in range(count) if 0 <= i +...  10.7 us
    all_to_all x1, starting transfers between devices, per_device(): parts = lax.all_to_all(parts, TEAM, 0, 0, tiled=True)  5.5 us
    ppermute x1, starting transfers between devices, per_device(): lax.ppermute(eight[2 * frames - 2:], 'm', [(i, i + 1) for i in range(pair...  5.3 us
    all_to_all x1, waiting for transfers between devices, per_device(): parts = lax.all_to_all(parts, TEAM, 0, 0, tiled=True)  4.81 us
  transfers between devices with their start and end apart: 13, of which 5 were waited for; matrix products, arithmetic and copies ran while one was open for 12% of the time, Pallas kernels for 5%

profile of v5, /device:TPU:1, one launch (start us, length us, event | category | flops | bytes accessed | tf_op | source)
XLA Modules:
  0.0 147.8 jit_solution(10488400047930304543)
XLA Ops:
  8.4 4.4 %collective-permute-start = (bf16[4,4,8,384]{3,2,1,0:T(8,128)(2,1)}, bf16[4,4,8,384]{3,2,1,0:T(8,128)(2,1)S(1)}, u32[]{:S(2)}, u32[]{:S(2)}) collective-permute-start(bf16[4,4,8,384]{3,2,1,0:T(8,128)(2,1)} %param.8), channel_id=1, source_target_pairs={{0,32},{32,0},{1,33},{33,1},{2,34},{34,2},{3,35},{35,3},{4,36},{36... | collective-permute-start | bytes 294920 | tf_op jit(solution)/shard_map/ppermute | solution.py:21
  12.8 2.2 %collective-permute-done = bf16[4,4,8,384]{3,2,1,0:T(8,128)(2,1)S(1)} collective-permute-done((bf16[4,4,8,384]{3,2,1,0:T(8,128)(2,1)}, bf16[4,4,8,384]{3,2,1,0:T(8,128)(2,1)S(1)}, u32[]{:S(2)}, u32[]{:S(2)}) %collective-permute-start) | collective-permute-done | bytes 98336 | tf_op jit(solution)/shard_map/ppermute | solution.py:21
  15.9 5.3 %collective-permute-start.1 = (bf16[2,4,8,384]{3,2,1,0:T(8,128)(2,1)S(1)}, bf16[2,4,8,384]{3,2,1,0:T(8,128)(2,1)S(1)}, u32[]{:S(2)}, u32[]{:S(2)}) collective-permute-start(bf16[2,4,8,384]{3,2,1,0:T(8,128)(2,1)S(1)} %slice.68), channel_id=1, source_target_pairs={{0,64},{64,128},{128,192},{192,256},{256,320},{320,384},{384,448},... | collective-permute-start | bytes 147464 | tf_op jit(solution)/shard_map/ppermute | solution.py:275
  21.2 1.2 collective-permute-done.1
  24.1 9.3 %all-to-all-start = ((f32[32,1,640]{2,1,0:T(1,128)}), f32[32,1,640]{2,1,0:T(1,128)S(1)}, u32[]{:S(2)}, u32[]{:S(2)}) async-start(f32[32,1,640]{2,1,0:T(1,128)} %reshape.181), calls=%async_computation | async-start | bytes 163840 | tf_op jit(solution)/shard_map/all_to_all | solution.py:29
  33.4 33.1 %all-gather.2.cloned.1.call-done = bf16[192,8,384]{2,0,1:T(8,128)(2,1)} async-done(((bf16[24,8,384]{2,0,1:T(8,128)(2,1)}), bf16[192,8,384]{2,0,1:T(8,128)(2,1)}) %all-gather.2.cloned.1.call-update) | async-done | bytes 1179664 | tf_op jit(solution)/shard_map/all_gather | solution.py:271
  68.6 6.2 %all-to-all-start.2 = ((bf16[32,32,384]{2,1,0:T(8,128)(2,1)}), bf16[32,32,384]{2,1,0:T(8,128)(2,1)S(1)}, u32[]{:S(2)}, u32[]{:S(2)}) async-start(bf16[32,32,384]{2,1,0:T(8,128)(2,1)} %broadcast_in_dim.46), calls=%async_computation.2 | async-start | bytes 1572864 | tf_op jit(solution)/shard_map/all_to_all | solution.py:29
  74.8 3.1 %collective-permute-start.2 = (bf16[10,4,8,384]{3,2,1,0:T(8,128)(2,1)S(1)}, bf16[10,4,8,384]{3,2,1,0:T(8,128)(2,1)S(1)}, u32[]{:S(2)}, u32[]{:S(2)}) collective-permute-start(bf16[10,4,8,384]{3,2,1,0:T(8,128)(2,1)S(1)} %get-tuple-element.28.refs_1_), channel_id=1, source_target_pairs={{0,2},{2,0},{1,3},{3,1},{4,6},{6,4},{5,7},{7,5},{8,10},{10,8},{9,1... | collective-permute-start | bytes 737288 | tf_op jit(solution)/shard_map/ppermute | solution.py:21
  78.7 12.0 %collective-permute-done.2.refs_2_ = bf16[10,4,8,384]{3,2,1,0:T(8,128)(2,1)S(1)} collective-permute-done((bf16[10,4,8,384]{3,2,1,0:T(8,128)(2,1)S(1)}, bf16[10,4,8,384]{3,2,1,0:T(8,128)(2,1)S(1)}, u32[]{:S(2)}, u32[]{:S(2)}) %collective-permute-start.2) | collective-permute-done | bytes 245792 | tf_op jit(solution)/shard_map/ppermute | solution.py:21
  91.5 3.6 %collective-permute-start.3 = (bf16[2,10,4,8,384]{4,3,2,1,0:T(8,128)(2,1)}, bf16[2,10,4,8,384]{4,3,2,1,0:T(8,128)(2,1)S(1)}, u32[]{:S(2)}, u32[]{:S(2)}) collective-permute-start(bf16[2,10,4,8,384]{4,3,2,1,0:T(8,128)(2,1)} %pad_maximum_fusion), channel_id=1, source_target_pairs={{0,1},{1,0},{2,3},{3,2},{4,5},{5,4},{6,7},{7,6},{8,9},{9,8},{10,11... | collective-permute-start | bytes 1474568 | tf_op jit(solution)/shard_map/ppermute | solution.py:21
  95.7 1.5 reduce
  97.2 1.7 %reshape.182 = f32[32,10,64]{2,1,0:T(8,128)} reshape(f32[32,640]{1,0:T(8,128)} %reduce) | data formatting | bytes 163840
  99.8 1.2 fusion.4
  102.1 4.9 %collective-permute-start.4 = (bf16[10,4,2,384]{3,2,1,0:T(2,128)(2,1)}, bf16[10,4,2,384]{3,2,1,0:T(2,128)(2,1)}, u32[]{:S(2)}, u32[]{:S(2)}) collective-permute-start(bf16[10,4,2,384]{3,2,1,0:T(2,128)(2,1)} %get-tuple-element.17), channel_id=1, source_target_pairs={{0,4},{1,5},{2,6},{3,7},{4,8},{5,9},{6,10},{7,11},{8,12},{9,13},{1... | collective-permute-start | bytes 184328 | tf_op jit(solution)/shard_map/ppermute | solution.py:25
  107.0 1.3 collective-permute-start.5
  108.3 2.6 %collective-permute-start.6 = (bf16[4,4,1,384]{3,2,1,0:T(2,128)(2,1)}, bf16[4,4,1,384]{3,2,1,0:T(2,128)(2,1)S(1)}, u32[]{:S(2)}, u32[]{:S(2)}) collective-permute-start(bf16[4,4,1,384]{3,2,1,0:T(2,128)(2,1)} %get-tuple-element.19), channel_id=1, source_target_pairs={{0,1},{1,2},{2,3},{3,4},{4,5},{5,6},{6,7},{7,8},{8,9},{9,10},{10,1... | collective-permute-start | bytes 36872 | tf_op jit(solution)/shard_map/ppermute | solution.py:25
  110.9 1.9 %collective-permute-start.7 = (bf16[4,4,1,384]{3,2,1,0:T(2,128)(2,1)}, bf16[4,4,1,384]{3,2,1,0:T(2,128)(2,1)S(1)}, u32[]{:S(2)}, u32[]{:S(2)}) collective-permute-start(bf16[4,4,1,384]{3,2,1,0:T(2,128)(2,1)} %get-tuple-element.20), channel_id=1, source_target_pairs={{1,0},{2,1},{3,2},{4,3},{5,4},{6,5},{7,6},{8,7},{9,8},{10,9},{11,1... | collective-permute-start | bytes 36872 | tf_op jit(solution)/shard_map/ppermute | solution.py:25
  113.6 1.1 broadcast_in_dim_reshape.11.refs_7_
  116.6 3.4 %shard_map.82 = (bf16[3,10,6,48,384]{4,3,2,1,0:T(8,128)(2,1)S(1)}, f32[8,128]{1,0:T(8,128)}) custom-call(s32[3]{0:T(128)S(1)} %pad_add_fusion.1.refs_0_, bf16[10,4,8,384]{3,2,1,0:T(8,128)(2,1)S(1)} %get-tuple-element.28.refs_1_, bf16[10,4,8,384]{3,2,1,0:T(8,128)(2,1)S(1)} %collective-permute-done.2.refs_2_, ...), custom_call_target="tpu_custom_call" | custom-call | flops 12288000 | bytes 7372800 | tf_op jit(solution)/shard_map/pallas_call | solution.py:96
  120.0 3.9 %shard_map.83 = bf16[8,160,192]{2,1,0:T(8,128)(2,1)} custom-call(s32[2]{0:T(128)S(1)} %pad_add_fusion.place_ref, bf16[3,10,6,48,384]{4,3,2,1,0:T(8,128)(2,1)S(1)} %get-tuple-element.23.act_ref, bf16[8,192,384]{2,1,0:T(8,128)(2,1)S(1)} %bitcast.24), custom_call_target="tpu_custom_call" | custom-call | flops 1585446912 | bytes 7667712 | tf_op jit(solution)/shard_map/pallas_call | solution.py:156
  123.9 5.5 %all-to-all-start.1 = ((bf16[8,160,192]{2,1,0:T(8,128)(2,1)}), bf16[8,160,192]{2,1,0:T(8,128)(2,1)S(1)}, u32[]{:S(2)}, u32[]{:S(2)}) async-start(bf16[8,160,192]{2,1,0:T(8,128)(2,1)} %shard_map.83), calls=%async_computation.1 | async-start | bytes 1310720 | tf_op jit(solution)/shard_map/all_to_all | solution.py:319
  130.0 1.9 %collective-permute-start.8 = (bf16[32,32,384]{2,1,0:T(8,128)(2,1)S(1)}, bf16[32,32,384]{2,1,0:T(8,128)(2,1)S(1)}, u32[]{:S(2)}, u32[]{:S(2)}) collective-permute-start(bf16[32,32,384]{2,1,0:T(8,128)(2,1)S(1)} %all-to-all-done.2.upper_ref), channel_id=1, source_target_pairs={{0,1},{1,0},{2,3},{3,2},{4,5},{5,4},{6,7},{7,6},{8,9},{9,8},{10,11... | collective-permute-start | bytes 2359304 | tf_op jit(solution)/shard_map/ppermute | solution.py:21
  133.9 4.8 %all-to-all-done.1.parts_ref = bf16[8,160,192]{2,1,0:T(8,128)(2,1)S(1)} async-done(((bf16[8,160,192]{2,1,0:T(8,128)(2,1)}), bf16[8,160,192]{2,1,0:T(8,128)(2,1)S(1)}, u32[]{:S(2)}, u32[]{:S(2)}) %all-to-all-start.1) | async-done | bytes 491552 | tf_op jit(solution)/shard_map/all_to_all | solution.py:319
  138.7 2.3 %shard_map.84 = bf16[4,8,16,192]{3,2,1,0:T(8,128)(2,1)} custom-call(s32[1]{0:T(128)} %bitcast.core_ref, bf16[8,160,192]{2,1,0:T(8,128)(2,1)S(1)} %all-to-all-done.1.parts_ref, bf16[160,384]{1,0:T(8,128)(2,1)S(1)} %reshape.145.skip_ref, f32[160,1]{1,0:T(8,128)S(1)} %fusion.14.inside_ref, f32[1,384]{1,0:T(1,128)S(1)} %broadcast_in_dim.44.bias_ref, ...), custom_call_target="tpu_custom_call" | custom-call | flops 125829120 | bytes 786432 | tf_op jit(solution)/shard_map/pallas_call | solution.py:230
  (80 shorter events, 15.8 us)
Async XLA Ops:
  6.5 1.1 copy-start
  6.5 71.5 %copy-start.2 = (bf16[4,4,8,384]{3,2,1,0:T(8,128)(2,1)S(1)}, bf16[4,4,8,384]{3,2,1,0:T(8,128)(2,1)}, u32[]{:S(2)}) copy-start(bf16[4,4,8,384]{3,2,1,0:T(8,128)(2,1)} %param.9) | copy-start | bytes 294916
  6.5 88.6 %copy-start.4 = (f32[384]{0:T(512)S(1)}, f32[384]{0:T(512)}, u32[]{:S(2)}) copy-start(f32[384]{0:T(512)} %param.10) | copy-start | bytes 4612
  6.5 88.6 %copy-start.5 = (f32[384]{0:T(512)S(1)}, f32[384]{0:T(512)}, u32[]{:S(2)}) copy-start(f32[384]{0:T(512)} %param.11) | copy-start | bytes 4612
  6.5 60.0 %all-gather.2.cloned.1.call-start = ((), (), s32[]{:S(2)}) async-start(), calls=%async_computation.3 | async-start | bytes 1327104 | tf_op jit(solution)/shard_map/all_gather | solution.py:271
  8.4 6.6 %collective-permute-start = (bf16[4,4,8,384]{3,2,1,0:T(8,128)(2,1)}, bf16[4,4,8,384]{3,2,1,0:T(8,128)(2,1)S(1)}, u32[]{:S(2)}, u32[]{:S(2)}) collective-permute-start(bf16[4,4,8,384]{3,2,1,0:T(8,128)(2,1)} %param.8), channel_id=1, source_target_pairs={{0,32},{32,0},{1,33},{33,1},{2,34},{34,2},{3,35},{35,3},{4,36},{36... | collective-permute-start | bytes 294920 | tf_op jit(solution)/shard_map/ppermute | solution.py:21
  15.9 6.5 %collective-permute-start.1 = (bf16[2,4,8,384]{3,2,1,0:T(8,128)(2,1)S(1)}, bf16[2,4,8,384]{3,2,1,0:T(8,128)(2,1)S(1)}, u32[]{:S(2)}, u32[]{:S(2)}) collective-permute-start(bf16[2,4,8,384]{3,2,1,0:T(8,128)(2,1)S(1)} %slice.68), channel_id=1, source_target_pairs={{0,64},{64,128},{128,192},{192,256},{256,320},{320,384},{384,448},... | collective-permute-start | bytes 147464 | tf_op jit(solution)/shard_map/ppermute | solution.py:275
  24.1 43.5 %all-to-all-start = ((f32[32,1,640]{2,1,0:T(1,128)}), f32[32,1,640]{2,1,0:T(1,128)S(1)}, u32[]{:S(2)}, u32[]{:S(2)}) async-start(f32[32,1,640]{2,1,0:T(1,128)} %reshape.181), calls=%async_computation | async-start | bytes 163840 | tf_op jit(solution)/shard_map/all_to_all | solution.py:29
  66.5 53.4 %copy-start.1 = (bf16[192,8,384]{2,0,1:T(8,128)(2,1)S(1)}, bf16[192,8,384]{2,0,1:T(8,128)(2,1)}, u32[]{:S(2)}) copy-start(bf16[192,8,384]{2,0,1:T(8,128)(2,1)} %all-gather.2.cloned.1.call-done) | copy-start | bytes 3538948
  68.6 55.3 %all-to-all-start.2 = ((bf16[32,32,384]{2,1,0:T(8,128)(2,1)}), bf16[32,32,384]{2,1,0:T(8,128)(2,1)S(1)}, u32[]{:S(2)}, u32[]{:S(2)}) async-start(bf16[32,32,384]{2,1,0:T(8,128)(2,1)} %broadcast_in_dim.46), calls=%async_computation.2 | async-start | bytes 1572864 | tf_op jit(solution)/shard_map/all_to_all | solution.py:29
  74.8 15.8 %collective-permute-start.2 = (bf16[10,4,8,384]{3,2,1,0:T(8,128)(2,1)S(1)}, bf16[10,4,8,384]{3,2,1,0:T(8,128)(2,1)S(1)}, u32[]{:S(2)}, u32[]{:S(2)}) collective-permute-start(bf16[10,4,8,384]{3,2,1,0:T(8,128)(2,1)S(1)} %get-tuple-element.28.refs_1_), channel_id=1, source_target_pairs={{0,2},{2,0},{1,3},{3,1},{4,6},{6,4},{5,7},{7,5},{8,10},{10,8},{9,1... | collective-permute-start | bytes 737288 | tf_op jit(solution)/shard_map/ppermute | solution.py:21
  91.5 9.6 %collective-permute-start.3 = (bf16[2,10,4,8,384]{4,3,2,1,0:T(8,128)(2,1)}, bf16[2,10,4,8,384]{4,3,2,1,0:T(8,128)(2,1)S(1)}, u32[]{:S(2)}, u32[]{:S(2)}) collective-permute-start(bf16[2,10,4,8,384]{4,3,2,1,0:T(8,128)(2,1)} %pad_maximum_fusion), channel_id=1, source_target_pairs={{0,1},{1,0},{2,3},{3,2},{4,5},{5,4},{6,7},{7,6},{8,9},{9,8},{10,11... | collective-permute-start | bytes 1474568 | tf_op jit(solution)/shard_map/ppermute | solution.py:21
  101.0 28.6 %copy-start.7 = (f32[192]{0:T(256)S(1)}, f32[192]{0:T(256)}, u32[]{:S(2)}) copy-start(f32[192]{0:T(256)} %param.15) | copy-start | bytes 2308
  101.0 28.9 %copy-start.6 = (f32[384]{0:T(512)S(1)}, f32[384]{0:T(512)}, u32[]{:S(2)}) copy-start(f32[384]{0:T(512)} %param.13) | copy-start | bytes 4612
  102.1 14.5 %collective-permute-start.4 = (bf16[10,4,2,384]{3,2,1,0:T(2,128)(2,1)}, bf16[10,4,2,384]{3,2,1,0:T(2,128)(2,1)}, u32[]{:S(2)}, u32[]{:S(2)}) collective-permute-start(bf16[10,4,2,384]{3,2,1,0:T(2,128)(2,1)} %get-tuple-element.17), channel_id=1, source_target_pairs={{0,4},{1,5},{2,6},{3,7},{4,8},{5,9},{6,10},{7,11},{8,12},{9,13},{1... | collective-permute-start | bytes 184328 | tf_op jit(solution)/shard_map/ppermute | solution.py:25
  107.0 9.6 %collective-permute-start.5 = (bf16[10,4,2,384]{3,2,1,0:T(2,128)(2,1)}, bf16[10,4,2,384]{3,2,1,0:T(2,128)(2,1)}, u32[]{:S(2)}, u32[]{:S(2)}) collective-permute-start(bf16[10,4,2,384]{3,2,1,0:T(2,128)(2,1)} %get-tuple-element.18), channel_id=1, source_target_pairs={{4,0},{5,1},{6,2},{7,3},{8,4},{9,5},{10,6},{11,7},{12,8},{13,9},{1... | collective-permute-start | bytes 184328 | tf_op jit(solution)/shard_map/ppermute | solution.py:25
  108.3 8.3 %collective-permute-start.6 = (bf16[4,4,1,384]{3,2,1,0:T(2,128)(2,1)}, bf16[4,4,1,384]{3,2,1,0:T(2,128)(2,1)S(1)}, u32[]{:S(2)}, u32[]{:S(2)}) collective-permute-start(bf16[4,4,1,384]{3,2,1,0:T(2,128)(2,1)} %get-tuple-element.19), channel_id=1, source_target_pairs={{0,1},{1,2},{2,3},{3,4},{4,5},{5,6},{6,7},{7,8},{8,9},{9,10},{10,1... | collective-permute-start | bytes 36872 | tf_op jit(solution)/shard_map/ppermute | solution.py:25
  110.9 5.7 %collective-permute-start.7 = (bf16[4,4,1,384]{3,2,1,0:T(2,128)(2,1)}, bf16[4,4,1,384]{3,2,1,0:T(2,128)(2,1)S(1)}, u32[]{:S(2)}, u32[]{:S(2)}) collective-permute-start(bf16[4,4,1,384]{3,2,1,0:T(2,128)(2,1)} %get-tuple-element.20), channel_id=1, source_target_pairs={{1,0},{2,1},{3,2},{4,3},{5,4},{6,5},{7,6},{8,7},{9,8},{10,9},{11,1... | collective-permute-start | bytes 36872 | tf_op jit(solution)/shard_map/ppermute | solution.py:25
  120.0 12.2 %copy-start.3 = (bf16[4,4,8,384]{3,2,1,0:T(8,128)(2,1)S(1)}, bf16[4,4,8,384]{3,2,1,0:T(8,128)(2,1)}, u32[]{:S(2)}) copy-start(bf16[4,4,8,384]{3,2,1,0:T(8,128)(2,1)} %param.9) | copy-start | bytes 294916
  123.9 14.9 %all-to-all-start.1 = ((bf16[8,160,192]{2,1,0:T(8,128)(2,1)}), bf16[8,160,192]{2,1,0:T(8,128)(2,1)S(1)}, u32[]{:S(2)}, u32[]{:S(2)}) async-start(bf16[8,160,192]{2,1,0:T(8,128)(2,1)} %shard_map.83), calls=%async_computation.1 | async-start | bytes 1310720 | tf_op jit(solution)/shard_map/all_to_all | solution.py:319
  130.0 8.8 %collective-permute-start.8 = (bf16[32,32,384]{2,1,0:T(8,128)(2,1)S(1)}, bf16[32,32,384]{2,1,0:T(8,128)(2,1)S(1)}, u32[]{:S(2)}, u32[]{:S(2)}) collective-permute-start(bf16[32,32,384]{2,1,0:T(8,128)(2,1)S(1)} %all-to-all-done.2.upper_ref), channel_id=1, source_target_pairs={{0,1},{1,0},{2,3},{3,2},{4,5},{5,4},{6,7},{7,6},{8,9},{9,8},{10,11... | collective-permute-start | bytes 2359304 | tf_op jit(solution)/shard_map/ppermute | solution.py:21
Sparse Core Ops, SparseCore 0:
  9.5 57.0 all-gather.1

commit v6 on v5

--- a/solution.py
+++ b/solution.py
@@ -40,33 +40,46 @@
     mean = jnp.mean(chan_mean, axis=2)
     apart = chan_mean - mean[:, :, None]
     m2 = jnp.sum(chan_m2.reshape(frames, GROUPS, width) + rows * cols * apart * apart, axis=2)
-    return jnp.concatenate([mean, m2], axis=1)
-
-
-def whole_stats(everyone, members):
-    means, m2s = everyone[:, :, :GROUPS], everyone[:, :, GROUPS:]
-    mean = jnp.mean(means, axis=0)
-    apart = means - mean
-    m2 = jnp.sum(m2s + members * apart * apart, axis=0)
-    return mean, lax.rsqrt(m2 / (members * everyone.shape[0]) + EPSILON)
+    return jnp.pad(jnp.concatenate([mean, m2], axis=1), ((0, -frames % 8), (0, 128 - 2 * GROUPS)))
+
+
+def chan_stats(everyone, chans, members):
+    strips = everyone.shape[0]
+    sums = jnp.sum(everyone, axis=0)
+    mean = sums / strips
+    apart = everyone - mean[None]
+    between = jnp.sum(apart * apart, axis=0)
+    lane = lax.broadcasted_iota(jnp.int32, (128, chans), 0)
+    chan = lax.broadcasted_iota(jnp.int32, (128, chans), 1)
+    width = chans // GROUPS
+
+    def widened(values, first):
+        low = (lane - first) * width
+        pick = jnp.logical_and(chan >= low, chan < low + width).astype(jnp.float32)
+        return jnp.dot(values, pick, precision=lax.Precision.HIGHEST, preferred_element_type=jnp.float32)
+
+    spread = (widened(sums, GROUPS) + members * widened(between, 0)) / (members * strips)
+    return widened(mean, 0), lax.rsqrt(spread + EPSILON)
 
 
 def act_kernel(
-    place_ref, own_ref, by_y_ref, by_c_ref, left_ref, right_ref, mean_ref, scale_ref, gain_ref, bias_ref,
-    out_ref, done_ref, slab_ref, *, columns,
+    place_ref, own_ref, by_y_ref, by_c_ref, left_ref, right_ref, stats_ref, gain_ref, bias_ref,
+    out_ref, done_ref, slab_ref, mean_ref, scale_ref, *, columns,
 ):
     frames, rows, cols, chans = own_ref.shape
     padded = slab_ref.shape[0]
     first, pair, quarter = place_ref[0], place_ref[1], place_ref[2]
     column = first - 6 + lax.broadcasted_iota(jnp.int32, (padded, chans), 0)
     inside = jnp.logical_and(column >= 0, column < columns)
+    mean_ref[...], scale_ref[...] = chan_stats(stats_ref[...], chans, float(rows * cols * (chans // GROUPS)))
+    scale_ref[...] *= gain_ref[...]
     slab_ref[...] = jnp.zeros_like(slab_ref)
     done_ref[...] = jnp.zeros_like(done_ref)
     nothing = jnp.zeros((padded, chans), out_ref.dtype)
 
     def one_frame(frame, carry):
         keep = jnp.logical_and(inside, jnp.logical_or(pair > 0, frame >= 2))
-        gain = scale_ref[frame] * gain_ref[...]
+        mean, gain = mean_ref[pl.ds(frame, 1), :], scale_ref[pl.ds(frame, 1), :]
         for dx in range(3):
             out_ref[dx, frame, 0] = nothing
             out_ref[dx, frame, rows + 1] = nothing
@@ -76,7 +89,7 @@
                 slab_ref[pl.ds(at, cols), :] = strip[frame, row].astype(jnp.float32)
             slab_ref[6:8, :] = left_ref[frame, row].astype(jnp.float32)
             slab_ref[8 + 4 * cols : 10 + 4 * cols, :] = right_ref[frame, row].astype(jnp.float32)
-            value = (slab_ref[...] - mean_ref[frame]) * gain + bias_ref[...]
+            value = (slab_ref[...] - mean) * gain + bias_ref[...]
             value = 0.5 * value
             value = jnp.where(keep, value + value * jnp.tanh(value), 0.0)
             for dx in range(3):
@@ -86,7 +99,7 @@
     lax.fori_loop(0, frames, one_frame, 0)
 
 
-def activate(place, own, by_y, by_c, left, right, mean, scale, gain, bias, columns):
+def activate(place, own, by_y, by_c, left, right, stats, gain, bias, columns):
     frames, rows, cols, chans = own.shape
 
     def kernel(*refs):
@@ -99,14 +112,18 @@
             jax.ShapeDtypeStruct((3, frames, rows + 2, PADDED, chans), jnp.bfloat16),
             jax.ShapeDtypeStruct((8, 128), jnp.float32),
         ),
-        in_specs=[pl.BlockSpec(memory_space=pltpu.SMEM)] + [vmem] * 9,
+        in_specs=[pl.BlockSpec(memory_space=pltpu.SMEM)] + [vmem] * 8,
         out_specs=(vmem, vmem),
-        scratch_shapes=[pltpu.VMEM((PADDED, chans), jnp.float32)],
+        scratch_shapes=[
+            pltpu.VMEM((PADDED, chans), jnp.float32),
+            pltpu.VMEM((stats.shape[1], chans), jnp.float32),
+            pltpu.VMEM((stats.shape[1], chans), jnp.float32),
+        ],
         compiler_params=pltpu.CompilerParams(vmem_limit_bytes=40 * 1024 * 1024),
         cost_estimate=pl.CostEstimate(
             flops=100 * own.size, bytes_accessed=60 * own.size, transcendentals=6 * own.size
         ),
-    )(place, own, by_y, by_c, left, right, mean[:, None], scale[:, None], gain[None], bias[None])
+    )(place, own, by_y, by_c, left, right, stats, gain[None], bias[None])
 
 
 def conv_kernel(place_ref, act_ref, weight_ref, out_ref, held_ref, stage_ref):
@@ -295,15 +312,11 @@
     column = strip * cols - 1 + jnp.arange(skip10.shape[0]) % (cols + 2)
     inside = jnp.logical_and(column >= 0, column < columns).astype(jnp.float32)[:, None]
 
-    width = chans // GROUPS
-    mean, scale = whole_stats(everyone, float(rows * cols * width))
-    mean = jnp.repeat(mean, width, axis=1)
-    scale = jnp.repeat(scale, width, axis=1)
     place = jnp.stack([quad * 4 * cols - 2, lax.axis_index("m"), quarter])
-    act, done = activate(place, ten, by_y, by_c, left, right, mean, scale, norm_gain, norm_bias, columns)
-
-    gathered, done = lax.optimization_barrier((gathered, done))
+    act, done = activate(place, ten, by_y, by_c, left, right, everyone, norm_gain, norm_bias, columns)
+
     up_rows = gathered[TAPS].reshape(pairs, shard, chans)[:, :share].reshape(pairs * share, chans)
+    up_rows = (up_rows.astype(jnp.float32) + done[0, 0]).astype(jnp.bfloat16)
     upper = handed_out(up_rows, CHIPS, strips)
     last = (quarter == 3).astype(jnp.int32)
     parts = conv_partial(jnp.stack([first_tap, last]), act, gathered, cols + 2)

time: 151 us -> 117 us (0.77); the launches traced: 148 us -> 116 us
  waiting for transfers between devices: 53.3 us -> 22.3 us
  other arithmetic: 8.83 us -> 4.44 us
  starting transfers between devices: 50.1 us -> 52.5 us
  local copies, waits for them, and re-layouts: 12.3 us -> 14.1 us
    all_gather x1, waiting for transfers between devices: 33.1 us -> 4.74 us  [per_device(): gathered = lax.all_gather(mine, 'm', axis=0, tiled=True).transpose(1, 0, 2)]
    ppermute x4, waiting for transfers between devices: 14.2 us -> 4.86 us  [swap(): return lax.ppermute(array, axis, [(0, 1), (1, 0)])]
    unnamed x18, local copies, waits for them, and re-layouts: 2.49 us -> 6.95 us
    all_to_all x2, waiting for transfers between devices: 0.01 us -> 3.7 us  [handed_out(): lax.all_to_all(jnp.broadcast_to(array[None], (members,) + array.shape), a...]
    ppermute x4, starting transfers between devices: 13 us -> 16.2 us  [swap(): return lax.ppermute(array, axis, [(0, 1), (1, 0)])]
    ppermute x4, waiting for transfers between devices: 0.01 us -> 3.11 us  [strip_shift(): lax.ppermute(array, TILE, [(i, i + by) for i in range(count) if 0 <= i +...]
    reduce_sum x2 -> x0, other arithmetic: 2.16 us -> none  [the longest x1 1.17 us: whole_stats(): m2 = jnp.sum(m2s + members * apart * apart, axis=0)]
    another operation x2 -> x0, local copies, waits for them, and re-layouts: 2.13 us -> none  [the longest x1 1.07 us: activate(): scale[:, None]]
  transfers between devices with their start and end apart: 13 -> 13, of which waited for: 5 -> 7; matrix products, arithmetic and copies ran while one was open for 12% -> 6% of each run, Pallas kernels for 5% -> 6%
where the time goes in v6:
time: 117 us; the launch traced here: 116 us
  starting transfers between devices  52.5 us (45%)
  waiting for transfers between devices  22.3 us (19%)
  local copies, waits for them, and re-layouts  14.1 us (12%)
  between operations  13.8 us (12%)
  Pallas kernels  9.29 us (8%)
  other arithmetic  4.44 us (4%)
    ppermute x4, starting transfers between devices, swap(): return lax.ppermute(array, axis, [(0, 1), (1, 0)])  16.2 us
    all_to_all x2, starting transfers between devices, handed_out(): lax.all_to_all(jnp.broadcast_to(array[None], (members,) + array.shape), a...  13.7 us
    ppermute x4, starting transfers between devices, strip_shift(): lax.ppermute(array, TILE, [(i, i + by) for i in range(count) if 0 <= i +...  10.7 us
    unnamed x18, local copies, waits for them, and re-layouts  6.95 us
    all_to_all x1, starting transfers between devices, per_device(): parts = lax.all_to_all(parts, TEAM, 0, 0, tiled=True)  6.51 us
    ppermute x1, starting transfers between devices, per_device(): lax.ppermute(eight[2 * frames - 2:], 'm', [(i, i + 1) for i in range(pair...  5.3 us
    ppermute x4, waiting for transfers between devices, swap(): return lax.ppermute(array, axis, [(0, 1), (1, 0)])  4.86 us
    all_gather x1, waiting for transfers between devices, per_device(): gathered = lax.all_gather(mine, 'm', axis=0, tiled=True).transpose(1, 0, 2)  4.74 us
  transfers between devices with their start and end apart: 13, of which 7 were waited for; matrix products, arithmetic and copies ran while one was open for 6% of the time, Pallas kernels for 6%

profile of v6, /device:TPU:1, one launch (start us, length us, event | category | flops | bytes accessed | tf_op | source)
XLA Modules:
  0.0 116.5 jit_solution(17787029494617587682)
XLA Ops:
  8.3 4.4 %collective-permute-start = (bf16[4,4,8,384]{3,2,1,0:T(8,128)(2,1)}, bf16[4,4,8,384]{3,2,1,0:T(8,128)(2,1)S(1)}, u32[]{:S(2)}, u32[]{:S(2)}) collective-permute-start(bf16[4,4,8,384]{3,2,1,0:T(8,128)(2,1)} %param.8), channel_id=1, source_target_pairs={{0,32},{32,0},{1,33},{33,1},{2,34},{34,2},{3,35},{35,3},{4,36},{36... | collective-permute-start | bytes 294920 | tf_op jit(solution)/shard_map/ppermute | solution.py:21
  12.7 2.2 %collective-permute-done = bf16[4,4,8,384]{3,2,1,0:T(8,128)(2,1)S(1)} collective-permute-done((bf16[4,4,8,384]{3,2,1,0:T(8,128)(2,1)}, bf16[4,4,8,384]{3,2,1,0:T(8,128)(2,1)S(1)}, u32[]{:S(2)}, u32[]{:S(2)}) %collective-permute-start) | collective-permute-done | bytes 98336 | tf_op jit(solution)/shard_map/ppermute | solution.py:21
  15.8 5.3 %collective-permute-start.1 = (bf16[2,4,8,384]{3,2,1,0:T(8,128)(2,1)S(1)}, bf16[2,4,8,384]{3,2,1,0:T(8,128)(2,1)S(1)}, u32[]{:S(2)}, u32[]{:S(2)}) collective-permute-start(bf16[2,4,8,384]{3,2,1,0:T(8,128)(2,1)S(1)} %slice.64), channel_id=1, source_target_pairs={{0,64},{64,128},{128,192},{192,256},{256,320},{320,384},{384,448},... | collective-permute-start | bytes 147464 | tf_op jit(solution)/shard_map/ppermute | solution.py:292
  22.4 3.2 %collective-permute-start.2 = (bf16[10,4,8,384]{3,2,1,0:T(8,128)(2,1)S(1)}, bf16[10,4,8,384]{3,2,1,0:T(8,128)(2,1)S(1)}, u32[]{:S(2)}, u32[]{:S(2)}) collective-permute-start(bf16[10,4,8,384]{3,2,1,0:T(8,128)(2,1)S(1)} %get-tuple-element.30.refs_1_), channel_id=1, source_target_pairs={{0,2},{2,0},{1,3},{3,1},{4,6},{6,4},{5,7},{7,5},{8,10},{10,8},{9,1... | collective-permute-start | bytes 737288 | tf_op jit(solution)/shard_map/ppermute | solution.py:21
  26.6 2.7 %collective-permute-done.2.refs_2_ = bf16[10,4,8,384]{3,2,1,0:T(8,128)(2,1)S(1)} collective-permute-done((bf16[10,4,8,384]{3,2,1,0:T(8,128)(2,1)S(1)}, bf16[10,4,8,384]{3,2,1,0:T(8,128)(2,1)S(1)}, u32[]{:S(2)}, u32[]{:S(2)}) %collective-permute-start.2) | collective-permute-done | bytes 245792 | tf_op jit(solution)/shard_map/ppermute | solution.py:21
  29.4 6.6 %collective-permute-start.3 = (bf16[2,10,4,8,384]{4,3,2,1,0:T(8,128)(2,1)S(1)}, bf16[2,10,4,8,384]{4,3,2,1,0:T(8,128)(2,1)S(1)}, u32[]{:S(2)}, u32[]{:S(2)}) collective-permute-start(bf16[2,10,4,8,384]{4,3,2,1,0:T(8,128)(2,1)S(1)} %pad_maximum_fusion), channel_id=1, source_target_pairs={{0,1},{1,0},{2,3},{3,2},{4,5},{5,4},{6,7},{7,6},{8,9},{9,8},{10,11... | collective-permute-start | bytes 1474568 | tf_op jit(solution)/shard_map/ppermute | solution.py:21
  37.6 5.8 %all-to-all-start = ((f32[32,16,128]{2,1,0:T(8,128)}), f32[32,16,128]{2,1,0:T(8,128)S(1)}, u32[]{:S(2)}, u32[]{:S(2)}) async-start(f32[32,16,128]{2,1,0:T(8,128)} %broadcast_in_dim.13), calls=%async_computation | async-start | bytes 524288 | tf_op jit(solution)/shard_map/all_to_all | solution.py:29
  43.9 4.8 %collective-permute-start.4 = (bf16[10,4,2,384]{3,2,1,0:T(2,128)(2,1)S(1)}, bf16[10,4,2,384]{3,2,1,0:T(2,128)(2,1)S(1)}, u32[]{:S(2)}, u32[]{:S(2)}) collective-permute-start(bf16[10,4,2,384]{3,2,1,0:T(2,128)(2,1)S(1)} %get-tuple-element.18), channel_id=1, source_target_pairs={{0,4},{1,5},{2,6},{3,7},{4,8},{5,9},{6,10},{7,11},{8,12},{9,13},{1... | collective-permute-start | bytes 184328 | tf_op jit(solution)/shard_map/ppermute | solution.py:25
  48.7 1.3 %collective-permute-start.5 = (bf16[10,4,2,384]{3,2,1,0:T(2,128)(2,1)S(1)}, bf16[10,4,2,384]{3,2,1,0:T(2,128)(2,1)S(1)}, u32[]{:S(2)}, u32[]{:S(2)}) collective-permute-start(bf16[10,4,2,384]{3,2,1,0:T(2,128)(2,1)S(1)} %get-tuple-element.19), channel_id=1, source_target_pairs={{4,0},{5,1},{6,2},{7,3},{8,4},{9,5},{10,6},{11,7},{12,8},{13,9},{1... | collective-permute-start | bytes 184328 | tf_op jit(solution)/shard_map/ppermute | solution.py:25
  50.0 2.7 %collective-permute-start.6 = (bf16[4,4,1,384]{3,2,1,0:T(2,128)(2,1)S(1)}, bf16[4,4,1,384]{3,2,1,0:T(2,128)(2,1)S(1)}, u32[]{:S(2)}, u32[]{:S(2)}) collective-permute-start(bf16[4,4,1,384]{3,2,1,0:T(2,128)(2,1)S(1)} %get-tuple-element.20), channel_id=1, source_target_pairs={{0,1},{1,2},{2,3},{3,4},{4,5},{5,6},{6,7},{7,8},{8,9},{9,10},{10,1... | collective-permute-start | bytes 36872 | tf_op jit(solution)/shard_map/ppermute | solution.py:25
  52.7 1.9 %collective-permute-start.7 = (bf16[4,4,1,384]{3,2,1,0:T(2,128)(2,1)S(1)}, bf16[4,4,1,384]{3,2,1,0:T(2,128)(2,1)S(1)}, u32[]{:S(2)}, u32[]{:S(2)}) collective-permute-start(bf16[4,4,1,384]{3,2,1,0:T(2,128)(2,1)S(1)} %get-tuple-element.21), channel_id=1, source_target_pairs={{1,0},{2,1},{3,2},{4,3},{5,4},{6,5},{7,6},{8,7},{9,8},{10,9},{11,1... | collective-permute-start | bytes 36872 | tf_op jit(solution)/shard_map/ppermute | solution.py:25
  54.7 3.1 %collective-permute-done.7 = bf16[4,4,1,384]{3,2,1,0:T(2,128)(2,1)S(1)} collective-permute-done((bf16[4,4,1,384]{3,2,1,0:T(2,128)(2,1)S(1)}, bf16[4,4,1,384]{3,2,1,0:T(2,128)(2,1)S(1)}, u32[]{:S(2)}, u32[]{:S(2)}) %collective-permute-start.7) | collective-permute-done | bytes 12320 | tf_op jit(solution)/shard_map/ppermute | solution.py:25
  57.8 3.1 %shard_map.82 = (bf16[3,10,6,48,384]{4,3,2,1,0:T(8,128)(2,1)S(1)}, f32[8,128]{1,0:T(8,128)S(1)}) custom-call(s32[3]{0:T(128)S(1)} %pad_add_fusion.1.refs_0_, bf16[10,4,8,384]{3,2,1,0:T(8,128)(2,1)S(1)} %get-tuple-element.30.refs_1_, bf16[10,4,8,384]{3,2,1,0:T(8,128)(2,1)S(1)} %collective-permute-done.2.refs_2_, ...), custom_call_target="tpu_custom_call" | custom-call | flops 12288000 | bytes 7372800 | tf_op jit(solution)/shard_map/pallas_call | solution.py:109
  61.0 2.7 %copy-done.1 = bf16[3,10,6,48,384]{4,3,2,1,0:T(8,128)(2,1)} copy-done((bf16[3,10,6,48,384]{4,3,2,1,0:T(8,128)(2,1)}, bf16[3,10,6,48,384]{4,3,2,1,0:T(8,128)(2,1)S(1)}, u32[]{:S(2)}) %copy-start.1) | copy-done | bytes 6635544
  64.2 4.7 %all-gather.2.cloned.1.call-done = bf16[192,8,384]{2,0,1:T(8,128)(2,1)} async-done(((bf16[24,8,384]{2,0,1:T(8,128)(2,1)}), bf16[192,8,384]{2,0,1:T(8,128)(2,1)}) %all-gather.2.cloned.1.call-update) | async-done | bytes 1179664 | tf_op jit(solution)/shard_map/all_gather | solution.py:288
  71.7 7.9 %all-to-all-start.2 = ((bf16[32,32,384]{2,1,0:T(8,128)(2,1)}), bf16[32,32,384]{2,1,0:T(8,128)(2,1)S(1)}, u32[]{:S(2)}, u32[]{:S(2)}) async-start(bf16[32,32,384]{2,1,0:T(8,128)(2,1)} %broadcast_in_dim.17), calls=%async_computation.2 | async-start | bytes 1572864 | tf_op jit(solution)/shard_map/all_to_all | solution.py:29
  79.7 2.9 %copy-done.2 = bf16[3,10,6,48,384]{4,3,2,1,0:T(8,128)(2,1)S(1)} copy-done((bf16[3,10,6,48,384]{4,3,2,1,0:T(8,128)(2,1)S(1)}, bf16[3,10,6,48,384]{4,3,2,1,0:T(8,128)(2,1)}, u32[]{:S(2)}) %copy-start.2) | copy-done | bytes 6635544
  82.6 1.3 %copy-done.3 = bf16[192,8,384]{2,0,1:T(8,128)(2,1)S(1)} copy-done((bf16[192,8,384]{2,0,1:T(8,128)(2,1)S(1)}, bf16[192,8,384]{2,0,1:T(8,128)(2,1)}, u32[]{:S(2)}) %copy-start.3) | copy-done | bytes 1179672
  83.8 3.9 %shard_map.83 = bf16[8,160,192]{2,1,0:T(8,128)(2,1)} custom-call(s32[2]{0:T(128)S(1)} %pad_add_fusion.place_ref, bf16[3,10,6,48,384]{4,3,2,1,0:T(8,128)(2,1)S(1)} %copy-done.2, bf16[8,192,384]{2,1,0:T(8,128)(2,1)S(1)} %bitcast.25), custom_call_target="tpu_custom_call" | custom-call | flops 1585446912 | bytes 7667712 | tf_op jit(solution)/shard_map/pallas_call | solution.py:173
  87.7 3.7 %all-to-all-done.2.upper_ref = bf16[32,32,384]{2,1,0:T(8,128)(2,1)S(1)} async-done(((bf16[32,32,384]{2,1,0:T(8,128)(2,1)}), bf16[32,32,384]{2,1,0:T(8,128)(2,1)S(1)}, u32[]{:S(2)}, u32[]{:S(2)}) %all-to-all-start.2) | async-done | bytes 786464 | tf_op jit(solution)/shard_map/all_to_all | solution.py:29
  91.4 6.5 %all-to-all-start.1 = ((bf16[8,160,192]{2,1,0:T(8,128)(2,1)}), bf16[8,160,192]{2,1,0:T(8,128)(2,1)S(1)}, u32[]{:S(2)}, u32[]{:S(2)}) async-start(bf16[8,160,192]{2,1,0:T(8,128)(2,1)} %shard_map.83), calls=%async_computation.1 | async-start | bytes 1310720 | tf_op jit(solution)/shard_map/all_to_all | solution.py:332
  98.6 2.0 %collective-permute-start.8 = (bf16[32,32,384]{2,1,0:T(8,128)(2,1)S(1)}, bf16[32,32,384]{2,1,0:T(8,128)(2,1)S(1)}, u32[]{:S(2)}, u32[]{:S(2)}) collective-permute-start(bf16[32,32,384]{2,1,0:T(8,128)(2,1)S(1)} %all-to-all-done.2.upper_ref), channel_id=1, source_target_pairs={{0,1},{1,0},{2,3},{3,2},{4,5},{5,4},{6,7},{7,6},{8,9},{9,8},{10,11... | collective-permute-start | bytes 2359304 | tf_op jit(solution)/shard_map/ppermute | solution.py:21
  102.6 4.7 %all-to-all-done.1.parts_ref = bf16[8,160,192]{2,1,0:T(8,128)(2,1)S(1)} async-done(((bf16[8,160,192]{2,1,0:T(8,128)(2,1)}), bf16[8,160,192]{2,1,0:T(8,128)(2,1)S(1)}, u32[]{:S(2)}, u32[]{:S(2)}) %all-to-all-start.1) | async-done | bytes 491552 | tf_op jit(solution)/shard_map/all_to_all | solution.py:332
  107.3 2.3 %shard_map.84 = bf16[4,8,16,192]{3,2,1,0:T(8,128)(2,1)} custom-call(s32[1]{0:T(128)} %bitcast.core_ref, bf16[8,160,192]{2,1,0:T(8,128)(2,1)S(1)} %all-to-all-done.1.parts_ref, bf16[160,384]{1,0:T(8,128)(2,1)S(1)} %reshape.153.skip_ref, f32[160,1]{1,0:T(8,128)S(1)} %fusion.12.inside_ref, f32[1,384]{1,0:T(1,128)S(1)} %broadcast_in_dim.16.bias_ref, ...), custom_call_target="tpu_custom_call" | custom-call | flops 125829120 | bytes 786432 | tf_op jit(solution)/shard_map/pallas_call | solution.py:247
  (71 shorter events, 12.8 us)
Async XLA Ops:
  6.5 1.1 copy-start
  6.5 48.2 %copy-start.5 = (f32[384]{0:T(512)S(1)}, f32[384]{0:T(512)}, u32[]{:S(2)}) copy-start(f32[384]{0:T(512)} %param.10) | copy-start | bytes 4612
  6.5 48.2 %copy-start.6 = (f32[384]{0:T(512)S(1)}, f32[384]{0:T(512)}, u32[]{:S(2)}) copy-start(f32[384]{0:T(512)} %param.11) | copy-start | bytes 4612
  6.5 62.4 %all-gather.2.cloned.1.call-start = ((), (), s32[]{:S(2)}) async-start(), calls=%async_computation.3 | async-start | bytes 1327104 | tf_op jit(solution)/shard_map/all_gather | solution.py:288
  8.3 6.6 %collective-permute-start = (bf16[4,4,8,384]{3,2,1,0:T(8,128)(2,1)}, bf16[4,4,8,384]{3,2,1,0:T(8,128)(2,1)S(1)}, u32[]{:S(2)}, u32[]{:S(2)}) collective-permute-start(bf16[4,4,8,384]{3,2,1,0:T(8,128)(2,1)} %param.8), channel_id=1, source_target_pairs={{0,32},{32,0},{1,33},{33,1},{2,34},{34,2},{3,35},{35,3},{4,36},{36... | collective-permute-start | bytes 294920 | tf_op jit(solution)/shard_map/ppermute | solution.py:21
  15.8 6.5 %collective-permute-start.1 = (bf16[2,4,8,384]{3,2,1,0:T(8,128)(2,1)S(1)}, bf16[2,4,8,384]{3,2,1,0:T(8,128)(2,1)S(1)}, u32[]{:S(2)}, u32[]{:S(2)}) collective-permute-start(bf16[2,4,8,384]{3,2,1,0:T(8,128)(2,1)S(1)} %slice.64), channel_id=1, source_target_pairs={{0,64},{64,128},{128,192},{192,256},{256,320},{320,384},{384,448},... | collective-permute-start | bytes 147464 | tf_op jit(solution)/shard_map/ppermute | solution.py:292
  22.4 6.9 %collective-permute-start.2 = (bf16[10,4,8,384]{3,2,1,0:T(8,128)(2,1)S(1)}, bf16[10,4,8,384]{3,2,1,0:T(8,128)(2,1)S(1)}, u32[]{:S(2)}, u32[]{:S(2)}) collective-permute-start(bf16[10,4,8,384]{3,2,1,0:T(8,128)(2,1)S(1)} %get-tuple-element.30.refs_1_), channel_id=1, source_target_pairs={{0,2},{2,0},{1,3},{3,1},{4,6},{6,4},{5,7},{7,5},{8,10},{10,8},{9,1... | collective-permute-start | bytes 737288 | tf_op jit(solution)/shard_map/ppermute | solution.py:21
  29.4 14.1 %collective-permute-start.3 = (bf16[2,10,4,8,384]{4,3,2,1,0:T(8,128)(2,1)S(1)}, bf16[2,10,4,8,384]{4,3,2,1,0:T(8,128)(2,1)S(1)}, u32[]{:S(2)}, u32[]{:S(2)}) collective-permute-start(bf16[2,10,4,8,384]{4,3,2,1,0:T(8,128)(2,1)S(1)} %pad_maximum_fusion), channel_id=1, source_target_pairs={{0,1},{1,0},{2,3},{3,2},{4,5},{5,4},{6,7},{7,6},{8,9},{9,8},{10,11... | collective-permute-start | bytes 1474568 | tf_op jit(solution)/shard_map/ppermute | solution.py:21
  37.6 20.2 %all-to-all-start = ((f32[32,16,128]{2,1,0:T(8,128)}), f32[32,16,128]{2,1,0:T(8,128)S(1)}, u32[]{:S(2)}, u32[]{:S(2)}) async-start(f32[32,16,128]{2,1,0:T(8,128)} %broadcast_in_dim.13), calls=%async_computation | async-start | bytes 524288 | tf_op jit(solution)/shard_map/all_to_all | solution.py:29
  43.9 14.0 %collective-permute-start.4 = (bf16[10,4,2,384]{3,2,1,0:T(2,128)(2,1)S(1)}, bf16[10,4,2,384]{3,2,1,0:T(2,128)(2,1)S(1)}, u32[]{:S(2)}, u32[]{:S(2)}) collective-permute-start(bf16[10,4,2,384]{3,2,1,0:T(2,128)(2,1)S(1)} %get-tuple-element.18), channel_id=1, source_target_pairs={{0,4},{1,5},{2,6},{3,7},{4,8},{5,9},{6,10},{7,11},{8,12},{9,13},{1... | collective-permute-start | bytes 184328 | tf_op jit(solution)/shard_map/ppermute | solution.py:25
  48.7 9.2 %collective-permute-start.5 = (bf16[10,4,2,384]{3,2,1,0:T(2,128)(2,1)S(1)}, bf16[10,4,2,384]{3,2,1,0:T(2,128)(2,1)S(1)}, u32[]{:S(2)}, u32[]{:S(2)}) collective-permute-start(bf16[10,4,2,384]{3,2,1,0:T(2,128)(2,1)S(1)} %get-tuple-element.19), channel_id=1, source_target_pairs={{4,0},{5,1},{6,2},{7,3},{8,4},{9,5},{10,6},{11,7},{12,8},{13,9},{1... | collective-permute-start | bytes 184328 | tf_op jit(solution)/shard_map/ppermute | solution.py:25
  50.0 4.8 %collective-permute-start.6 = (bf16[4,4,1,384]{3,2,1,0:T(2,128)(2,1)S(1)}, bf16[4,4,1,384]{3,2,1,0:T(2,128)(2,1)S(1)}, u32[]{:S(2)}, u32[]{:S(2)}) collective-permute-start(bf16[4,4,1,384]{3,2,1,0:T(2,128)(2,1)S(1)} %get-tuple-element.20), channel_id=1, source_target_pairs={{0,1},{1,2},{2,3},{3,4},{4,5},{5,6},{6,7},{7,8},{8,9},{9,10},{10,1... | collective-permute-start | bytes 36872 | tf_op jit(solution)/shard_map/ppermute | solution.py:25
  52.7 5.1 %collective-permute-start.7 = (bf16[4,4,1,384]{3,2,1,0:T(2,128)(2,1)S(1)}, bf16[4,4,1,384]{3,2,1,0:T(2,128)(2,1)S(1)}, u32[]{:S(2)}, u32[]{:S(2)}) collective-permute-start(bf16[4,4,1,384]{3,2,1,0:T(2,128)(2,1)S(1)} %get-tuple-element.21), channel_id=1, source_target_pairs={{1,0},{2,1},{3,2},{4,3},{5,4},{6,5},{7,6},{8,7},{9,8},{10,9},{11,1... | collective-permute-start | bytes 36872 | tf_op jit(solution)/shard_map/ppermute | solution.py:25
  61.0 2.8 %copy-start.1 = (bf16[3,10,6,48,384]{4,3,2,1,0:T(8,128)(2,1)}, bf16[3,10,6,48,384]{4,3,2,1,0:T(8,128)(2,1)S(1)}, u32[]{:S(2)}) copy-start(bf16[3,10,6,48,384]{4,3,2,1,0:T(8,128)(2,1)S(1)} %get-tuple-element.24.act_ref) | copy-start | bytes 19906564
  63.7 34.2 %copy-start.7 = (f32[384]{0:T(512)S(1)}, f32[384]{0:T(512)}, u32[]{:S(2)}) copy-start(f32[384]{0:T(512)} %param.13) | copy-start | bytes 4612
  63.7 34.4 %copy-start.8 = (f32[192]{0:T(256)S(1)}, f32[192]{0:T(256)}, u32[]{:S(2)}) copy-start(f32[192]{0:T(256)} %param.15) | copy-start | bytes 2308
  69.0 31.9 %copy-start.4 = (bf16[4,4,8,384]{3,2,1,0:T(8,128)(2,1)S(1)}, bf16[4,4,8,384]{3,2,1,0:T(8,128)(2,1)}, u32[]{:S(2)}) copy-start(bf16[4,4,8,384]{3,2,1,0:T(8,128)(2,1)} %param.9) | copy-start | bytes 294916
  71.7 19.8 %all-to-all-start.2 = ((bf16[32,32,384]{2,1,0:T(8,128)(2,1)}), bf16[32,32,384]{2,1,0:T(8,128)(2,1)S(1)}, u32[]{:S(2)}, u32[]{:S(2)}) async-start(bf16[32,32,384]{2,1,0:T(8,128)(2,1)} %broadcast_in_dim.17), calls=%async_computation.2 | async-start | bytes 1572864 | tf_op jit(solution)/shard_map/all_to_all | solution.py:29
  79.7 2.9 %copy-start.2 = (bf16[3,10,6,48,384]{4,3,2,1,0:T(8,128)(2,1)S(1)}, bf16[3,10,6,48,384]{4,3,2,1,0:T(8,128)(2,1)}, u32[]{:S(2)}) copy-start(bf16[3,10,6,48,384]{4,3,2,1,0:T(8,128)(2,1)} %copy-done.1) | copy-start | bytes 19906564
  82.5 1.3 %copy-start.3 = (bf16[192,8,384]{2,0,1:T(8,128)(2,1)S(1)}, bf16[192,8,384]{2,0,1:T(8,128)(2,1)}, u32[]{:S(2)}) copy-start(bf16[192,8,384]{2,0,1:T(8,128)(2,1)} %all-gather.2.cloned.1.call-done) | copy-start | bytes 3538948
  91.4 15.9 %all-to-all-start.1 = ((bf16[8,160,192]{2,1,0:T(8,128)(2,1)}), bf16[8,160,192]{2,1,0:T(8,128)(2,1)S(1)}, u32[]{:S(2)}, u32[]{:S(2)}) async-start(bf16[8,160,192]{2,1,0:T(8,128)(2,1)} %shard_map.83), calls=%async_computation.1 | async-start | bytes 1310720 | tf_op jit(solution)/shard_map/all_to_all | solution.py:332
  98.6 8.8 %collective-permute-start.8 = (bf16[32,32,384]{2,1,0:T(8,128)(2,1)S(1)}, bf16[32,32,384]{2,1,0:T(8,128)(2,1)S(1)}, u32[]{:S(2)}, u32[]{:S(2)}) collective-permute-start(bf16[32,32,384]{2,1,0:T(8,128)(2,1)S(1)} %all-to-all-done.2.upper_ref), channel_id=1, source_target_pairs={{0,1},{1,0},{2,3},{3,2},{4,5},{5,4},{6,7},{7,6},{8,9},{9,8},{10,11... | collective-permute-start | bytes 2359304 | tf_op jit(solution)/shard_map/ppermute | solution.py:21
Sparse Core Ops, SparseCore 0:
  12.8 56.0 all-gather.1

commit v7 on v6

--- a/solution.py
+++ b/solution.py
@@ -11,7 +11,6 @@
 TIME = ("m", "p")
 TILE = ("x", "y1", "y0", "c")
 TEAM = ("p", "y0", "c")
-CHIPS = ("p", "x", "y1", "y0")
 TAPS = 7
 PADDED = 48
 NT = (((1,), (1,)), ((), ()))
@@ -62,27 +61,30 @@
     return widened(mean, 0), lax.rsqrt(spread + EPSILON)
 
 
-def act_kernel(
-    place_ref, own_ref, by_y_ref, by_c_ref, left_ref, right_ref, stats_ref, gain_ref, bias_ref,
-    out_ref, done_ref, slab_ref, mean_ref, scale_ref, *, columns,
+def conv_kernel(
+    place_ref, own_ref, by_y_ref, by_c_ref, left_ref, right_ref, stats_ref, gain_ref, bias_ref, weight_ref,
+    out_ref, act_ref, slab_ref, mean_ref, scale_ref, held_ref, stage_ref, *, columns,
 ):
     frames, rows, cols, chans = own_ref.shape
     padded = slab_ref.shape[0]
-    first, pair, quarter = place_ref[0], place_ref[1], place_ref[2]
+    outs = weight_ref.shape[1]
+    members, span = out_ref.shape[0], (frames - 2) // 2
+    wide = cols + 2
+    first, pair, quarter, first_tap, doubled = [place_ref[i] for i in range(5)]
+
     column = first - 6 + lax.broadcasted_iota(jnp.int32, (padded, chans), 0)
     inside = jnp.logical_and(column >= 0, column < columns)
     mean_ref[...], scale_ref[...] = chan_stats(stats_ref[...], chans, float(rows * cols * (chans // GROUPS)))
     scale_ref[...] *= gain_ref[...]
     slab_ref[...] = jnp.zeros_like(slab_ref)
-    done_ref[...] = jnp.zeros_like(done_ref)
-    nothing = jnp.zeros((padded, chans), out_ref.dtype)
+    nothing = jnp.zeros((padded, chans), act_ref.dtype)
 
     def one_frame(frame, carry):
         keep = jnp.logical_and(inside, jnp.logical_or(pair > 0, frame >= 2))
         mean, gain = mean_ref[pl.ds(frame, 1), :], scale_ref[pl.ds(frame, 1), :]
         for dx in range(3):
-            out_ref[dx, frame, 0] = nothing
-            out_ref[dx, frame, rows + 1] = nothing
+            act_ref[dx, frame, 0] = nothing
+            act_ref[dx, frame, rows + 1] = nothing
         for row in range(rows):
             for flip, strip in enumerate((own_ref, by_c_ref.at[0], by_y_ref, by_c_ref.at[1])):
                 at = pl.multiple_of(8 + cols * jnp.bitwise_xor(quarter, flip), 8)
@@ -93,45 +95,11 @@
             value = 0.5 * value
             value = jnp.where(keep, value + value * jnp.tanh(value), 0.0)
             for dx in range(3):
-                out_ref[dx, frame, row + 1] = pltpu.roll(value, padded - 6 - dx, 0).astype(out_ref.dtype)
+                act_ref[dx, frame, row + 1] = pltpu.roll(value, padded - 6 - dx, 0).astype(act_ref.dtype)
         return carry
 
     lax.fori_loop(0, frames, one_frame, 0)
 
-
-def activate(place, own, by_y, by_c, left, right, stats, gain, bias, columns):
-    frames, rows, cols, chans = own.shape
-
-    def kernel(*refs):
-        act_kernel(*refs, columns=columns)
-
-    vmem = pl.BlockSpec(memory_space=pltpu.VMEM)
-    return pl.pallas_call(
-        kernel,
-        out_shape=(
-            jax.ShapeDtypeStruct((3, frames, rows + 2, PADDED, chans), jnp.bfloat16),
-            jax.ShapeDtypeStruct((8, 128), jnp.float32),
-        ),
-        in_specs=[pl.BlockSpec(memory_space=pltpu.SMEM)] + [vmem] * 8,
-        out_specs=(vmem, vmem),
-        scratch_shapes=[
-            pltpu.VMEM((PADDED, chans), jnp.float32),
-            pltpu.VMEM((stats.shape[1], chans), jnp.float32),
-            pltpu.VMEM((stats.shape[1], chans), jnp.float32),
-        ],
-        compiler_params=pltpu.CompilerParams(vmem_limit_bytes=40 * 1024 * 1024),
-        cost_estimate=pl.CostEstimate(
-            flops=100 * own.size, bytes_accessed=60 * own.size, transcendentals=6 * own.size
-        ),
-    )(place, own, by_y, by_c, left, right, stats, gain[None], bias[None])
-
-
-def conv_kernel(place_ref, act_ref, weight_ref, out_ref, held_ref, stage_ref):
-    outs, chans = weight_ref.shape[1:]
-    frames, rows, padded = act_ref.shape[1] - 2, act_ref.shape[2] - 2, act_ref.shape[3]
-    members, span = out_ref.shape[0], frames // 2
-    cols = out_ref.shape[1] // (span * rows)
-    first, doubled = place_ref[0], place_ref[1]
     for i in range(TAPS):
         weight = weight_ref[i]
         if i == 0:
@@ -139,57 +107,90 @@
         held_ref[i // 2, :, (i % 2) * chans : (i % 2 + 1) * chans] = weight
 
     def window(chunk, i):
-        tap = first + i
+        tap = first_tap + i
         taken = act_ref[tap % 3, pl.ds(tap // 9 + chunk, 2), pl.ds(tap // 3 % 3, rows)]
         return taken.reshape(2 * rows * padded, chans)
 
-    for chunk in range(0, frames, 2):
+    for chunk in range(0, frames - 2, 2):
         total = None
-        for pair in range((TAPS + 1) // 2):
-            taken, weight = window(chunk, 2 * pair), held_ref[pair]
-            if 2 * pair + 1 < TAPS:
-                taken = jnp.concatenate([taken, window(chunk, 2 * pair + 1)], axis=1)
+        for both in range((TAPS + 1) // 2):
+            taken, weight = window(chunk, 2 * both), held_ref[both]
+            if 2 * both + 1 < TAPS:
+                taken = jnp.concatenate([taken, window(chunk, 2 * both + 1)], axis=1)
             else:
                 weight = weight[:, :chans]
             part = lax.dot_general(taken, weight, NT, preferred_element_type=jnp.float32)
-            total = part if pair == 0 else total + part
+            total = part if both == 0 else total + part
         total = total.reshape(2, rows, padded, outs)
         for step in range(2):
             plane, frame = (chunk + step) // span, (chunk + step) % span
             for row in range(rows):
-                at = (frame * rows + row) * cols
+                at = (frame * rows + row) * wide
                 for strip in range(4):
-                    stage_ref[4 * plane + strip, at : at + cols, :] = total[step, row, strip * 8 : strip * 8 + cols]
+                    stage_ref[4 * plane + strip, at : at + wide, :] = total[step, row, strip * 8 : strip * 8 + wide]
     for member in range(members):
         out_ref[member] = stage_ref[member].astype(out_ref.dtype)
 
 
-def conv_partial(place, act, weight, cols):
-    slots, outs, chans = weight.shape
-    _, frames, rows, padded, _ = act.shape
-    frames, rows = frames - 2, rows - 2
-    block = (8, frames // 2 * rows * cols, outs)
+def conv_partial(place, own, by_y, by_c, left, right, stats, gain, bias, weight, columns):
+    frames, rows, cols, chans = own.shape
+    outs = weight.shape[1]
+    block = (8, (frames - 2) // 2 * rows * (cols + 2), outs)
+
+    def kernel(*refs):
+        conv_kernel(*refs, columns=columns)
+
     vmem = pl.BlockSpec(memory_space=pltpu.VMEM)
     return pl.pallas_call(
-        conv_kernel,
+        kernel,
         out_shape=jax.ShapeDtypeStruct(block, jnp.bfloat16),
-        in_specs=[pl.BlockSpec(memory_space=pltpu.SMEM), vmem, vmem],
+        in_specs=[pl.BlockSpec(memory_space=pltpu.SMEM)] + [vmem] * 9,
         out_specs=vmem,
         scratch_shapes=[
+            pltpu.VMEM((3, frames, rows + 2, PADDED, chans), jnp.bfloat16),
+            pltpu.VMEM((PADDED, chans), jnp.float32),
+            pltpu.VMEM((stats.shape[1], chans), jnp.float32),
+            pltpu.VMEM((stats.shape[1], chans), jnp.float32),
             pltpu.VMEM(((TAPS + 1) // 2, outs, 2 * chans), jnp.bfloat16),
             pltpu.VMEM(block, jnp.float32),
         ],
         compiler_params=pltpu.CompilerParams(vmem_limit_bytes=40 * 1024 * 1024),
         cost_estimate=pl.CostEstimate(
-            flops=2 * frames * rows * padded * outs * chans * TAPS,
-            bytes_accessed=2 * (TAPS * outs * chans + act.size),
-            transcendentals=0,
+            flops=2 * (frames - 2) * rows * PADDED * outs * chans * TAPS,
+            bytes_accessed=2 * (TAPS * outs * chans + 8 * own.size),
+            transcendentals=6 * own.size,
         ),
-    )(place, act, weight)
+    )(place, own, by_y, by_c, left, right, stats, gain[None], bias[None], weight)
+
+
+def order_kernel(turn_ref, own_ref, by_c_ref, out_ref, stage_ref):
+    held = stage_ref.shape[1] // 8
+    for core, ref in enumerate((own_ref, by_c_ref)):
+        for k in range(4):
+            rows = jnp.dot(turn_ref[...], ref[k], preferred_element_type=jnp.float32)
+            at = (4 * core + k) * held
+            for tap in range(9):
+                stage_ref[tap, at : at + held, :] = rows[tap * held : (tap + 1) * held]
+    for tap in range(9):
+        out_ref[tap] = stage_ref[tap].astype(out_ref.dtype)
+
+
+def in_order(turn, own, by_c, outs):
+    vmem = pl.BlockSpec(memory_space=pltpu.VMEM)
+    shape = (9, outs, own.shape[-1])
+    return pl.pallas_call(
+        order_kernel,
+        out_shape=jax.ShapeDtypeStruct(shape, jnp.bfloat16),
+        in_specs=[vmem] * 3,
+        out_specs=vmem,
+        scratch_shapes=[pltpu.VMEM(shape, jnp.float32)],
+        compiler_params=pltpu.CompilerParams(vmem_limit_bytes=40 * 1024 * 1024),
+        cost_estimate=pl.CostEstimate(flops=16 * turn.size * own.shape[-1], bytes_accessed=6 * own.size, transcendentals=0),
+    )(turn, own, by_c)
 
 
 def tail_kernel(
-    core_ref, parts_ref, skip_ref, inside_ref, bias_ref, pick_ref, upper_ref, upper_by_c_ref, up_bias_ref, order_ref,
+    parts_ref, skip_ref, inside_ref, bias_ref, pick_ref, upper_ref, up_bias_ref, order_ref,
     out_ref, tap_ref, fine_ref, all_ref,
 ):
     frames, fine_rows, fine_cols, outs = out_ref.shape
@@ -205,16 +206,8 @@
         for part in (lower_half, upper_half):
             summed = summed + jnp.dot(part, pick_ref[parity], preferred_element_type=jnp.float32)
     summed = jnp.where(inside_ref[...] > 0.0, summed, 0.0).astype(jnp.bfloat16)
-    chips, held = upper_ref.shape[0] // 2, outs // (2 * upper_ref.shape[1])
     for tap in range(9):
-        weight = []
-        for group in range(tap * held, (tap + 1) * held):
-            for parity in range(2):
-                at = parity * chips + group // 2
-                mine = core_ref[0] == group % 2
-                weight.append(jnp.where(mine, upper_ref[at], upper_by_c_ref[at]))
-        weight = jnp.concatenate(weight, axis=0)
-        tap_ref[tap] = lax.dot_general(summed, weight, NT, preferred_element_type=jnp.float32)
+        tap_ref[tap] = lax.dot_general(summed, upper_ref[tap], NT, preferred_element_type=jnp.float32)
 
     spare = jnp.zeros((cols, 256 - outs), jnp.float32)
     for frame in range(frames):
@@ -241,13 +234,13 @@
     out_ref[...] = result.astype(out_ref.dtype).reshape(out_ref.shape)
 
 
-def tail(core, parts, skip, inside, bias, pick, upper, upper_by_c, up_bias, order, shape):
+def tail(parts, skip, inside, bias, pick, upper, up_bias, order, shape):
     frames, fine_rows, fine_cols, outs = shape
     vmem = pl.BlockSpec(memory_space=pltpu.VMEM)
     return pl.pallas_call(
         tail_kernel,
         out_shape=jax.ShapeDtypeStruct(shape, jnp.bfloat16),
-        in_specs=[pl.BlockSpec(memory_space=pltpu.SMEM)] + [vmem] * 9,
+        in_specs=[vmem] * 8,
         out_specs=vmem,
         scratch_shapes=[
             pltpu.VMEM((9, skip.shape[0], outs), jnp.float32),
@@ -258,7 +251,7 @@
         cost_estimate=pl.CostEstimate(
             flops=2 * skip.shape[0] * upper.size, bytes_accessed=2 * upper.size, transcendentals=0
         ),
-    )(core, parts, skip, inside, bias, pick, upper, upper_by_c, up_bias, order)
+    )(parts, skip, inside, bias, pick, upper, up_bias, order)
 
 
 def per_device(sizes, features, skip, norm_gain, norm_bias, conv_weight, conv_bias, up_weight, up_bias):
@@ -274,13 +267,13 @@
     shard, up_shard = conv_weight.shape[0], up_weight.shape[0]
     outs = up_shard * 2 * pairs
     first_tap = jnp.minimum(quarter * TAPS, 27 - TAPS)
-    share = next(r for r in range(1, up_shard + 1) if up_shard % r == 0 and 9 * up_shard // r <= strips)
-    up_rows = up_weight.transpose(1, 0, 2).reshape(9 * up_shard, chans)
-    up_rows = lax.dynamic_slice_in_dim(up_rows, jnp.minimum(strip * share, 9 * up_shard - share), share, axis=0)
+    share = up_shard // 4
+    up_rows = lax.dynamic_slice_in_dim(up_weight.transpose(1, 0, 2), quarter * share, share, axis=1)
+    up_rows = jnp.pad(up_rows.reshape(9 * share, chans), ((0, 2 * shard - 9 * share), (0, 0)))
     mine = jnp.concatenate(
         [
             lax.dynamic_slice_in_dim(conv_weight, first_tap, TAPS, axis=1),
-            jnp.pad(up_rows, ((0, shard - share), (0, 0)))[:, None],
+            up_rows.reshape(2, shard, chans).transpose(1, 0, 2),
         ],
         axis=1,
     )
@@ -312,27 +305,45 @@
     column = strip * cols - 1 + jnp.arange(skip10.shape[0]) % (cols + 2)
     inside = jnp.logical_and(column >= 0, column < columns).astype(jnp.float32)[:, None]
 
-    place = jnp.stack([quad * 4 * cols - 2, lax.axis_index("m"), quarter])
-    act, done = activate(place, ten, by_y, by_c, left, right, everyone, norm_gain, norm_bias, columns)
-
-    up_rows = gathered[TAPS].reshape(pairs, shard, chans)[:, :share].reshape(pairs * share, chans)
-    up_rows = (up_rows.astype(jnp.float32) + done[0, 0]).astype(jnp.bfloat16)
-    upper = handed_out(up_rows, CHIPS, strips)
+    ready = sum(jnp.minimum(jnp.abs(a[0, 0, 0].astype(jnp.float32)), 0.0) for a in (left, right, skip_left, skip_right))
+    up_rows = jnp.concatenate(
+        [gathered[TAPS], gathered[TAPS + 1].reshape(pairs, shard, chans)[:, :share].reshape(pairs * share, chans)]
+    )
+    up_rows = jnp.pad((up_rows.astype(jnp.float32) + ready).astype(jnp.bfloat16), ((0, -up_rows.shape[0] % 16), (0, 0)))
+    up_rows = jnp.stack([up_rows, swap(up_rows, "p")])
     last = (quarter == 3).astype(jnp.int32)
-    parts = conv_partial(jnp.stack([first_tap, last]), act, gathered, cols + 2)
-    upper = upper.reshape(strips, pairs * share, chans)
-    upper_by_c = swap(upper, "c")
+    place = jnp.stack([quad * 4 * cols - 2, lax.axis_index("m"), quarter, first_tap, last])
+    parts = conv_partial(
+        place, ten, by_y, by_c, left, right, everyone, norm_gain, norm_bias, gathered, columns
+    )
+    up_rows = jnp.concatenate([up_rows, swap(up_rows, "y0")])
+    up_by_c = swap(up_rows, "c")
+
+    row = jnp.arange(9 * pairs * share).reshape(9, pairs, share)
+    row_of = jnp.concatenate(
+        [row[:8].transpose(1, 0, 2).reshape(-1), row[8].reshape(-1)]
+    )
+    count = up_rows.shape[1]
+    row_of = jnp.pad(row_of, (0, count - row_of.shape[0]), constant_values=-1)
+    turn = (jnp.arange(count)[:, None] == row_of[None, :]).astype(jnp.bfloat16)
+    upper = in_order(turn, up_rows, up_by_c, outs)
 
     channel = jnp.arange(chans).reshape(pairs, 2, shard).transpose(1, 0, 2).reshape(2, chans // 2)
     pick = (channel[:, :, None] == jnp.arange(chans)[None, None, :]).astype(jnp.bfloat16)
-    gathered_as, turn = (pairs, 2, up_shard // share, share), (2, 1, 0, 3)
-    out_channel = jnp.arange(outs).reshape(gathered_as).transpose(turn).reshape(outs)
+    holder = jnp.arange(8)
+    parity = jnp.bitwise_xor(lax.axis_index("p"), holder % 2)
+    whose = jnp.bitwise_xor(quarter, holder // 2 % 2 * 2 + holder // 4)
+    out_channel = (
+        (2 * jnp.arange(pairs)[None, :, None] + parity[:, None, None]) * up_shard
+        + whose[:, None, None] * share
+        + jnp.arange(share)[None, None, :]
+    ).reshape(outs)
     order = jnp.pad(out_channel, (0, 256 - outs), constant_values=-1)[:, None] == jnp.arange(outs)[None, :]
-    up_bias = up_bias.reshape(gathered_as).transpose(turn).reshape(1, outs)
+    order = order.astype(jnp.bfloat16)
+    up_bias = jnp.dot(order[:outs].astype(jnp.float32), up_bias, precision=lax.Precision.HIGHEST)[None]
     parts = lax.all_to_all(parts, TEAM, 0, 0, tiled=True)
     return tail(
-        lax.axis_index("c").reshape(1), parts, skip10, inside, conv_bias[None], pick, upper, upper_by_c,
-        up_bias, order.astype(jnp.bfloat16), (frames, 2 * rows, 2 * cols, outs),
+        parts, skip10, inside, conv_bias[None], pick, upper, up_bias, order, (frames, 2 * rows, 2 * cols, outs)
     )
 
 

time: 117 us -> 132 us (1.13)
  waiting for transfers between devices: 22.3 us -> 35.5 us
  starting transfers between devices: 52.5 us -> 56.6 us
  local copies, waits for them, and re-layouts: 14.1 us -> 11.2 us
    ppermute x4 -> x6, waiting for transfers between devices: 4.86 us -> 21.6 us  [swap(): return lax.ppermute(array, axis, [(0, 1), (1, 0)])]
    all_gather x1, waiting for transfers between devices: 4.74 us -> 12.9 us  [per_device(): gathered = lax.all_gather(mine, 'm', axis=0, tiled=True).transpose(1, 0, 2)]
    ppermute x4 -> x6, starting transfers between devices: 16.2 us -> 24.3 us  [swap(): return lax.ppermute(array, axis, [(0, 1), (1, 0)])]
    all_to_all x1, waiting for transfers between devices: 4.73 us -> 0.01 us  [per_device(): parts = lax.all_to_all(parts, TEAM, 0, 0, tiled=True)]
    all_to_all x2 -> x1, starting transfers between devices: 13.7 us -> 9.93 us  [handed_out(): lax.all_to_all(jnp.broadcast_to(array[None], (members,) + array.shape), a...]
    all_to_all x2 -> x1, waiting for transfers between devices: 3.7 us -> 0.01 us  [handed_out(): lax.all_to_all(jnp.broadcast_to(array[None], (members,) + array.shape), a...]
    ppermute x4, waiting for transfers between devices: 3.11 us -> 0.01 us  [strip_shift(): lax.ppermute(array, TILE, [(i, i + by) for i in range(count) if 0 <= i +...]
    slice x2, local copies, waits for them, and re-layouts: 1.47 us -> 0.01 us  [the longest x1 0.01 us: per_device(): gathered[TAPS + 1].reshape(pairs, shard, chans)[:, :share]]
  transfers between devices with their start and end apart: 13 -> 14, of which waited for: 7 -> 8; matrix products, arithmetic and copies ran while one was open for 6% -> 6% of each run, Pallas kernels for 6% -> 0%
where the time goes in v7:
time: 132 us; the launch traced here: 131 us
  starting transfers between devices  56.6 us (43%)
  waiting for transfers between devices  35.5 us (27%)
  between operations  13.9 us (11%)
  local copies, waits for them, and re-layouts  11.2 us (8%)
  Pallas kernels  9.3 us (7%)
  other arithmetic  4.71 us (4%)
    ppermute x6, starting transfers between devices, swap(): return lax.ppermute(array, axis, [(0, 1), (1, 0)])  24.3 us
    ppermute x6, waiting for transfers between devices, swap(): return lax.ppermute(array, axis, [(0, 1), (1, 0)])  21.6 us
    all_gather x1, waiting for transfers between devices, per_device(): gathered = lax.all_gather(mine, 'm', axis=0, tiled=True).transpose(1, 0, 2)  12.9 us
    all_to_all x1, starting transfers between devices, handed_out(): lax.all_to_all(jnp.broadcast_to(array[None], (members,) + array.shape), a...  9.93 us
    ppermute x4, starting transfers between devices, strip_shift(): lax.ppermute(array, TILE, [(i, i + by) for i in range(count) if 0 <= i +...  9.43 us
    all_to_all x1, starting transfers between devices, per_device(): parts = lax.all_to_all(parts, TEAM, 0, 0, tiled=True)  7.64 us
    pallas_call x1, Pallas kernels, conv_partial(): pl.pallas_call(kernel, out_shape=jax.ShapeDtypeStruct(block, jnp.bfloat16...  6.42 us
    unnamed x36, local copies, waits for them, and re-layouts  6.05 us
  transfers between devices with their start and end apart: 14, of which 8 were waited for; matrix products, arithmetic and copies ran while one was open for 6% of the time, Pallas kernels for 0%

profile of v7, /device:TPU:1, one launch (start us, length us, event | category | flops | bytes accessed | tf_op | source)
XLA Modules:
  0.0 131.4 jit_solution(3811463849211720558)
XLA Ops:
  6.6 1.0 dynamic-slice_bitcast_fusion
  8.4 4.4 %collective-permute-start = (bf16[4,4,8,384]{3,2,1,0:T(8,128)(2,1)}, bf16[4,4,8,384]{3,2,1,0:T(8,128)(2,1)S(1)}, u32[]{:S(2)}, u32[]{:S(2)}) collective-permute-start(bf16[4,4,8,384]{3,2,1,0:T(8,128)(2,1)} %param.8), channel_id=1, source_target_pairs={{0,32},{32,0},{1,33},{33,1},{2,34},{34,2},{3,35},{35,3},{4,36},{36... | collective-permute-start | bytes 294920 | tf_op jit(solution)/shard_map/ppermute | solution.py:20
  13.0 2.0 %collective-permute-done = bf16[4,4,8,384]{3,2,1,0:T(8,128)(2,1)S(1)} collective-permute-done((bf16[4,4,8,384]{3,2,1,0:T(8,128)(2,1)}, bf16[4,4,8,384]{3,2,1,0:T(8,128)(2,1)S(1)}, u32[]{:S(2)}, u32[]{:S(2)}) %collective-permute-start) | collective-permute-done | bytes 98336 | tf_op jit(solution)/shard_map/ppermute | solution.py:20
  15.9 5.3 %collective-permute-start.1 = (bf16[2,4,8,384]{3,2,1,0:T(8,128)(2,1)S(1)}, bf16[2,4,8,384]{3,2,1,0:T(8,128)(2,1)S(1)}, u32[]{:S(2)}, u32[]{:S(2)}) collective-permute-start(bf16[2,4,8,384]{3,2,1,0:T(8,128)(2,1)S(1)} %slice.92), channel_id=1, source_target_pairs={{0,64},{64,128},{128,192},{192,256},{256,320},{320,384},{384,448},... | collective-permute-start | bytes 147464 | tf_op jit(solution)/shard_map/ppermute | solution.py:285
  22.4 3.1 %collective-permute-start.2 = (bf16[10,4,8,384]{3,2,1,0:T(8,128)(2,1)S(1)}, bf16[10,4,8,384]{3,2,1,0:T(8,128)(2,1)S(1)}, u32[]{:S(2)}, u32[]{:S(2)}) collective-permute-start(bf16[10,4,8,384]{3,2,1,0:T(8,128)(2,1)S(1)} %get-tuple-element.26.refs_1_), channel_id=1, source_target_pairs={{0,2},{2,0},{1,3},{3,1},{4,6},{6,4},{5,7},{7,5},{8,10},{10,8},{9,1... | collective-permute-start | bytes 737288 | tf_op jit(solution)/shard_map/ppermute | solution.py:20
  26.6 2.7 %collective-permute-done.2.refs_2_ = bf16[10,4,8,384]{3,2,1,0:T(8,128)(2,1)S(1)} collective-permute-done((bf16[10,4,8,384]{3,2,1,0:T(8,128)(2,1)S(1)}, bf16[10,4,8,384]{3,2,1,0:T(8,128)(2,1)S(1)}, u32[]{:S(2)}, u32[]{:S(2)}) %collective-permute-start.2) | collective-permute-done | bytes 245792 | tf_op jit(solution)/shard_map/ppermute | solution.py:20
  29.4 6.6 %collective-permute-start.3 = (bf16[2,10,4,8,384]{4,3,2,1,0:T(8,128)(2,1)S(1)}, bf16[2,10,4,8,384]{4,3,2,1,0:T(8,128)(2,1)S(1)}, u32[]{:S(2)}, u32[]{:S(2)}) collective-permute-start(bf16[2,10,4,8,384]{4,3,2,1,0:T(8,128)(2,1)S(1)} %pad_maximum_fusion.1), channel_id=1, source_target_pairs={{0,1},{1,0},{2,3},{3,2},{4,5},{5,4},{6,7},{7,6},{8,9},{9,8},{10,11... | collective-permute-start | bytes 1474568 | tf_op jit(solution)/shard_map/ppermute | solution.py:20
  37.9 3.4 %collective-permute-start.4 = (bf16[10,4,2,384]{3,2,1,0:T(2,128)(2,1)S(1)}, bf16[10,4,2,384]{3,2,1,0:T(2,128)(2,1)S(1)}, u32[]{:S(2)}, u32[]{:S(2)}) collective-permute-start(bf16[10,4,2,384]{3,2,1,0:T(2,128)(2,1)S(1)} %get-tuple-element.16), channel_id=1, source_target_pairs={{0,4},{1,5},{2,6},{3,7},{4,8},{5,9},{6,10},{7,11},{8,12},{9,13},{1... | collective-permute-start | bytes 184328 | tf_op jit(solution)/shard_map/ppermute | solution.py:24
  41.4 1.3 collective-permute-start.5
  42.7 2.8 %collective-permute-start.6 = (bf16[4,4,1,384]{3,2,1,0:T(2,128)(2,1)S(1)}, bf16[4,4,1,384]{3,2,1,0:T(2,128)(2,1)S(1)}, u32[]{:S(2)}, u32[]{:S(2)}) collective-permute-start(bf16[4,4,1,384]{3,2,1,0:T(2,128)(2,1)S(1)} %get-tuple-element.18), channel_id=1, source_target_pairs={{0,1},{1,2},{2,3},{3,4},{4,5},{5,6},{6,7},{7,8},{8,9},{9,10},{10,1... | collective-permute-start | bytes 36872 | tf_op jit(solution)/shard_map/ppermute | solution.py:24
  45.5 1.9 %collective-permute-start.7 = (bf16[4,4,1,384]{3,2,1,0:T(2,128)(2,1)S(1)}, bf16[4,4,1,384]{3,2,1,0:T(2,128)(2,1)S(1)}, u32[]{:S(2)}, u32[]{:S(2)}) collective-permute-start(bf16[4,4,1,384]{3,2,1,0:T(2,128)(2,1)S(1)} %get-tuple-element.19), channel_id=1, source_target_pairs={{1,0},{2,1},{3,2},{4,3},{5,4},{6,5},{7,6},{8,7},{9,8},{10,9},{11,1... | collective-permute-start | bytes 36872 | tf_op jit(solution)/shard_map/ppermute | solution.py:24
  48.2 9.9 %all-to-all-start = ((f32[32,16,128]{2,1,0:T(8,128)}), f32[32,16,128]{2,1,0:T(8,128)S(1)}, u32[]{:S(2)}, u32[]{:S(2)}) async-start(f32[32,16,128]{2,1,0:T(8,128)} %broadcast_in_dim.10), calls=%async_computation | async-start | bytes 524288 | tf_op jit(solution)/shard_map/all_to_all | solution.py:28
  58.2 12.9 %all-gather.2.cloned.1.call-done = bf16[192,9,384]{2,0,1:T(8,128)(2,1)} async-done(((bf16[24,9,384]{2,0,1:T(8,128)(2,1)}), bf16[192,9,384]{2,0,1:T(8,128)(2,1)}) %all-gather.2.cloned.1.call-update) | async-done | bytes 1327120 | tf_op jit(solution)/shard_map/all_gather | solution.py:281
  71.2 1.0 slice_bitcast_fusion.2
  72.2 1.3 copy-done.6
  73.5 6.4 %shard_map.82 = bf16[8,160,192]{2,1,0:T(8,128)(2,1)} custom-call(s32[5]{0:T(128)S(1)} %stack.45.refs_0_, bf16[10,4,8,384]{3,2,1,0:T(8,128)(2,1)S(1)} %get-tuple-element.26.refs_1_, bf16[10,4,8,384]{3,2,1,0:T(8,128)(2,1)S(1)} %collective-permute-done.2.refs_2_, bf16[2,10,4,8,384]{4,3,2,1,0:T(8,128)(2,1)S(1)} %collective-permute-done.3.refs_3_, ...), custom_call_target="tpu_custom_call" | custom-call | flops 1585446912 | bytes 2998272 | tf_op jit(solution)/shard_map/pallas_call | solution.py:144
  79.9 7.6 %all-to-all-start.1 = ((bf16[8,160,192]{2,1,0:T(8,128)(2,1)}), bf16[8,160,192]{2,1,0:T(8,128)(2,1)S(1)}, u32[]{:S(2)}, u32[]{:S(2)}) async-start(bf16[8,160,192]{2,1,0:T(8,128)(2,1)} %shard_map.82), calls=%async_computation.1 | async-start | bytes 1310720 | tf_op jit(solution)/shard_map/all_to_all | solution.py:344
  87.7 3.3 %collective-permute-start.8 = (bf16[224,384]{1,0:T(8,128)(2,1)S(1)}, bf16[224,384]{1,0:T(8,128)(2,1)S(1)}, u32[]{:S(2)}, u32[]{:S(2)}) collective-permute-start(bf16[224,384]{1,0:T(8,128)(2,1)S(1)} %get-tuple-element.36), channel_id=1, source_target_pairs={{0,32},{32,0},{1,33},{33,1},{2,34},{34,2},{3,35},{35,3},{4,36},{36... | collective-permute-start | bytes 516104 | tf_op jit(solution)/shard_map/ppermute | solution.py:20
  91.8 8.9 %collective-permute-done.8 = bf16[224,384]{1,0:T(8,128)(2,1)S(1)} collective-permute-done((bf16[224,384]{1,0:T(8,128)(2,1)S(1)}, bf16[224,384]{1,0:T(8,128)(2,1)S(1)}, u32[]{:S(2)}, u32[]{:S(2)}) %collective-permute-start.8) | collective-permute-done | bytes 172064 | tf_op jit(solution)/shard_map/ppermute | solution.py:20
  100.7 3.2 %collective-permute-start.9 = (bf16[2,224,384]{2,1,0:T(8,128)(2,1)S(1)}, bf16[2,224,384]{2,1,0:T(8,128)(2,1)S(1)}, u32[]{:S(2)}, u32[]{:S(2)}) collective-permute-start(bf16[2,224,384]{2,1,0:T(8,128)(2,1)S(1)} %pad_maximum_fusion.2), channel_id=1, source_target_pairs={{0,2},{2,0},{1,3},{3,1},{4,6},{6,4},{5,7},{7,5},{8,10},{10,8},{9,1... | collective-permute-start | bytes 1032200 | tf_op jit(solution)/shard_map/ppermute | solution.py:20
  104.1 7.3 %collective-permute-done.9 = bf16[2,224,384]{2,1,0:T(8,128)(2,1)S(1)} collective-permute-done((bf16[2,224,384]{2,1,0:T(8,128)(2,1)S(1)}, bf16[2,224,384]{2,1,0:T(8,128)(2,1)S(1)}, u32[]{:S(2)}, u32[]{:S(2)}) %collective-permute-start.9) | collective-permute-done | bytes 344096 | tf_op jit(solution)/shard_map/ppermute | solution.py:20
  111.5 3.7 %collective-permute-start.10 = (bf16[4,224,384]{2,1,0:T(8,128)(2,1)S(1)}, bf16[4,224,384]{2,1,0:T(8,128)(2,1)S(1)}, u32[]{:S(2)}, u32[]{:S(2)}) collective-permute-start(bf16[4,224,384]{2,1,0:T(8,128)(2,1)S(1)} %pad_maximum_fusion.own_ref), channel_id=1, source_target_pairs={{0,1},{1,0},{2,3},{3,2},{4,5},{5,4},{6,7},{7,6},{8,9},{9,8},{10,11... | collective-permute-start | bytes 2064392 | tf_op jit(solution)/shard_map/ppermute | solution.py:20
  117.9 1.1 copy-done.2
  122.3 2.2 %shard_map.84 = bf16[4,8,16,192]{3,2,1,0:T(8,128)(2,1)} custom-call(bf16[8,160,192]{2,1,0:T(8,128)(2,1)S(1)} %all-to-all-done.1.parts_ref, bf16[160,384]{1,0:T(8,128)(2,1)S(1)} %copy-done.4, f32[160,1]{1,0:T(8,128)S(1)} %fusion.14.inside_ref, f32[1,384]{1,0:T(1,128)S(1)} %broadcast_in_dim.13.bias_ref, bf16[2,192,384]{2,1,0:T(8,128)(2,1)S(1)} %fusion.pick_ref, ...), custom_call_target="tpu_custom_call" | custom-call | flops 212336640 | bytes 1327104 | tf_op jit(solution)/shard_map/pallas_call | solution.py:240
  (103 shorter events, 14.0 us)
Async XLA Ops:
  6.5 19.0 %copy-start.14 = (f32[384]{0:T(512)S(1)}, f32[384]{0:T(512)}, u32[]{:S(2)}) copy-start(f32[384]{0:T(512)} %param.10) | copy-start | bytes 4612
  6.5 19.0 %copy-start.15 = (f32[384]{0:T(512)S(1)}, f32[384]{0:T(512)}, u32[]{:S(2)}) copy-start(f32[384]{0:T(512)} %param.11) | copy-start | bytes 4612
  6.5 19.0 %copy-start.16 = (f32[384]{0:T(512)S(1)}, f32[384]{0:T(512)}, u32[]{:S(2)}) copy-start(f32[384]{0:T(512)} %param.13) | copy-start | bytes 4612
  6.5 20.1 %copy-start.7 = (bf16[4,4,8,384]{3,2,1,0:T(8,128)(2,1)S(1)}, bf16[4,4,8,384]{3,2,1,0:T(8,128)(2,1)}, u32[]{:S(2)}) copy-start(bf16[4,4,8,384]{3,2,1,0:T(8,128)(2,1)} %param.9) | copy-start | bytes 294916
  6.6 64.6 %all-gather.2.cloned.1.call-start = ((), (), s32[]{:S(2)}) async-start(), calls=%async_computation.2 | async-start | bytes 1492992 | tf_op jit(solution)/shard_map/all_gather | solution.py:281
  8.4 6.6 %collective-permute-start = (bf16[4,4,8,384]{3,2,1,0:T(8,128)(2,1)}, bf16[4,4,8,384]{3,2,1,0:T(8,128)(2,1)S(1)}, u32[]{:S(2)}, u32[]{:S(2)}) collective-permute-start(bf16[4,4,8,384]{3,2,1,0:T(8,128)(2,1)} %param.8), channel_id=1, source_target_pairs={{0,32},{32,0},{1,33},{33,1},{2,34},{34,2},{3,35},{35,3},{4,36},{36... | collective-permute-start | bytes 294920 | tf_op jit(solution)/shard_map/ppermute | solution.py:20
  15.9 6.5 %collective-permute-start.1 = (bf16[2,4,8,384]{3,2,1,0:T(8,128)(2,1)S(1)}, bf16[2,4,8,384]{3,2,1,0:T(8,128)(2,1)S(1)}, u32[]{:S(2)}, u32[]{:S(2)}) collective-permute-start(bf16[2,4,8,384]{3,2,1,0:T(8,128)(2,1)S(1)} %slice.92), channel_id=1, source_target_pairs={{0,64},{64,128},{128,192},{192,256},{256,320},{320,384},{384,448},... | collective-permute-start | bytes 147464 | tf_op jit(solution)/shard_map/ppermute | solution.py:285
  22.4 6.9 %collective-permute-start.2 = (bf16[10,4,8,384]{3,2,1,0:T(8,128)(2,1)S(1)}, bf16[10,4,8,384]{3,2,1,0:T(8,128)(2,1)S(1)}, u32[]{:S(2)}, u32[]{:S(2)}) collective-permute-start(bf16[10,4,8,384]{3,2,1,0:T(8,128)(2,1)S(1)} %get-tuple-element.26.refs_1_), channel_id=1, source_target_pairs={{0,2},{2,0},{1,3},{3,1},{4,6},{6,4},{5,7},{7,5},{8,10},{10,8},{9,1... | collective-permute-start | bytes 737288 | tf_op jit(solution)/shard_map/ppermute | solution.py:20
  29.4 8.1 %collective-permute-start.3 = (bf16[2,10,4,8,384]{4,3,2,1,0:T(8,128)(2,1)S(1)}, bf16[2,10,4,8,384]{4,3,2,1,0:T(8,128)(2,1)S(1)}, u32[]{:S(2)}, u32[]{:S(2)}) collective-permute-start(bf16[2,10,4,8,384]{4,3,2,1,0:T(8,128)(2,1)S(1)} %pad_maximum_fusion.1), channel_id=1, source_target_pairs={{0,1},{1,0},{2,3},{3,2},{4,5},{5,4},{6,7},{7,6},{8,9},{9,8},{10,11... | collective-permute-start | bytes 1474568 | tf_op jit(solution)/shard_map/ppermute | solution.py:20
  37.9 20.2 %collective-permute-start.4 = (bf16[10,4,2,384]{3,2,1,0:T(2,128)(2,1)S(1)}, bf16[10,4,2,384]{3,2,1,0:T(2,128)(2,1)S(1)}, u32[]{:S(2)}, u32[]{:S(2)}) collective-permute-start(bf16[10,4,2,384]{3,2,1,0:T(2,128)(2,1)S(1)} %get-tuple-element.16), channel_id=1, source_target_pairs={{0,4},{1,5},{2,6},{3,7},{4,8},{5,9},{6,10},{7,11},{8,12},{9,13},{1... | collective-permute-start | bytes 184328 | tf_op jit(solution)/shard_map/ppermute | solution.py:24
  41.4 16.8 %collective-permute-start.5 = (bf16[10,4,2,384]{3,2,1,0:T(2,128)(2,1)S(1)}, bf16[10,4,2,384]{3,2,1,0:T(2,128)(2,1)S(1)}, u32[]{:S(2)}, u32[]{:S(2)}) collective-permute-start(bf16[10,4,2,384]{3,2,1,0:T(2,128)(2,1)S(1)} %get-tuple-element.17), channel_id=1, source_target_pairs={{4,0},{5,1},{6,2},{7,3},{8,4},{9,5},{10,6},{11,7},{12,8},{13,9},{1... | collective-permute-start | bytes 184328 | tf_op jit(solution)/shard_map/ppermute | solution.py:24
  42.7 15.5 %collective-permute-start.6 = (bf16[4,4,1,384]{3,2,1,0:T(2,128)(2,1)S(1)}, bf16[4,4,1,384]{3,2,1,0:T(2,128)(2,1)S(1)}, u32[]{:S(2)}, u32[]{:S(2)}) collective-permute-start(bf16[4,4,1,384]{3,2,1,0:T(2,128)(2,1)S(1)} %get-tuple-element.18), channel_id=1, source_target_pairs={{0,1},{1,2},{2,3},{3,4},{4,5},{5,6},{6,7},{7,8},{8,9},{9,10},{10,1... | collective-permute-start | bytes 36872 | tf_op jit(solution)/shard_map/ppermute | solution.py:24
  45.5 12.7 %collective-permute-start.7 = (bf16[4,4,1,384]{3,2,1,0:T(2,128)(2,1)S(1)}, bf16[4,4,1,384]{3,2,1,0:T(2,128)(2,1)S(1)}, u32[]{:S(2)}, u32[]{:S(2)}) collective-permute-start(bf16[4,4,1,384]{3,2,1,0:T(2,128)(2,1)S(1)} %get-tuple-element.19), channel_id=1, source_target_pairs={{1,0},{2,1},{3,2},{4,3},{5,4},{6,5},{7,6},{8,7},{9,8},{10,9},{11,1... | collective-permute-start | bytes 36872 | tf_op jit(solution)/shard_map/ppermute | solution.py:24
  48.2 24.0 %all-to-all-start = ((f32[32,16,128]{2,1,0:T(8,128)}), f32[32,16,128]{2,1,0:T(8,128)S(1)}, u32[]{:S(2)}, u32[]{:S(2)}) async-start(f32[32,16,128]{2,1,0:T(8,128)} %broadcast_in_dim.10), calls=%async_computation | async-start | bytes 524288 | tf_op jit(solution)/shard_map/all_to_all | solution.py:28
  58.1 21.8 %copy-start.9 = (bf16[4,4,1,384]{3,2,1,0:T(2,128)(2,1)}, bf16[4,4,1,384]{3,2,1,0:T(2,128)(2,1)S(1)}, u32[]{:S(2)}) copy-start(bf16[4,4,1,384]{3,2,1,0:T(2,128)(2,1)S(1)} %collective-permute-done.6) | copy-start | bytes 36868
  58.2 21.8 %copy-start.11 = (bf16[4,4,1,384]{3,2,1,0:T(2,128)(2,1)}, bf16[4,4,1,384]{3,2,1,0:T(2,128)(2,1)S(1)}, u32[]{:S(2)}) copy-start(bf16[4,4,1,384]{3,2,1,0:T(2,128)(2,1)S(1)} %collective-permute-done.7) | copy-start | bytes 36868
  79.9 24.0 %copy-start.17 = (f32[192]{0:T(256)S(1)}, f32[192]{0:T(256)}, u32[]{:S(2)}) copy-start(f32[192]{0:T(256)} %param.15) | copy-start | bytes 2308
  79.9 40.6 %all-to-all-start.1 = ((bf16[8,160,192]{2,1,0:T(8,128)(2,1)}), bf16[8,160,192]{2,1,0:T(8,128)(2,1)S(1)}, u32[]{:S(2)}, u32[]{:S(2)}) async-start(bf16[8,160,192]{2,1,0:T(8,128)(2,1)} %shard_map.82), calls=%async_computation.1 | async-start | bytes 1310720 | tf_op jit(solution)/shard_map/all_to_all | solution.py:344
  87.7 27.6 %copy-start.13 = (s32[224]{0:T(256)S(1)}, s32[224]{0:T(256)}, u32[]{:S(2)}) copy-start(s32[224]{0:T(256)} %pad.22) | copy-start | bytes 2692
  87.7 13.0 %collective-permute-start.8 = (bf16[224,384]{1,0:T(8,128)(2,1)S(1)}, bf16[224,384]{1,0:T(8,128)(2,1)S(1)}, u32[]{:S(2)}, u32[]{:S(2)}) collective-permute-start(bf16[224,384]{1,0:T(8,128)(2,1)S(1)} %get-tuple-element.36), channel_id=1, source_target_pairs={{0,32},{32,0},{1,33},{33,1},{2,34},{34,2},{3,35},{35,3},{4,36},{36... | collective-permute-start | bytes 516104 | tf_op jit(solution)/shard_map/ppermute | solution.py:20
  100.7 15.4 %copy-start.10 = (bf16[4,4,1,384]{3,2,1,0:T(2,128)(2,1)S(1)}, bf16[4,4,1,384]{3,2,1,0:T(2,128)(2,1)}, u32[]{:S(2)}) copy-start(bf16[4,4,1,384]{3,2,1,0:T(2,128)(2,1)} %copy-done.9) | copy-start | bytes 36868
  100.7 15.4 %copy-start.12 = (bf16[4,4,1,384]{3,2,1,0:T(2,128)(2,1)S(1)}, bf16[4,4,1,384]{3,2,1,0:T(2,128)(2,1)}, u32[]{:S(2)}) copy-start(bf16[4,4,1,384]{3,2,1,0:T(2,128)(2,1)} %copy-done.11) | copy-start | bytes 36868
  100.7 10.7 %collective-permute-start.9 = (bf16[2,224,384]{2,1,0:T(8,128)(2,1)S(1)}, bf16[2,224,384]{2,1,0:T(8,128)(2,1)S(1)}, u32[]{:S(2)}, u32[]{:S(2)}) collective-permute-start(bf16[2,224,384]{2,1,0:T(8,128)(2,1)S(1)} %pad_maximum_fusion.2), channel_id=1, source_target_pairs={{0,2},{2,0},{1,3},{3,1},{4,6},{6,4},{5,7},{7,5},{8,10},{10,8},{9,1... | collective-permute-start | bytes 1032200 | tf_op jit(solution)/shard_map/ppermute | solution.py:20
  111.5 5.4 %collective-permute-start.10 = (bf16[4,224,384]{2,1,0:T(8,128)(2,1)S(1)}, bf16[4,224,384]{2,1,0:T(8,128)(2,1)S(1)}, u32[]{:S(2)}, u32[]{:S(2)}) collective-permute-start(bf16[4,224,384]{2,1,0:T(8,128)(2,1)S(1)} %pad_maximum_fusion.own_ref), channel_id=1, source_target_pairs={{0,1},{1,0},{2,3},{3,2},{4,5},{5,4},{6,7},{7,6},{8,9},{9,8},{10,11... | collective-permute-start | bytes 2064392 | tf_op jit(solution)/shard_map/ppermute | solution.py:20
  (8 other events, 22.5 us)
Sparse Core Ops, SparseCore 0:
  12.9 58.2 all-gather.1
